TPU v7x, 32 devices: a whole 2x2x4 slice. The times are simulated.
32 devices in a mesh: groups: 2 (over y), batch: 16 (over z, x, core).
Axes of the slice: x: 2, y: 2, z: 4, core: 2. Of those that a mesh axis runs over, the one named last changes fastest.
Arguments:
- tokens: bfloat16 [96, 6144], P(('groups', 'batch')), parts along dimension 0, may hold values from -6 to 6
- w_proj: bfloat16 [6144, 16384], P(None, 'batch'), may hold values from -0.078125 to 0.078125
- w_out: bfloat16 [4096, 6144], P(None, 'batch'), may hold values from -0.09375 to 0.09375
- decay_rate: float32 [32], replicated, may hold values from 0.02 to 2
- norm_gain: float32 [4096], replicated, may hold values from 0.1 to 1.9
- cache_tiles: bfloat16 [5376, 128, 128], P(('groups', 'batch')), parts along dimension 0, may hold values from -6 to 6
- tile_scales: float32 [5376], P(('groups', 'batch')), parts along dimension 0, may hold values from 0.1 to 1
- tile_holder: int32 [96, 32], P(('groups', 'batch')), parts along dimension 0, may hold values from 0 to 15, as said below
- tile_rank: int32 [96, 32], P(('groups', 'batch')), parts along dimension 0, may hold values from 0 to 11, as said below
- send_slot: int32 [32, 16, 12], P(('groups', 'batch')), parts along dimension 0, may hold values from -1 to 167, as said below
Outputs:
- mixed_out: bfloat16 [96, 6144], P('groups', 'batch'), parts along dimension 0
- new_cache: bfloat16 [5376, 128, 128], P(('groups', 'batch')), parts along dimension 0
There are 2 independent parts, one for each index of `groups`. A program takes and returns all parts, laid end to end along the dimension named above; an argument that names none is the same for every part. Nothing has to cross between parts.
Inputs may be any that keep to these rules, and one draw needn't show every extreme that they name: tile_holder[s, h] is the device along batch whose slots hold the tile of session s and head h; a holder holds up to 168 tiles, and some holders hold that many. tile_rank[s, h] is the tile's position among the tiles that its holder sends to the owner of s (device s // 3); some holder sends 12 tiles to some owner in every draw. send_slot[p, o, r] is the slot in holder p of the tile at position r that p sends to owner o, -1 where p sends fewer than r + 1 tiles to o; it agrees with tile_holder and tile_rank, names every tile of every session once and names no slot twice.
All inputs are finite; a program needn't handle non-finite values.
Results may differ from a plain program's by a relative error of at most 0.0085.
Values may be sent and summed in bfloat16 or wider, within the bound.
No kernel may reach another device: no remote copies, remote signals or barrier semaphores. Data moves between devices by JAX's collectives and lax.ppermute only.
A program may use at most 128 MiB of HBM per device.

v0:
```python
import jax
import jax.numpy as jnp
from jax import lax
from jax.sharding import PartitionSpec as P


def advance(tile_rows, scale_rows, factor, queries, key_rows, values):
    tile_scale = scale_rows[:, None, None]
    states = factor[:, None, None] * (tile_rows.astype(jnp.float32) * tile_scale)
    states = (
        states + key_rows.astype(jnp.float32)[:, :, None] * values.astype(jnp.float32)[:, None, :]
    )
    readout = jnp.einsum(
        "ti,tij->tj", queries.astype(jnp.float32), states, precision=lax.Precision.HIGHEST
    )
    fresh_tiles = (states / tile_scale).astype(jnp.bfloat16)
    return (readout, fresh_tiles)


def on_device(
    tokens,
    w_proj,
    w_out,
    decay_rate,
    norm_gain,
    cache_tiles,
    tile_scales,
    tile_holder,
    tile_rank,
    send_slot,
):
    devices = lax.axis_size("batch")
    head_dim = cache_tiles.shape[-1]
    head_count = decay_rate.shape[0]
    inner_width = head_count * head_dim
    own_rows = tokens.shape[0]
    tiles_own = own_rows * head_count
    slot_count = cache_tiles.shape[0]
    capacity = send_slot.shape[-1]
    projected = jnp.dot(
        lax.all_gather(tokens, "batch", axis=0, tiled=True),
        w_proj,
        preferred_element_type=jnp.float32,
    )
    col_count = w_proj.shape[1]
    columns = lax.axis_index("batch") * col_count + jnp.arange(col_count, dtype=jnp.int32)
    local_active = jnp.where(
        columns[None, :] < 3 * inner_width, jax.nn.silu(projected), jax.nn.sigmoid(projected)
    ).astype(jnp.bfloat16)
    activated = lax.all_to_all(local_active, "batch", split_axis=0, concat_axis=1, tiled=True)
    queries = activated[:, :inner_width].reshape(tiles_own, head_dim)
    key_rows = activated[:, inner_width : 2 * inner_width].reshape(tiles_own, head_dim)
    values = activated[:, 2 * inner_width : 3 * inner_width].reshape(tiles_own, head_dim)
    gate_values = activated[:, 3 * inner_width :].astype(jnp.float32)
    factor = jnp.tile(jnp.exp(-decay_rate), own_rows)
    slot_list = send_slot.reshape(-1)
    safe_slots = jnp.maximum(slot_list, 0)
    target_slots = jnp.where(slot_list < 0, slot_count, slot_list)
    pick_rows = (tile_holder * capacity + tile_rank).reshape(-1)
    got_tiles, got_scales = (
        lax.all_to_all(cache_tiles[safe_slots], "batch", split_axis=0, concat_axis=0, tiled=True),
        lax.all_to_all(
            tile_scales[safe_slots].astype(jnp.bfloat16),
            "batch",
            split_axis=0,
            concat_axis=0,
            tiled=True,
        ).astype(jnp.float32),
    )
    readout, fresh_tiles = advance(
        got_tiles[pick_rows], got_scales[pick_rows], factor, queries, key_rows, values
    )
    outgoing = (
        jnp.zeros((devices * capacity, head_dim, head_dim), jnp.bfloat16)
        .at[pick_rows]
        .set(fresh_tiles)
    )
    returned = lax.all_to_all(outgoing, "batch", split_axis=0, concat_axis=0, tiled=True)
    new_cache = cache_tiles.at[target_slots].set(returned, mode="drop")
    readout = readout.reshape(own_rows, inner_width)
    squares = jnp.mean(readout * readout, axis=1, keepdims=True)
    hidden = (readout * lax.rsqrt(squares + 1e-06) * norm_gain * gate_values).astype(jnp.bfloat16)
    mixed_out = jnp.dot(
        lax.all_gather(hidden, "batch", axis=0, tiled=True),
        w_out,
        preferred_element_type=jnp.float32,
    ).astype(jnp.bfloat16)
    return (mixed_out, new_cache)


def solution(mesh):
    return jax.shard_map(
        on_device,
        mesh=mesh,
        in_specs=(
            P(("groups", "batch"), None),
            P(None, "batch"),
            P(None, "batch"),
            P(),
            P(),
            P(("groups", "batch"), None, None),
            P(("groups", "batch")),
            P(("groups", "batch"), None),
            P(("groups", "batch"), None),
            P(("groups", "batch"), None, None),
        ),
        out_specs=(P("groups", "batch"), P(("groups", "batch"), None, None)),
        check_vma=False,
    )
```

profile of v0, /device:TPU:13, one launch (start us, length us, event | category | flops | bytes accessed | tf_op | source)
XLA Modules:
  0.0 426.8 jit_solution(4103920369961401885)
XLA Ops:
  0.7 7.4 %copy.20 = bf16[168,128,128]{2,1,0:T(8,128)(2,1)} copy(bf16[168,128,128]{2,1,0:T(8,128)(2,1)} %param.15) | data formatting | bytes 11010048
  8.1 0.1 copy.13
  8.2 0.1 reshape.136
  8.3 1.6 gather_fusion.2
  9.9 0.7 convert_element_type.75
  10.6 6.6 %all-to-all-start.2 = ((bf16[16,12,1]{1,2,0:T(2,128)(2,1)}), bf16[16,12,1]{1,2,0:T(2,128)(2,1)S(1)}, u32[]{:S(2)}, u32[]{:S(2)}) async-start(bf16[16,12,1]{1,2,0:T(2,128)(2,1)} %convert_element_type.75), calls=%async_computation.2 | async-start | bytes 16384 | tf_op jit(solution)/shard_map/all_to_all | solution.py:62
  17.2 22.4 %all-gather = bf16[16,3,6144]{2,1,0:T(4,128)(2,1)} all-gather(bf16[1,3,6144]{2,1,0:T(4,128)(2,1)S(1)} %bitcast.23), channel_id=1, replica_groups=mesh['groups'=2,'batch'=16] {'batch'}, dimensions={0}, use_global_device_ids=true | all-gather | bytes 626688 | tf_op jit(solution)/shard_map/all_gather | solution.py:41
  39.6 2.2 reshape.191
  41.8 7.1 %fusion.5 = bf16[48,1024]{1,0:T(8,128)(2,1)S(1)} fusion(pred[1024]{0:T(1024)(128)(4,1)S(1)} %add_compare_fusion, bf16[48,6144]{1,0:T(8,128)(2,1)} %reshape.191, bf16[6144,1024]{1,0:T(8,128)(2,1)} %param.11), kind=kOutput, calls=%fused_computation.15 | convolution fusion | flops 604274688 | bytes 13272064 | tf_op jit(solution)/shard_map/dot_general | solution.py:40
  48.9 0.7 all_to_all.24
  49.6 6.4 %all-to-all-start = ((bf16[16,3,1024]{2,1,0:T(4,128)(2,1)}), bf16[16,3,1024]{2,1,0:T(4,128)(2,1)S(1)}, u32[]{:S(2)}, u32[]{:S(2)}) async-start(bf16[16,3,1024]{2,1,0:T(4,128)(2,1)} %all_to_all.24), calls=%async_computation | async-start | bytes 262144 | tf_op jit(solution)/shard_map/all_to_all | solution.py:50
  56.0 10.5 %gather_fusion = bf16[192,128,128]{2,1,0:T(8,128)(2,1)} fusion(bf16[168,128,128]{2,1,0:T(8,128)(2,1)} %copy.20, s32[1024]{0:T(1024)S(1)} %pad_clamp_fusion.1), kind=kCustom, calls=%fused_computation | custom fusion | bytes 12583680 | tf_op jit(solution)/shard_map/gather | solution.py:61
  66.6 6.3 %all-to-all-start.1 = ((bf16[192,128,128]{2,1,0:T(8,128)(2,1)}), bf16[192,128,128]{2,1,0:T(8,128)(2,1)}, u32[]{:S(2)}, u32[]{:S(2)}) async-start(bf16[192,128,128]{2,1,0:T(8,128)(2,1)} %gather_fusion), calls=%async_computation.1 | async-start | bytes 12582912 | tf_op jit(solution)/shard_map/all_to_all | solution.py:61
  72.9 0.1 mul.69
  73.0 0.1 reshape.137
  73.1 0.1 reshape.139
  73.2 1.3 gather_fusion.3
  74.6 133.5 %all-to-all-done.1 = bf16[192,128,128]{2,1,0:T(8,128)(2,1)} async-done(((bf16[192,128,128]{2,1,0:T(8,128)(2,1)}), bf16[192,128,128]{2,1,0:T(8,128)(2,1)}, u32[]{:S(2)}, u32[]{:S(2)}) %all-to-all-start.1) | async-done | bytes 6291488 | tf_op jit(solution)/shard_map/all_to_all | solution.py:61
  208.1 5.5 %gather_fusion.1 = bf16[96,128,128]{2,1,0:T(8,128)(2,1)} fusion(bf16[192,128,128]{2,1,0:T(8,128)(2,1)} %all-to-all-done.1, s32[1024]{0:T(1024)S(1)} %pad_clamp_fusion), kind=kCustom, calls=%fused_computation.1 | custom fusion | bytes 6291840 | tf_op jit(solution)/shard_map/gather | solution.py:71
  213.6 5.6 %divide_convert_fusion = bf16[96,128,128]{2,1,0:T(8,128)(2,1)} fusion(bf16[96,128,128]{2,1,0:T(8,128)(2,1)} %gather_fusion.1, f32[96,128]{1,0:T(8,128)S(1)} %reshape.141, f32[96,128]{1,0:T(8,128)S(1)} %reshape.140, f32[96]{0:T(128)S(1)} %gather_fusion.3, f32[96]{0:T(128)S(1)} %mul.69), kind=kLoop, calls=%fused_computation.6 | loop fusion | flops 11010048 | bytes 6390528 | tf_op jit(solution)/shard_map/convert_element_type | solution.py:16
  219.2 4.2 broadcast_in_dim.13
  223.5 14.8 %scatter_fusion = bf16[192,128,128]{2,1,0:T(8,128)(2,1)} fusion(bf16[192,128,128]{2,1,0:T(8,128)(2,1)} %broadcast_in_dim.13, s32[96]{0:T(128)S(1)} %fusion.7, bf16[96,128,128]{2,1,0:T(8,128)(2,1)} %divide_convert_fusion), kind=kCustom, calls=%fused_computation.4 | custom fusion | bytes 9437568 | tf_op jit(solution)/shard_map/scatter | solution.py:76
  238.2 7.0 %all-to-all-start.3 = ((bf16[192,128,128]{2,1,0:T(8,128)(2,1)}), bf16[192,128,128]{2,1,0:T(8,128)(2,1)}, u32[]{:S(2)}, u32[]{:S(2)}) async-start(bf16[192,128,128]{2,1,0:T(8,128)(2,1)} %scatter_fusion), calls=%async_computation.3 | async-start | bytes 12582912 | tf_op jit(solution)/shard_map/all_to_all | solution.py:78
  245.3 5.6 %fusion = f32[96,1,128]{2,1,0:T(1,128)S(1)} fusion(bf16[96,128,1]{1,2,0:T(2,128)(2,1)S(1)} %reshape.197, bf16[96,128,128]{2,1,0:T(8,128)(2,1)} %gather_fusion.1, f32[96,128]{1,0:T(8,128)S(1)} %reshape.141, f32[96,128]{1,0:T(8,128)S(1)} %reshape.140, f32[96]{0:T(128)S(1)} %gather_fusion.3, f32[96]{0:T(128)S(1)} %mul.69), kind=kOutput, calls=%fused_computation.8 | convolution fusion | flops 26738688 | bytes 3318528 | tf_op jit(solution)/shard_map/ti,tij->tj/dot_general | solution.py:13
  250.9 0.1 multiply_reduce_fusion
  251.0 0.1 reduce_sum.14
  251.1 0.1 reduce_sum.18
  251.3 0.1 fusion.6
  251.4 144.7 %all-gather.1 = bf16[16,3,4096]{2,1,0:T(4,128)(2,1)} all-gather(bf16[1,3,4096]{2,1,0:T(4,128)(2,1)S(1)} %fusion.6), channel_id=1, replica_groups=mesh['groups'=2,'batch'=16] {'batch'}, dimensions={0}, use_global_device_ids=true | all-gather | bytes 417792 | tf_op jit(solution)/shard_map/all_gather | solution.py:84
  396.1 1.4 reshape.193
  397.5 1.2 convolution_convert_fusion
  398.7 28.1 %scatter_fusion.1 = bf16[168,128,128]{2,1,0:T(8,128)(2,1)} fusion(bf16[168,128,128]{2,1,0:T(8,128)(2,1)} %copy.20, s32[192]{0:T(256)S(1)} %bitcast.24, bf16[192,128,128]{2,1,0:T(8,128)(2,1)} %all-to-all-done.3), kind=kCustom, calls=%fused_computation.5 | custom fusion | bytes 18875136 | tf_op jit(solution)/shard_map/scatter | solution.py:79
  (34 shorter events, 0.3 us)
Async XLA Ops:
  0.6 396.9 %copy-start = (bf16[4096,384]{1,0:T(8,128)(2,1)S(1)}, bf16[4096,384]{1,0:T(8,128)(2,1)}, u32[]{:S(2)}) copy-start(bf16[4096,384]{1,0:T(8,128)(2,1)} %param.12) | copy-start | bytes 9437188
  0.6 16.5 %copy-start.2 = (bf16[3,6144]{1,0:T(4,128)(2,1)S(1)}, bf16[3,6144]{1,0:T(4,128)(2,1)}, u32[]{:S(2)}) copy-start(bf16[3,6144]{1,0:T(4,128)(2,1)} %param.10) | copy-start | bytes 110596
  0.7 7.6 %copy-start.1 = (f32[168]{0:T(256)S(1)}, f32[168]{0:T(256)}, u32[]{:S(2)}) copy-start(f32[168]{0:T(256)} %param.16) | copy-start | bytes 2020
  0.7 7.4 %copy-start.4 = (s32[1,16,12]{1,0,2:T(1,128)S(1)}, s32[1,16,12]{1,0,2:T(1,128)}, u32[]{:S(2)}) copy-start(s32[1,16,12]{1,0,2:T(1,128)} %param.19) | copy-start | bytes 2308
  10.6 39.0 %all-to-all-start.2 = ((bf16[16,12,1]{1,2,0:T(2,128)(2,1)}), bf16[16,12,1]{1,2,0:T(2,128)(2,1)S(1)}, u32[]{:S(2)}, u32[]{:S(2)}) async-start(bf16[16,12,1]{1,2,0:T(2,128)(2,1)} %convert_element_type.75), calls=%async_computation.2 | async-start | bytes 16384 | tf_op jit(solution)/shard_map/all_to_all | solution.py:62
  49.6 17.0 %all-to-all-start = ((bf16[16,3,1024]{2,1,0:T(4,128)(2,1)}), bf16[16,3,1024]{2,1,0:T(4,128)(2,1)S(1)}, u32[]{:S(2)}, u32[]{:S(2)}) async-start(bf16[16,3,1024]{2,1,0:T(4,128)(2,1)} %all_to_all.24), calls=%async_computation | async-start | bytes 262144 | tf_op jit(solution)/shard_map/all_to_all | solution.py:50
  66.6 6.3 %copy-start.7 = (f32[32]{0:T(128)S(1)}, f32[32]{0:T(128)}, u32[]{:S(2)}) copy-start(f32[32]{0:T(128)} %param.13) | copy-start | bytes 388
  66.6 6.4 %copy-start.5 = (s32[3,32]{1,0:T(4,128)S(1)}, s32[3,32]{1,0:T(4,128)}, u32[]{:S(2)}) copy-start(s32[3,32]{1,0:T(4,128)} %param.18) | copy-start | bytes 1156
  66.6 6.4 %copy-start.6 = (s32[3,32]{1,0:T(4,128)S(1)}, s32[3,32]{1,0:T(4,128)}, u32[]{:S(2)}) copy-start(s32[3,32]{1,0:T(4,128)} %param.17) | copy-start | bytes 1156
  66.6 141.5 %all-to-all-start.1 = ((bf16[192,128,128]{2,1,0:T(8,128)(2,1)}), bf16[192,128,128]{2,1,0:T(8,128)(2,1)}, u32[]{:S(2)}, u32[]{:S(2)}) async-start(bf16[192,128,128]{2,1,0:T(8,128)(2,1)} %gather_fusion), calls=%async_computation.1 | async-start | bytes 12582912 | tf_op jit(solution)/shard_map/all_to_all | solution.py:61
  238.2 160.4 %all-to-all-start.3 = ((bf16[192,128,128]{2,1,0:T(8,128)(2,1)}), bf16[192,128,128]{2,1,0:T(8,128)(2,1)}, u32[]{:S(2)}, u32[]{:S(2)}) async-start(bf16[192,128,128]{2,1,0:T(8,128)(2,1)} %scatter_fusion), calls=%async_computation.3 | async-start | bytes 12582912 | tf_op jit(solution)/shard_map/all_to_all | solution.py:78
  245.2 6.0 %copy-start.3 = (f32[4096]{0:T(1024)S(1)}, f32[4096]{0:T(1024)}, u32[]{:S(2)}) copy-start(f32[4096]{0:T(1024)} %param.14) | copy-start | bytes 49156
where the time goes:
time: 428 us; the launch traced here: 427 us
  blocking collectives  167 us (39%)
  waiting for transfers between devices  134 us (31%)
  local copies, waits for them, and re-layouts  79.1 us (18%)
  starting transfers between devices  26.3 us (6%)
  matrix products  13.9 us (3%)
  other arithmetic  6.05 us (1%)
    all_gather x1, blocking collectives, on_device(): lax.all_gather(hidden, 'batch', axis=0, tiled=True)  145 us
    all_to_all x1, waiting for transfers between devices, on_device(): lax.all_to_all(cache_tiles[safe_slots], 'batch', split_axis=0, concat_axi...  134 us
    scatter x1, local copies, waits for them, and re-layouts, on_device(): new_cache = cache_tiles.at[target_slots].set(returned, mode='drop')  28.1 us
    all_gather x1, blocking collectives, on_device(): lax.all_gather(tokens, 'batch', axis=0, tiled=True)  22.4 us
    scatter x1, local copies, waits for them, and re-layouts, on_device(): outgoing = jnp.zeros((devices * capacity, head_dim, head_dim), jnp.bfloat...  14.8 us
    unnamed x20, local copies, waits for them, and re-layouts  11.1 us
    gather x1, local copies, waits for them, and re-layouts, on_device(): cache_tiles[safe_slots]  10.5 us
  transfers between devices with their start and end apart: 4, of which 1 were waited for; matrix products, arithmetic and copies ran while one was open for 7% of the time, Pallas kernels for 0%

commit v1 on v0

v1 whole, which is shorter than its diff:
```python
import functools

import jax
import jax.numpy as jnp
from jax import lax
from jax.experimental import pallas as pl
from jax.experimental.pallas import tpu as pltpu
from jax.sharding import PartitionSpec as P

VMEM_LIMIT = 60 * 1024 * 1024
BF16 = jnp.bfloat16
F32 = jnp.float32


def block_order(devices):
    order, bit = [0], devices // 2
    while bit >= 1:
        order = order + [o ^ bit for o in order]
        bit //= 2
    return order


def gather_blocks(block, devices):
    held = block[None]
    bit = devices // 2
    while bit >= 1:
        got = lax.ppermute(held, "batch", [(i, i ^ bit) for i in range(devices)])
        held = jnp.concatenate([held, got], axis=0)
        bit //= 2
    return held


def project_kernel(
    chunk, inner_width, flag_ref, source_ref, x_ref, w_ref, act_ref, index_ref, rows, wbuf, sems
):
    devices, _, width = x_ref.shape
    sessions = act_ref.shape[0]
    own = sessions // devices
    steps = width // chunk
    copies = []
    for step in range(steps):
        part = pl.ds(step * chunk, chunk)
        copies.append(pltpu.make_async_copy(w_ref.at[part], wbuf.at[part], sems.at[step]))
        copies[-1].start()
    indices = []
    for j in range(devices):
        block = x_ref[j].astype(F32)
        rows[j * own : (j + 1) * own, :] = block[:own]
        for i in range(own):
            indices.append(block[own : own + 1, i * 128 : (i + 1) * 128])
    total = jnp.zeros(act_ref.shape, F32)
    for step in range(steps):
        copies[step].wait()
        part = slice(step * chunk, (step + 1) * chunk)
        total += jnp.dot(
            rows[:, part].astype(BF16), wbuf[part, :], preferred_element_type=F32
        )
    gate = jax.nn.sigmoid(total)
    active = jnp.where(flag_ref[0] > 0, gate, total * gate).astype(BF16)
    place = (
        lax.broadcasted_iota(jnp.int32, (sessions, sessions), 1) == source_ref[...]
    ).astype(F32).astype(BF16)
    act_ref[...] = jnp.dot(place, active, preferred_element_type=F32).astype(BF16)
    table = jnp.concatenate(indices, axis=0).astype(BF16)
    index_ref[...] = jnp.dot(place, table, preferred_element_type=F32).astype(jnp.int32)


def project(x, w, flag, source, inner_width):
    devices, _, width = x.shape
    sessions = source.shape[0]
    cols = w.shape[1]
    chunk = width // 8
    return pl.pallas_call(
        functools.partial(project_kernel, chunk, inner_width),
        out_shape=(
            jax.ShapeDtypeStruct((sessions, cols), BF16),
            jax.ShapeDtypeStruct((sessions, 128), jnp.int32),
        ),
        in_specs=[
            pl.BlockSpec(memory_space=pltpu.SMEM),
            pl.BlockSpec(memory_space=pltpu.VMEM),
            pl.BlockSpec(memory_space=pltpu.VMEM),
            pl.BlockSpec(memory_space=pl.ANY),
        ],
        out_specs=(
            pl.BlockSpec(memory_space=pltpu.VMEM),
            pl.BlockSpec(memory_space=pltpu.VMEM),
        ),
        scratch_shapes=[
            pltpu.VMEM((sessions, width), F32),
            pltpu.VMEM(w.shape, BF16),
            pltpu.SemaphoreType.DMA((width // chunk,)),
        ],
        compiler_params=pltpu.CompilerParams(vmem_limit_bytes=VMEM_LIMIT),
        cost_estimate=pl.CostEstimate(
            flops=2 * sessions * width * cols, bytes_accessed=2 * width * cols, transcendentals=0
        ),
        name="project",
    )(flag, source, x, w)


def readout_kernel(
    heads,
    order_ref,
    slot_ref,
    row_ref,
    head_ref,
    decay_ref,
    scale_ref,
    act_ref,
    cache_ref,
    out_ref,
    key_ref,
    value_ref,
    flat,
    tiles,
    query,
    sems,
):
    devices, sessions, cols = act_ref.shape
    per = cols // 128
    pieces = sems.shape[0]
    step = cache_ref.shape[0] // pieces
    copies = []
    for piece in range(pieces):
        part = pl.ds(piece * step, step)
        copies.append(pltpu.make_async_copy(cache_ref.at[part], tiles.at[part], sems.at[piece]))
        copies[-1].start()
    rows_each = per * sessions

    def place(j):
        device = order_ref[j]

        @pl.when(device < 3 * devices // 4)
        def _():
            base = pl.multiple_of(device * rows_each, 8)
            for b in range(per):
                flat[pl.ds(base + b * sessions, sessions), :] = act_ref[
                    j, :, b * 128 : (b + 1) * 128
                ].astype(F32)

    if devices <= 16:
        for j in range(devices):
            place(j)
    else:
        pl.loop(0, devices)(place)
    entries = out_ref.shape[0]
    comp = heads * sessions

    @pl.loop(0, entries // 8)
    def _(group):
        for u in range(8):
            e = group * 8 + u
            row = row_ref[e]
            query[pl.ds(e, 1), :] = flat[pl.ds(row, 1), :]
            key_ref[pl.ds(e, 1), :] = flat[pl.ds(row + comp, 1), :]
            value_ref[pl.ds(e, 1), :] = flat[pl.ds(row + 2 * comp, 1), :]

    for copy in copies:
        copy.wait()

    @pl.loop(0, entries // 8)
    def _(group):
        base = pl.multiple_of(group * 8, 8)
        q8 = query[pl.ds(base, 8), :]
        outs = []
        for u in range(8):
            e = base + u
            slot = jnp.maximum(slot_ref[e], 0)
            factor = decay_ref[head_ref[e]] * scale_ref[slot]
            prod = jnp.dot(
                q8[u : u + 1].astype(BF16), tiles[slot], preferred_element_type=F32
            )
            outs.append(prod * factor)
        near = jnp.sum(q8 * key_ref[pl.ds(base, 8), :], axis=1, keepdims=True)
        query[pl.ds(base, 8), :] = (
            jnp.concatenate(outs, axis=0) + near * value_ref[pl.ds(base, 8), :]
        )

    out_ref[...] = query[...].astype(BF16)


def read_states(act, cache, order, slot, row, head, decay, scale, heads):
    entries = slot.shape[0]
    devices, sessions, cols = act.shape
    smem = pl.BlockSpec(memory_space=pltpu.SMEM)
    vmem = pl.BlockSpec(memory_space=pltpu.VMEM)
    return pl.pallas_call(
        functools.partial(readout_kernel, heads),
        out_shape=(
            jax.ShapeDtypeStruct((entries, 128), BF16),
            jax.ShapeDtypeStruct((entries, 128), F32),
            jax.ShapeDtypeStruct((entries, 128), F32),
        ),
        in_specs=[smem] * 6 + [vmem, pl.BlockSpec(memory_space=pl.ANY)],
        out_specs=(vmem, vmem, vmem),
        scratch_shapes=[
            pltpu.VMEM((3 * heads * sessions, 128), F32),
            pltpu.VMEM(cache.shape, BF16),
            pltpu.VMEM((entries, 128), F32),
            pltpu.SemaphoreType.DMA((8,)),
        ],
        compiler_params=pltpu.CompilerParams(vmem_limit_bytes=VMEM_LIMIT),
        cost_estimate=pl.CostEstimate(
            flops=2 * entries * 128 * 128, bytes_accessed=2 * cache.size, transcendentals=0
        ),
        name="readout",
    )(order, slot, row, head, decay, scale, act, cache)


def update_kernel(
    slot_ref, head_ref, decay_ref, inverse_ref, key_ref, value_ref, cache_ref, out_ref
):
    @pl.loop(0, cache_ref.shape[0] // 8)
    def _(group):
        base = group * 8
        out_ref[pl.ds(base, 8)] = cache_ref[pl.ds(base, 8)]

    @pl.loop(0, slot_ref.shape[0] // 8)
    def _(group):
        base = pl.multiple_of(group * 8, 8)
        keys = key_ref[pl.ds(base, 8), :].astype(BF16)
        values = value_ref[pl.ds(base, 8), :].astype(BF16)
        for u in range(8):
            slot = slot_ref[base + u]

            @pl.when(slot >= 0)
            def _():
                outer = lax.dot_general(
                    keys[u : u + 1],
                    values[u : u + 1],
                    (((0,), (0,)), ((), ())),
                    preferred_element_type=F32,
                )
                fresh = decay_ref[head_ref[base + u]] * cache_ref[slot].astype(F32)
                out_ref[slot] = (fresh + outer * inverse_ref[slot]).astype(BF16)


def update_tiles(cache, key_rows, values, slot, head, decay, inverse):
    smem = pl.BlockSpec(memory_space=pltpu.SMEM)
    vmem = pl.BlockSpec(memory_space=pltpu.VMEM)
    return pl.pallas_call(
        update_kernel,
        out_shape=jax.ShapeDtypeStruct(cache.shape, BF16),
        in_specs=[smem] * 4 + [vmem] * 3,
        out_specs=vmem,
        compiler_params=pltpu.CompilerParams(vmem_limit_bytes=VMEM_LIMIT),
        cost_estimate=pl.CostEstimate(
            flops=4 * cache.size, bytes_accessed=4 * cache.size, transcendentals=0
        ),
        name="update",
    )(slot, head, decay, inverse, key_rows, values, cache)


def finish_kernel(
    order_ref, pick_ref, read_ref, act_ref, gain_ref, w_ref, out_ref, flat, hidden, merged
):
    devices, entries, _ = read_ref.shape
    sessions = act_ref.shape[1]
    per = act_ref.shape[2] // 128
    heads = merged.shape[1] // 128
    first = 3 * devices // 4

    def place(j):
        device = order_ref[j]
        base = pl.multiple_of(device * entries, 8)
        flat[pl.ds(base, entries), :] = read_ref[j].astype(F32)

    if devices <= 16:
        for j in range(devices):
            place(j)
    else:
        pl.loop(0, devices)(place)

    @pl.loop(0, heads * sessions // 16)
    def _(group):
        for u in range(16):
            e = group * 16 + u
            hidden[pl.ds(e, 1), :] = flat[pl.ds(pick_ref[e], 1), :]

    squares = jnp.zeros((sessions, 128), F32)
    for h in range(heads):
        block = hidden[h * sessions : (h + 1) * sessions, :]
        squares += block * block
    mean = jnp.sum(squares, axis=1, keepdims=True) * (1.0 / (heads * 128))
    norm = lax.rsqrt(mean + 1e-6)
    for h in range(heads):
        block = hidden[h * sessions : (h + 1) * sessions, :]
        device = first + h // per
        gate = act_ref[order_ref[devices + device], :, (h % per) * 128 : (h % per + 1) * 128]
        block = block * norm * gain_ref[h : h + 1, :] * gate.astype(F32)
        merged[:, h * 128 : (h + 1) * 128] = block.astype(BF16)
    out_ref[...] = jnp.dot(merged[...], w_ref[...], preferred_element_type=F32).astype(BF16)


def finish(read, act, order, pick, gain, w_out):
    devices, entries, _ = read.shape
    sessions = act.shape[1]
    width = w_out.shape[0]
    smem = pl.BlockSpec(memory_space=pltpu.SMEM)
    vmem = pl.BlockSpec(memory_space=pltpu.VMEM)
    return pl.pallas_call(
        finish_kernel,
        out_shape=jax.ShapeDtypeStruct((sessions, w_out.shape[1]), BF16),
        in_specs=[smem] * 2 + [vmem] * 4,
        out_specs=vmem,
        scratch_shapes=[
            pltpu.VMEM((devices * entries, 128), F32),
            pltpu.VMEM((sessions * width // 128, 128), F32),
            pltpu.VMEM((sessions, width), BF16),
        ],
        compiler_params=pltpu.CompilerParams(vmem_limit_bytes=VMEM_LIMIT),
        cost_estimate=pl.CostEstimate(
            flops=2 * sessions * w_out.size, bytes_accessed=2 * w_out.size, transcendentals=0
        ),
        name="finish",
    )(order, pick, read, act, gain, w_out)


def on_device(
    tokens,
    w_proj,
    w_out,
    decay_rate,
    norm_gain,
    cache_tiles,
    tile_scales,
    tile_holder,
    tile_rank,
    send_slot,
):
    devices = lax.axis_size("batch")
    me = lax.axis_index("batch")
    heads = decay_rate.shape[0]
    inner_width = heads * cache_tiles.shape[-1]
    own, width = tokens.shape
    sessions = own * devices
    capacity = send_slot.shape[-1]
    cols = w_proj.shape[1]

    relative = jnp.array(block_order(devices), jnp.int32)
    inverse_order = [0] * devices
    for j, o in enumerate(block_order(devices)):
        inverse_order[o] = j
    bits = devices.bit_length() - 1
    owners = jnp.arange(devices, dtype=jnp.int32)
    crossed = owners ^ me
    position = sum(((crossed >> k) & 1) << (bits - 1 - k) for k in range(bits))
    order = jnp.concatenate([relative ^ me, position])
    source = (position[:, None] * own + jnp.arange(own, dtype=jnp.int32)[None]).reshape(sessions, 1)
    flag = (me * cols >= 3 * inner_width).astype(jnp.int32).reshape(1)

    table = jnp.concatenate([tile_holder, tile_rank], axis=1).astype(BF16)
    table = jnp.pad(table, ((0, 0), (0, 128 - 2 * heads))).reshape(1, own * 128)
    table = jnp.pad(table, ((0, 0), (0, width - own * 128)))
    sent = jnp.concatenate([tokens, table], axis=0)

    blocks = gather_blocks(sent, devices)
    act, index = project(blocks, w_proj, flag, source, inner_width)
    all_act = gather_blocks(act, devices)

    holder = index[:, :heads]
    rank = index[:, heads : 2 * heads]
    owner = jnp.arange(sessions, dtype=jnp.int32)[:, None] // own
    pick = ((holder * devices + owner) * capacity + rank).T.reshape(-1)
    local = (
        jnp.arange(heads, dtype=jnp.int32)[None, :] * own
        + jnp.arange(own, dtype=jnp.int32)[:, None]
    ).reshape(-1)
    mine = jnp.where(holder == me, rank, -1).reshape(devices, own * heads)
    ranks = jnp.arange(capacity, dtype=jnp.int32)
    found = jnp.sum(
        jnp.where(mine[:, None, :] == ranks[None, :, None], local[None, None, :], 0), axis=2
    )
    head = found // own
    session = found % own + own * jnp.arange(devices, dtype=jnp.int32)[:, None]
    row = (head * sessions + session).reshape(-1)
    head = head.reshape(-1)
    slot = send_slot.reshape(-1)
    decay = jnp.exp(-decay_rate)

    read, key_rows, values = read_states(
        all_act, cache_tiles, order, slot, row, head, decay, tile_scales, heads
    )
    all_read = gather_blocks(read, devices)
    new_cache = update_tiles(
        cache_tiles, key_rows, values, slot, head, decay, 1.0 / tile_scales
    )
    mixed_out = finish(all_read, all_act, order, pick, norm_gain.reshape(heads, 128), w_out)
    return (mixed_out, new_cache)


def solution(mesh):
    return jax.shard_map(
        on_device,
        mesh=mesh,
        in_specs=(
            P(("groups", "batch"), None),
            P(None, "batch"),
            P(None, "batch"),
            P(),
            P(),
            P(("groups", "batch"), None, None),
            P(("groups", "batch")),
            P(("groups", "batch"), None),
            P(("groups", "batch"), None),
            P(("groups", "batch"), None, None),
        ),
        out_specs=(P("groups", "batch"), P(("groups", "batch"), None, None)),
        check_vma=False,
    )
```

time: 428 us -> 136 us (0.32)
  the two profiles are of different devices: /device:TPU:13 before, /device:TPU:27 now
where the time goes in v1:
time: 136 us; the launch traced here: 134 us
  Pallas kernels  59.6 us (44%)
  waiting for transfers between devices  40.4 us (30%)
  other arithmetic  13 us (10%)
  starting transfers between devices  12.6 us (9%)
  local copies, waits for them, and re-layouts  8.03 us (6%)
    ppermute x12, waiting for transfers between devices, gather_blocks(): got = lax.ppermute(held, 'batch', [(i, i ^ bit) for i in range(devices)])  40.4 us
    pallas_call x1, Pallas kernels, update_tiles(): pl.pallas_call(update_kernel, out_shape=jax.ShapeDtypeStruct(cache.shape,...  37.6 us
    ppermute x12, starting transfers between devices, gather_blocks(): got = lax.ppermute(held, 'batch', [(i, i ^ bit) for i in range(devices)])  12.6 us
    pallas_call x1, Pallas kernels, read_states(): pl.pallas_call(functools.partial(readout_kernel, heads), out_shape=(jax.S...  9.23 us
    pallas_call x1, Pallas kernels, project(): pl.pallas_call(functools.partial(project_kernel, chunk, inner_width), out...  7.03 us
    concatenate x9, other arithmetic, gather_blocks(): held = jnp.concatenate([held, got], axis=0)  5.77 us
    pallas_call x1, Pallas kernels, finish(): pl.pallas_call(finish_kernel, out_shape=jax.ShapeDtypeStruct((sessions, w...  5.72 us
    unnamed x23, local copies, waits for them, and re-layouts  4.77 us
  transfers between devices with their start and end apart: 12, of which 10 were waited for; matrix products, arithmetic and copies ran while one was open for 7% of the time, Pallas kernels for 28%

profile of v1, /device:TPU:27, one launch (start us, length us, event | category | flops | bytes accessed | tf_op | source)
XLA Modules:
  0.0 134.5 jit_solution(1910403921435318532)
XLA Ops:
  2.1 0.8 constant_dynamic-update-slice_fusion.4
  3.1 1.2 negate_exponential_fusion.decay_ref
  5.3 0.8 copy.22
  7.8 3.3 %collective-permute-done.1 = bf16[2,4,6144]{2,1,0:T(4,128)(2,1)S(1)} collective-permute-done((bf16[2,4,6144]{2,1,0:T(4,128)(2,1)S(1)}, bf16[2,4,6144]{2,1,0:T(4,128)(2,1)S(1)}, u32[]{:S(2)}, u32[]{:S(2)}) %collective-permute-start.1) | collective-permute-done | bytes 98336 | tf_op jit(solution)/shard_map/ppermute | solution.py:27
  11.5 4.2 %collective-permute-done.2 = bf16[4,4,6144]{2,1,0:T(4,128)(2,1)S(1)} collective-permute-done((bf16[4,4,6144]{2,1,0:T(4,128)(2,1)S(1)}, bf16[4,4,6144]{2,1,0:T(4,128)(2,1)S(1)}, u32[]{:S(2)}, u32[]{:S(2)}) %collective-permute-start.2) | collective-permute-done | bytes 196640 | tf_op jit(solution)/shard_map/ppermute | solution.py:27
  16.0 4.0 %collective-permute-start.3 = (bf16[8,4,6144]{2,1,0:T(4,128)(2,1)S(1)}, bf16[8,4,6144]{2,1,0:T(4,128)(2,1)S(1)}, u32[]{:S(2)}, u32[]{:S(2)}) collective-permute-start(bf16[8,4,6144]{2,1,0:T(4,128)(2,1)S(1)} %pad_maximum_fusion.1), channel_id=1, source_target_pairs={{0,1},{1,0},{2,3},{3,2},{4,5},{5,4},{6,7},{7,6},{8,9},{9,8},{10,11... | collective-permute-start | bytes 1179656 | tf_op jit(solution)/shard_map/ppermute | solution.py:27
  20.1 1.3 collective-permute-done.3
  21.6 0.9 copy-done.2
  22.5 7.0 %project.1 = (bf16[48,1024]{1,0:T(8,128)(2,1)}, s32[48,128]{1,0:T(8,128)}) custom-call(s32[1]{0:T(128)} %bitcast.flag_ref, s32[48,1]{1,0:T(8,128)} %add.129.source_ref, bf16[16,4,6144]{2,1,0:T(4,128)(2,1)} %copy-done.2, bf16[6144,1024]{1,0:T(8,128)(2,1)} %w_ref.2), custom_call_target="tpu_custom_call" | custom-call | flops 603979776 | bytes 12582912 | tf_op jit(solution)/shard_map/project/pallas_call | solution.py:73
  29.5 1.7 %collective-permute-start.4 = (bf16[1,48,1024]{2,1,0:T(8,128)(2,1)}, bf16[1,48,1024]{2,1,0:T(8,128)(2,1)S(1)}, u32[]{:S(2)}, u32[]{:S(2)}) collective-permute-start(bf16[1,48,1024]{2,1,0:T(8,128)(2,1)} %bitcast.17), channel_id=1, source_target_pairs={{0,8},{1,9},{2,10},{3,11},{4,12},{5,13},{6,14},{7,15},{8,0},{9,1},... | collective-permute-start | bytes 294920 | tf_op jit(solution)/shard_map/ppermute | solution.py:27
  31.9 5.2 %collective-permute-done.4 = bf16[1,48,1024]{2,1,0:T(8,128)(2,1)S(1)} collective-permute-done((bf16[1,48,1024]{2,1,0:T(8,128)(2,1)}, bf16[1,48,1024]{2,1,0:T(8,128)(2,1)S(1)}, u32[]{:S(2)}, u32[]{:S(2)}) %collective-permute-start.4) | collective-permute-done | bytes 98336 | tf_op jit(solution)/shard_map/ppermute | solution.py:27
  37.0 0.9 pad_maximum_fusion.5
  38.0 0.9 compare_select_fusion
  39.3 4.7 %collective-permute-done.5 = bf16[2,48,1024]{2,1,0:T(8,128)(2,1)S(1)} collective-permute-done((bf16[2,48,1024]{2,1,0:T(8,128)(2,1)S(1)}, bf16[2,48,1024]{2,1,0:T(8,128)(2,1)S(1)}, u32[]{:S(2)}, u32[]{:S(2)}) %collective-permute-start.5) | collective-permute-done | bytes 196640 | tf_op jit(solution)/shard_map/ppermute | solution.py:27
  44.0 0.9 pad_maximum_fusion.2
  45.8 8.5 %collective-permute-done.6 = bf16[4,48,1024]{2,1,0:T(8,128)(2,1)S(1)} collective-permute-done((bf16[4,48,1024]{2,1,0:T(8,128)(2,1)S(1)}, bf16[4,48,1024]{2,1,0:T(8,128)(2,1)S(1)}, u32[]{:S(2)}, u32[]{:S(2)}) %collective-permute-start.6) | collective-permute-done | bytes 393248 | tf_op jit(solution)/shard_map/ppermute | solution.py:27
  54.3 1.0 pad_maximum_fusion
  55.3 2.3 %collective-permute-start.7 = (bf16[8,48,1024]{2,1,0:T(8,128)(2,1)S(1)}, bf16[8,48,1024]{2,1,0:T(8,128)(2,1)S(1)}, u32[]{:S(2)}, u32[]{:S(2)}) collective-permute-start(bf16[8,48,1024]{2,1,0:T(8,128)(2,1)S(1)} %pad_maximum_fusion), channel_id=1, source_target_pairs={{0,1},{1,0},{2,3},{3,2},{4,5},{5,4},{6,7},{7,6},{8,9},{9,8},{10,11... | collective-permute-start | bytes 2359304 | tf_op jit(solution)/shard_map/ppermute | solution.py:27
  58.2 1.3 collective-permute-done.7
  59.6 1.2 copy-done
  60.8 9.2 %readout.1 = (bf16[192,128]{1,0:T(8,128)(2,1)}, f32[192,128]{1,0:T(8,128)}, f32[192,128]{1,0:T(8,128)}) custom-call(s32[32]{0:T(128)} %pad_add_fusion.order_ref, s32[192]{0:T(256)} %reshape.129.slot_ref, s32[192]{0:T(256)} %get-tuple-element.12.row_ref, s32[192]{0:T(256)} %get-tuple-element.13.head_ref, f32[32]{0:T(128)} %negate_exponential_fusion.decay_ref, ...), custom_call_target="tpu_custom_call" | custom-call | flops 6291456 | bytes 5505024 | tf_op jit(solution)/shard_map/readout/pallas_call | solution.py:188
  70.1 5.6 %collective-permute-done.8 = bf16[1,192,128]{2,1,0:T(8,128)(2,1)S(1)} collective-permute-done((bf16[1,192,128]{2,1,0:T(8,128)(2,1)}, bf16[1,192,128]{2,1,0:T(8,128)(2,1)S(1)}, u32[]{:S(2)}, u32[]{:S(2)}) %collective-permute-start.8) | collective-permute-done | bytes 49184 | tf_op jit(solution)/shard_map/ppermute | solution.py:27
  75.7 0.8 pad_maximum_fusion.8
  76.6 3.5 %collective-permute-done.9 = bf16[2,192,128]{2,1,0:T(8,128)(2,1)S(1)} collective-permute-done((bf16[2,192,128]{2,1,0:T(8,128)(2,1)S(1)}, bf16[2,192,128]{2,1,0:T(8,128)(2,1)S(1)}, u32[]{:S(2)}, u32[]{:S(2)}) %collective-permute-start.9) | collective-permute-done | bytes 98336 | tf_op jit(solution)/shard_map/ppermute | solution.py:27
  80.0 0.8 pad_maximum_fusion.6
  82.5 2.9 %collective-permute-done.10 = bf16[4,192,128]{2,1,0:T(8,128)(2,1)S(1)} collective-permute-done((bf16[4,192,128]{2,1,0:T(8,128)(2,1)S(1)}, bf16[4,192,128]{2,1,0:T(8,128)(2,1)S(1)}, u32[]{:S(2)}, u32[]{:S(2)}) %collective-permute-start.10) | collective-permute-done | bytes 196640 | tf_op jit(solution)/shard_map/ppermute | solution.py:27
  85.4 0.8 pad_maximum_fusion.3
  86.3 3.1 %collective-permute-start.11 = (bf16[8,192,128]{2,1,0:T(8,128)(2,1)S(1)}, bf16[8,192,128]{2,1,0:T(8,128)(2,1)S(1)}, u32[]{:S(2)}, u32[]{:S(2)}) collective-permute-start(bf16[8,192,128]{2,1,0:T(8,128)(2,1)S(1)} %pad_maximum_fusion.3), channel_id=1, source_target_pairs={{0,1},{1,0},{2,3},{3,2},{4,5},{5,4},{6,7},{7,6},{8,9},{9,8},{10,11... | collective-permute-start | bytes 1179656 | tf_op jit(solution)/shard_map/ppermute | solution.py:27
  89.3 0.8 constant_dynamic-update-slice_fusion.14
  90.1 37.6 %update.1 = bf16[168,128,128]{2,1,0:T(8,128)(2,1)} custom-call(s32[192]{0:T(256)} %reshape.129.slot_ref, s32[192]{0:T(256)} %get-tuple-element.13.head_ref, f32[32]{0:T(128)} %negate_exponential_fusion.decay_ref, f32[168]{0:T(256)} %broadcast_divide_fusion.1.inverse_ref, f32[192,128]{1,0:T(8,128)} %get-tuple-element.10.key_ref, ...), custom_call_target="tpu_custom_call" | custom-call | flops 11010048 | bytes 11010048 | tf_op jit(solution)/shard_map/update/pallas_call | solution.py:242
  127.9 0.9 copy-done.3
  128.7 5.7 %finish.1 = bf16[48,384]{1,0:T(8,128)(2,1)} custom-call(s32[32]{0:T(128)} %pad_add_fusion.order_ref, s32[1536]{0:T(1024)} %reshape.128.pick_ref, bf16[16,192,128]{2,1,0:T(8,128)(2,1)} %copy-done.3, bf16[16,48,1024]{2,1,0:T(8,128)(2,1)} %copy-done, f32[32,128]{1,0:T(8,128)} %bitcast.25, bf16[4096,384]{1,0:T(8,128)(2,1)} %w_ref.3), custom_call_target="tpu_custom_call" | custom-call | flops 150994944 | bytes 3145728 | tf_op jit(solution)/shard_map/finish/pallas_call | solution.py:302
  (64 shorter events, 9.9 us)
Async XLA Ops:
  2.9 4.5 %collective-permute-start = (bf16[1,4,6144]{2,1,0:T(4,128)(2,1)S(1)}, bf16[1,4,6144]{2,1,0:T(4,128)(2,1)S(1)}, u32[]{:S(2)}, u32[]{:S(2)}) collective-permute-start(bf16[1,4,6144]{2,1,0:T(4,128)(2,1)S(1)} %get-tuple-element.15), channel_id=1, source_target_pairs={{0,8},{1,9},{2,10},{3,11},{4,12},{5,13},{6,14},{7,15},{8,0},{9,1},... | collective-permute-start | bytes 147464 | tf_op jit(solution)/shard_map/ppermute | solution.py:27
  7.5 3.5 %collective-permute-start.1 = (bf16[2,4,6144]{2,1,0:T(4,128)(2,1)S(1)}, bf16[2,4,6144]{2,1,0:T(4,128)(2,1)S(1)}, u32[]{:S(2)}, u32[]{:S(2)}) collective-permute-start(bf16[2,4,6144]{2,1,0:T(4,128)(2,1)S(1)} %pad_maximum_fusion.7), channel_id=1, source_target_pairs={{0,4},{1,5},{2,6},{3,7},{4,0},{5,1},{6,2},{7,3},{8,12},{9,13},{10,... | collective-permute-start | bytes 294920 | tf_op jit(solution)/shard_map/ppermute | solution.py:27
  11.2 4.6 %collective-permute-start.2 = (bf16[4,4,6144]{2,1,0:T(4,128)(2,1)S(1)}, bf16[4,4,6144]{2,1,0:T(4,128)(2,1)S(1)}, u32[]{:S(2)}, u32[]{:S(2)}) collective-permute-start(bf16[4,4,6144]{2,1,0:T(4,128)(2,1)S(1)} %pad_maximum_fusion.4), channel_id=1, source_target_pairs={{0,2},{1,3},{2,0},{3,1},{4,6},{5,7},{6,4},{7,5},{8,10},{9,11},{10,... | collective-permute-start | bytes 589832 | tf_op jit(solution)/shard_map/ppermute | solution.py:27
  16.0 5.3 %collective-permute-start.3 = (bf16[8,4,6144]{2,1,0:T(4,128)(2,1)S(1)}, bf16[8,4,6144]{2,1,0:T(4,128)(2,1)S(1)}, u32[]{:S(2)}, u32[]{:S(2)}) collective-permute-start(bf16[8,4,6144]{2,1,0:T(4,128)(2,1)S(1)} %pad_maximum_fusion.1), channel_id=1, source_target_pairs={{0,1},{1,0},{2,3},{3,2},{4,5},{5,4},{6,7},{7,6},{8,9},{9,8},{10,11... | collective-permute-start | bytes 1179656 | tf_op jit(solution)/shard_map/ppermute | solution.py:27
  21.6 0.9 copy-start.2
  29.5 28.7 %copy-start.1 = (bf16[48,1024]{1,0:T(8,128)(2,1)S(1)}, bf16[48,1024]{1,0:T(8,128)(2,1)}, u32[]{:S(2)}) copy-start(bf16[48,1024]{1,0:T(8,128)(2,1)} %get-tuple-element.8) | copy-start | bytes 294916
  29.5 7.5 %collective-permute-start.4 = (bf16[1,48,1024]{2,1,0:T(8,128)(2,1)}, bf16[1,48,1024]{2,1,0:T(8,128)(2,1)S(1)}, u32[]{:S(2)}, u32[]{:S(2)}) collective-permute-start(bf16[1,48,1024]{2,1,0:T(8,128)(2,1)} %bitcast.17), channel_id=1, source_target_pairs={{0,8},{1,9},{2,10},{3,11},{4,12},{5,13},{6,14},{7,15},{8,0},{9,1},... | collective-permute-start | bytes 294920 | tf_op jit(solution)/shard_map/ppermute | solution.py:27
  38.0 6.1 %collective-permute-start.5 = (bf16[2,48,1024]{2,1,0:T(8,128)(2,1)S(1)}, bf16[2,48,1024]{2,1,0:T(8,128)(2,1)S(1)}, u32[]{:S(2)}, u32[]{:S(2)}) collective-permute-start(bf16[2,48,1024]{2,1,0:T(8,128)(2,1)S(1)} %pad_maximum_fusion.5), channel_id=1, source_target_pairs={{0,4},{1,5},{2,6},{3,7},{4,0},{5,1},{6,2},{7,3},{8,12},{9,13},{10,... | collective-permute-start | bytes 589832 | tf_op jit(solution)/shard_map/ppermute | solution.py:27
  45.0 9.4 %collective-permute-start.6 = (bf16[4,48,1024]{2,1,0:T(8,128)(2,1)S(1)}, bf16[4,48,1024]{2,1,0:T(8,128)(2,1)S(1)}, u32[]{:S(2)}, u32[]{:S(2)}) collective-permute-start(bf16[4,48,1024]{2,1,0:T(8,128)(2,1)S(1)} %pad_maximum_fusion.2), channel_id=1, source_target_pairs={{0,2},{1,3},{2,0},{3,1},{4,6},{5,7},{6,4},{7,5},{8,10},{9,11},{10,... | collective-permute-start | bytes 1179656 | tf_op jit(solution)/shard_map/ppermute | solution.py:27
  55.3 4.2 %collective-permute-start.7 = (bf16[8,48,1024]{2,1,0:T(8,128)(2,1)S(1)}, bf16[8,48,1024]{2,1,0:T(8,128)(2,1)S(1)}, u32[]{:S(2)}, u32[]{:S(2)}) collective-permute-start(bf16[8,48,1024]{2,1,0:T(8,128)(2,1)S(1)} %pad_maximum_fusion), channel_id=1, source_target_pairs={{0,1},{1,0},{2,3},{3,2},{4,5},{5,4},{6,7},{7,6},{8,9},{9,8},{10,11... | collective-permute-start | bytes 2359304 | tf_op jit(solution)/shard_map/ppermute | solution.py:27
  59.6 1.2 copy-start
  60.8 20.4 %copy-start.4 = (f32[168]{0:T(256)S(1)}, f32[168]{0:T(256)}, u32[]{:S(2)}) copy-start(f32[168]{0:T(256)} %scale_ref.1) | copy-start | bytes 2020
  70.0 5.7 %collective-permute-start.8 = (bf16[1,192,128]{2,1,0:T(8,128)(2,1)}, bf16[1,192,128]{2,1,0:T(8,128)(2,1)S(1)}, u32[]{:S(2)}, u32[]{:S(2)}) collective-permute-start(bf16[1,192,128]{2,1,0:T(8,128)(2,1)} %bitcast.21), channel_id=1, source_target_pairs={{0,8},{1,9},{2,10},{3,11},{4,12},{5,13},{6,14},{7,15},{8,0},{9,1},... | collective-permute-start | bytes 147464 | tf_op jit(solution)/shard_map/ppermute | solution.py:27
  76.5 3.5 %collective-permute-start.9 = (bf16[2,192,128]{2,1,0:T(8,128)(2,1)S(1)}, bf16[2,192,128]{2,1,0:T(8,128)(2,1)S(1)}, u32[]{:S(2)}, u32[]{:S(2)}) collective-permute-start(bf16[2,192,128]{2,1,0:T(8,128)(2,1)S(1)} %pad_maximum_fusion.8), channel_id=1, source_target_pairs={{0,4},{1,5},{2,6},{3,7},{4,0},{5,1},{6,2},{7,3},{8,12},{9,13},{10,... | collective-permute-start | bytes 294920 | tf_op jit(solution)/shard_map/ppermute | solution.py:27
  80.8 4.6 %collective-permute-start.10 = (bf16[4,192,128]{2,1,0:T(8,128)(2,1)S(1)}, bf16[4,192,128]{2,1,0:T(8,128)(2,1)S(1)}, u32[]{:S(2)}, u32[]{:S(2)}) collective-permute-start(bf16[4,192,128]{2,1,0:T(8,128)(2,1)S(1)} %pad_maximum_fusion.6), channel_id=1, source_target_pairs={{0,2},{1,3},{2,0},{3,1},{4,6},{5,7},{6,4},{7,5},{8,10},{9,11},{10,... | collective-permute-start | bytes 589832 | tf_op jit(solution)/shard_map/ppermute | solution.py:27
  86.3 41.5 %collective-permute-start.11 = (bf16[8,192,128]{2,1,0:T(8,128)(2,1)S(1)}, bf16[8,192,128]{2,1,0:T(8,128)(2,1)S(1)}, u32[]{:S(2)}, u32[]{:S(2)}) collective-permute-start(bf16[8,192,128]{2,1,0:T(8,128)(2,1)S(1)} %pad_maximum_fusion.3), channel_id=1, source_target_pairs={{0,1},{1,0},{2,3},{3,2},{4,5},{5,4},{6,7},{7,6},{8,9},{9,8},{10,11... | collective-permute-start | bytes 1179656 | tf_op jit(solution)/shard_map/ppermute | solution.py:27
  127.9 0.9 copy-start.3

commit v2 on v0

v2 whole, which is shorter than its diff:
```python
import functools

import jax
import jax.numpy as jnp
from jax import lax
from jax.experimental import pallas as pl
from jax.experimental.pallas import tpu as pltpu
from jax.sharding import PartitionSpec as P

VMEM_LIMIT = 60 * 1024 * 1024
BF16 = jnp.bfloat16
F32 = jnp.float32
I32 = jnp.int32
SMEM = pl.BlockSpec(memory_space=pltpu.SMEM)
VMEM = pl.BlockSpec(memory_space=pltpu.VMEM)
ANY = pl.BlockSpec(memory_space=pl.ANY)


def block_order(devices):
    order, bit = [0], devices // 2
    while bit >= 1:
        order = order + [o ^ bit for o in order]
        bit //= 2
    return order


def gather_pieces(block, devices):
    held, bit = [block], devices // 2
    while bit >= 1:
        pairs = [(i, i ^ bit) for i in range(devices)]
        held = held + [lax.ppermute(piece, "batch", pairs) for piece in held]
        bit //= 2
    return held


def pack_kernel(heads, tokens_ref, holder_ref, rank_ref, out_ref):
    own, width = tokens_ref.shape
    parts = []
    for i in range(own):
        parts.append(holder_ref[i : i + 1, :].astype(F32))
        parts.append(rank_ref[i : i + 1, :].astype(F32))
        parts.append(jnp.zeros((1, 128 - 2 * heads), F32))
    parts.append(jnp.zeros((1, width - own * 128), F32))
    table = jnp.concatenate(parts, axis=1)
    block = jnp.concatenate([tokens_ref[...].astype(F32), table], axis=0)
    out_ref[...] = block.astype(BF16)


def pack(tokens, holder, rank):
    own, width = tokens.shape
    return pl.pallas_call(
        functools.partial(pack_kernel, holder.shape[1]),
        out_shape=jax.ShapeDtypeStruct((own + 1, width), BF16),
        in_specs=[VMEM] * 3,
        out_specs=VMEM,
        name="pack",
    )(tokens, holder, rank)


def project_kernel(devices, heads, slots, steps, *refs):
    me_ref, send_ref, w_ref = refs[:3]
    pieces = refs[3 : 3 + devices]
    act_ref, pick_ref, slot_ref, rows, wbuf, sems = refs[3 + devices :]
    order = block_order(devices)
    bits = devices.bit_length() - 1
    sessions, cols = act_ref.shape
    own = sessions // devices
    capacity = send_ref.shape[1]
    width = w_ref.shape[0]
    chunk = width // steps
    me = me_ref[0]
    copies = []
    for step in range(steps):
        part = pl.ds(step * chunk, chunk)
        copies.append(pltpu.make_async_copy(w_ref.at[part], wbuf.at[part], sems.at[step]))
        copies[-1].start()

    lane = lax.broadcasted_iota(I32, (1, sessions), 1)
    target = jnp.zeros((1, sessions), I32)
    source = jnp.zeros((1, sessions), I32)
    indices = []
    for j in range(devices):
        block = pieces[j][...].astype(F32)
        rows[j * own : (j + 1) * own, :] = block[:own]
        for i in range(own):
            indices.append(block[own : own + 1, i * 128 : (i + 1) * 128])
        inside = (lane >= j * own) & (lane < (j + 1) * own)
        target = jnp.where(inside, lane + ((me ^ order[j]) - j) * own, target)
        crossed = me ^ j
        position = jnp.int32(0)
        for k in range(bits):
            position = position + (((crossed >> k) & 1) << (bits - 1 - k))
        source = jnp.where(inside, lane + (position - j) * own, source)
    grid_row = lax.broadcasted_iota(I32, (sessions, sessions), 0)
    place = (grid_row == target).astype(F32).astype(BF16)
    place_t = (grid_row == source).astype(F32).astype(BF16)

    table = jnp.concatenate(indices, axis=0)
    table = jnp.dot(table.T.astype(BF16), place_t, preferred_element_type=F32).astype(I32)
    holder = table[:heads]
    rank = table[heads : 2 * heads]
    owner = (lane * (65536 // own + 1)) >> 16
    pick_ref[...] = (holder * devices + owner) * capacity + rank

    owner_row = lax.broadcasted_iota(I32, (devices, sessions), 0)
    spread = (owner_row == owner).astype(F32).astype(BF16)
    sent = send_ref[...].astype(F32).T.astype(BF16)
    sent = jnp.dot(sent, spread, preferred_element_type=F32).astype(I32)
    slot = jnp.full((heads, sessions), -1, I32)
    for r in range(capacity):
        slot = jnp.where(rank == r, sent[r : r + 1, :], slot)
    slot = jnp.where(holder == me, slot, -1)
    entry = owner * capacity + rank
    padded = slot_ref.shape[1]
    slot_lane = lax.broadcasted_iota(I32, (heads, padded), 1)
    head_row = lax.broadcasted_iota(I32, (heads, padded), 0)
    found = jnp.zeros((heads, padded), I32)
    found_entry = jnp.zeros((heads, padded), I32)
    for s in range(sessions):
        same = slot[:, s : s + 1] == slot_lane
        found = jnp.where(same, head_row * sessions + (s + 1), found)
        found_entry = jnp.where(same, entry[:, s : s + 1], found_entry)
    code = jnp.sum(found.astype(F32), axis=0, keepdims=True).astype(I32) - 1
    code_entry = jnp.sum(found_entry.astype(F32), axis=0, keepdims=True).astype(I32)
    used = code >= 0
    head = jnp.sum((found > 0).astype(F32) * head_row.astype(F32), axis=0, keepdims=True)
    slot_ref[0:1, :] = jnp.where(used, code, 3 * heads * sessions)
    slot_ref[1:2, :] = jnp.where(used, head.astype(I32), -1)
    slot_ref[2:3, :] = jnp.where(used, code_entry, devices * capacity)
    slot_ref[3:8, :] = jnp.zeros((5, padded), I32)

    total = jnp.zeros(act_ref.shape, F32)
    for step in range(steps):
        copies[step].wait()
        part = slice(step * chunk, (step + 1) * chunk)
        total += jnp.dot(rows[:, part].astype(BF16), wbuf[part, :], preferred_element_type=F32)
    gate = jax.nn.sigmoid(total)
    is_gate = me * cols >= 3 * heads * 128
    active = jnp.where(is_gate, gate, total * gate).astype(BF16)
    act_ref[...] = jnp.dot(place, active, preferred_element_type=F32).astype(BF16)


def project(pieces, w, me, send, heads, slots):
    devices = len(pieces)
    own = pieces[0].shape[0] - 1
    sessions = own * devices
    width, cols = w.shape
    steps = 8
    padded = (slots + 127) // 128 * 128
    return pl.pallas_call(
        functools.partial(project_kernel, devices, heads, slots, steps),
        out_shape=(
            jax.ShapeDtypeStruct((sessions, cols), BF16),
            jax.ShapeDtypeStruct((heads, sessions), I32),
            jax.ShapeDtypeStruct((8, padded), I32),
        ),
        in_specs=[SMEM, VMEM, ANY] + [VMEM] * devices,
        out_specs=(VMEM, VMEM, VMEM),
        scratch_shapes=[
            pltpu.VMEM((sessions, width), F32),
            pltpu.VMEM(w.shape, BF16),
            pltpu.SemaphoreType.DMA((steps,)),
        ],
        compiler_params=pltpu.CompilerParams(vmem_limit_bytes=VMEM_LIMIT),
        cost_estimate=pl.CostEstimate(
            flops=2 * sessions * width * cols, bytes_accessed=2 * width * cols, transcendentals=0
        ),
        name="project",
    )(me, send, w, *pieces)


def advance_kernel(devices, heads, chunks, *refs):
    me_ref, slot_ref, rate_ref, scale_ref, cache_ref = refs[:5]
    pieces = refs[5 : 5 + devices]
    (read_ref, gate_ref, out_ref, flat, tiles, fresh, query, keys, values, reads, in_sems, out_sems) = refs[
        5 + devices :
    ]
    order = block_order(devices)
    sessions, cols = pieces[0].shape
    per = cols // 128
    slots = cache_ref.shape[0]
    step = slots // chunks
    me = me_ref[0]
    copies, backs = [], []
    for c in range(chunks):
        part = pl.ds(c * step, step)
        copies.append(pltpu.make_async_copy(cache_ref.at[part], tiles.at[part], in_sems.at[c]))
        backs.append(pltpu.make_async_copy(fresh.at[part], out_ref.at[part], out_sems.at[c]))
        copies[-1].start()
    first = 3 * devices // 4
    last_row = 3 * heads * sessions
    flat[last_row : last_row + 8, :] = jnp.zeros((8, 128), F32)
    for j in range(devices):
        device = me ^ order[j]

        @pl.when(device < first)
        def _():
            base = pl.multiple_of(device * (per * sessions), 8)
            for b in range(per):
                flat[pl.ds(base + b * sessions, sessions), :] = pieces[j][
                    :, b * 128 : (b + 1) * 128
                ].astype(F32)

        @pl.when(device >= first)
        def _():
            gate_ref[device - first] = pieces[j][...]

    comp = heads * sessions

    @pl.loop(0, slots // 8)
    def _(group):
        for u in range(8):
            e = group * 8 + u
            row = slot_ref[0, e]
            query[pl.ds(e, 1), :] = flat[pl.ds(row, 1), :]
            keys[pl.ds(e, 1), :] = flat[pl.ds(jnp.minimum(row + comp, last_row), 1), :]
            values[pl.ds(e, 1), :] = flat[pl.ds(jnp.minimum(row + 2 * comp, last_row), 1), :]

    rows8 = lax.broadcasted_iota(I32, (8, 128), 0)

    def advance(group):
        base = pl.multiple_of(group * 8, 8)
        q8 = query[pl.ds(base, 8), :]
        k8 = keys[pl.ds(base, 8), :]
        v8 = values[pl.ds(base, 8), :]
        rate = jnp.zeros((8, 128), F32)
        scale = jnp.ones((8, 128), F32)
        for u in range(8):
            head = slot_ref[1, base + u]
            one = jnp.where(head < 0, 0.0, rate_ref[jnp.maximum(head, 0)])
            rate = jnp.where(rows8 == u, one, rate)
            scale = jnp.where(rows8 == u, scale_ref[base + u], scale)
        decay = jnp.exp(-rate)
        scaled = v8 * (1.0 / scale)
        high = scaled.astype(BF16)
        rest = scaled - high.astype(F32)
        middle = rest.astype(BF16)
        low = (rest - middle.astype(F32)).astype(BF16)
        zero = jnp.zeros((8, 128), BF16)
        spread = [
            jnp.concatenate([jnp.where(rows8 == u, t.astype(F32), 0.0) for u in range(8)], axis=1)
            for t in (high, middle, low, zero)
        ]
        spread = jnp.concatenate(spread, axis=0).astype(BF16)
        k32 = jnp.concatenate([k8, k8, k8, k8], axis=0).T.astype(BF16)
        outer = jnp.dot(k32, spread, preferred_element_type=F32)
        wide = jnp.concatenate([tiles[base + u] for u in range(8)], axis=1)
        prod = jnp.dot(q8.astype(BF16), wide, preferred_element_type=F32)
        seen = jnp.zeros((8, 128), F32)
        for u in range(8):
            part = slice(u * 128, (u + 1) * 128)
            seen = jnp.where(rows8 == u, prod[:, part], seen)
            fresh[base + u] = (
                decay[u : u + 1, :] * wide[:, part].astype(F32) + outer[:, part]
            ).astype(BF16)
        near = jnp.sum(q8 * k8, axis=1, keepdims=True)
        result = seen * (decay * scale) + near * v8
        for u in range(8):
            reads[pl.ds(slot_ref[2, base + u], 1), :] = result[u : u + 1, :]

    for c in range(chunks):
        copies[c].wait()
        pl.loop(c * (step // 8), (c + 1) * (step // 8))(advance)
        backs[c].start()
    entries = read_ref.shape[0]
    read_ref[...] = reads[:entries, :].astype(BF16)
    for back in backs:
        back.wait()


def advance_tiles(pieces, cache, me, slot, rate, scale, heads, capacity):
    devices = len(pieces)
    entries = devices * capacity
    sessions, cols = pieces[0].shape
    slots = cache.shape[0]
    chunks = 7 if slots % 56 == 0 else 1
    return pl.pallas_call(
        functools.partial(advance_kernel, devices, heads, chunks),
        out_shape=(
            jax.ShapeDtypeStruct((entries, 128), BF16),
            jax.ShapeDtypeStruct((devices // 4, sessions, cols), BF16),
            jax.ShapeDtypeStruct(cache.shape, BF16),
        ),
        in_specs=[SMEM] * 4 + [ANY] + [VMEM] * devices,
        out_specs=(VMEM, VMEM, ANY),
        scratch_shapes=[
            pltpu.VMEM((3 * heads * sessions + 8, 128), F32),
            pltpu.VMEM(cache.shape, BF16),
            pltpu.VMEM(cache.shape, BF16),
            pltpu.VMEM((slots, 128), F32),
            pltpu.VMEM((slots, 128), F32),
            pltpu.VMEM((slots, 128), F32),
            pltpu.VMEM((entries + 8, 128), F32),
            pltpu.SemaphoreType.DMA((chunks,)),
            pltpu.SemaphoreType.DMA((chunks,)),
        ],
        compiler_params=pltpu.CompilerParams(vmem_limit_bytes=VMEM_LIMIT),
        cost_estimate=pl.CostEstimate(
            flops=4 * cache.size, bytes_accessed=4 * cache.size, transcendentals=0
        ),
        name="advance",
    )(me, slot, rate, scale, cache, *pieces)


def finish_kernel(devices, *refs):
    me_ref, pick_ref, gate_ref, gain_ref, w_ref = refs[:5]
    pieces = refs[5 : 5 + devices]
    out_ref, flat, hidden, merged, wbuf, sem = refs[5 + devices :]
    order = block_order(devices)
    entries = pieces[0].shape[0]
    sessions = gate_ref.shape[1]
    per = gate_ref.shape[2] // 128
    heads = merged.shape[1] // 128
    me = me_ref[0]
    copy = pltpu.make_async_copy(w_ref, wbuf, sem)
    copy.start()
    for j in range(devices):
        base = pl.multiple_of((me ^ order[j]) * entries, 8)
        flat[pl.ds(base, entries), :] = pieces[j][...].astype(F32)

    @pl.loop(0, heads)
    def _(h):
        base = pl.multiple_of(h * sessions, 8)
        for s in range(sessions):
            hidden[pl.ds(base + s, 1), :] = flat[pl.ds(pick_ref[h, s], 1), :]

    squares = jnp.zeros((sessions, 128), F32)
    for h in range(heads):
        block = hidden[h * sessions : (h + 1) * sessions, :]
        squares += block * block
    mean = jnp.sum(squares, axis=1, keepdims=True) * (1.0 / (heads * 128))
    norm = lax.rsqrt(mean + 1e-6)
    for h in range(heads):
        block = hidden[h * sessions : (h + 1) * sessions, :]
        gate = gate_ref[h // per, :, (h % per) * 128 : (h % per + 1) * 128]
        block = block * norm * gain_ref[h : h + 1, :] * gate.astype(F32)
        merged[:, h * 128 : (h + 1) * 128] = block.astype(BF16)
    copy.wait()
    out_ref[...] = jnp.dot(merged[...], wbuf[...], preferred_element_type=F32).astype(BF16)


def finish(pieces, gates, me, pick, gain, w_out):
    devices = len(pieces)
    entries = pieces[0].shape[0]
    sessions = gates.shape[1]
    width = w_out.shape[0]
    return pl.pallas_call(
        functools.partial(finish_kernel, devices),
        out_shape=jax.ShapeDtypeStruct((sessions, w_out.shape[1]), BF16),
        in_specs=[SMEM, SMEM, VMEM, VMEM, ANY] + [VMEM] * devices,
        out_specs=VMEM,
        scratch_shapes=[
            pltpu.VMEM((devices * entries, 128), F32),
            pltpu.VMEM((sessions * width // 128, 128), F32),
            pltpu.VMEM((sessions, width), BF16),
            pltpu.VMEM(w_out.shape, BF16),
            pltpu.SemaphoreType.DMA,
        ],
        compiler_params=pltpu.CompilerParams(vmem_limit_bytes=VMEM_LIMIT),
        cost_estimate=pl.CostEstimate(
            flops=2 * sessions * w_out.size, bytes_accessed=2 * w_out.size, transcendentals=0
        ),
        name="finish",
    )(me, pick, gates, gain, w_out, *pieces)


def on_device(
    tokens,
    w_proj,
    w_out,
    decay_rate,
    norm_gain,
    cache_tiles,
    tile_scales,
    tile_holder,
    tile_rank,
    send_slot,
):
    devices = lax.axis_size("batch")
    me = lax.axis_index("batch").astype(I32).reshape(1)
    heads = decay_rate.shape[0]
    capacity = send_slot.shape[-1]
    slots = cache_tiles.shape[0]

    tokens_all = gather_pieces(pack(tokens, tile_holder, tile_rank), devices)
    act, pick, slot = project(tokens_all, w_proj, me, send_slot[0], heads, slots)
    act_all = gather_pieces(act, devices)
    read, gates, new_cache = advance_tiles(
        act_all, cache_tiles, me, slot, decay_rate, tile_scales, heads, capacity
    )
    read_all = gather_pieces(read, devices)
    mixed_out = finish(read_all, gates, me, pick, norm_gain.reshape(heads, 128), w_out)
    return (mixed_out, new_cache)


def solution(mesh):
    return jax.shard_map(
        on_device,
        mesh=mesh,
        in_specs=(
            P(("groups", "batch"), None),
            P(None, "batch"),
            P(None, "batch"),
            P(),
            P(),
            P(("groups", "batch"), None, None),
            P(("groups", "batch")),
            P(("groups", "batch"), None),
            P(("groups", "batch"), None),
            P(("groups", "batch"), None, None),
        ),
        out_specs=(P("groups", "batch"), P(("groups", "batch"), None, None)),
        check_vma=False,
    )
```

time: 428 us -> 80.6 us (0.19)
  the two profiles are of different devices: /device:TPU:13 before, /device:TPU:0 now
where the time goes in v2:
time: 80.6 us; the launch traced here: 80.1 us
  starting transfers between devices  29.9 us (37%)
  Pallas kernels  23.8 us (30%)
  waiting for transfers between devices  22.2 us (28%)
  local copies, waits for them, and re-layouts  3.07 us (4%)
  between operations  1.18 us (1%)
    ppermute x45, starting transfers between devices, gather_pieces(): held = held + [lax.ppermute(piece, 'batch', pairs) for piece in held]  29.9 us
    ppermute x45, waiting for transfers between devices, gather_pieces(): held = held + [lax.ppermute(piece, 'batch', pairs) for piece in held]  22.2 us
    pallas_call x1, Pallas kernels, advance_tiles(): pl.pallas_call(functools.partial(advance_kernel, devices, heads, chunks),...  10.6 us
    pallas_call x1, Pallas kernels, project(): pl.pallas_call(functools.partial(project_kernel, devices, heads, slots, s...  7.29 us
    pallas_call x1, Pallas kernels, finish(): pl.pallas_call(functools.partial(finish_kernel, devices), out_shape=jax.S...  4.36 us
    unnamed x91, local copies, waits for them, and re-layouts  3.07 us
  transfers between devices with their start and end apart: 45, of which 19 were waited for; matrix products, arithmetic and copies ran while one was open for 2% of the time, Pallas kernels for 0%

profile of v2, /device:TPU:0, one launch (start us, length us, event | category | flops | bytes accessed | tf_op | source)
XLA Modules:
  0.0 80.1 jit_solution(15863263285119838939)
XLA Ops:
  0.6 1.5 %pack.1.refs_3_ = bf16[4,6144]{1,0:T(4,128)(2,1)} custom-call(bf16[3,6144]{1,0:T(4,128)(2,1)} %tokens_ref.1, s32[3,32]{1,0:T(4,128)} %holder_ref.1, s32[3,32]{1,0:T(4,128)} %rank_ref.1), custom_call_target="tpu_custom_call" | custom-call | tf_op jit(solution)/shard_map/pack/pallas_call | solution.py:51
  2.1 4.0 %collective-permute-start = (bf16[4,6144]{1,0:T(4,128)(2,1)}, bf16[4,6144]{1,0:T(4,128)(2,1)S(1)}, u32[]{:S(2)}, u32[]{:S(2)}) collective-permute-start(bf16[4,6144]{1,0:T(4,128)(2,1)} %pack.1.refs_3_), channel_id=1, source_target_pairs={{0,8},{1,9},{2,10},{3,11},{4,12},{5,13},{6,14},{7,15},{8,0},{9,1},... | collective-permute-start | bytes 147464 | tf_op jit(solution)/shard_map/ppermute | solution.py:31
  6.2 1.5 %collective-permute-start.3 = (bf16[4,6144]{1,0:T(4,128)(2,1)}, bf16[4,6144]{1,0:T(4,128)(2,1)S(1)}, u32[]{:S(2)}, u32[]{:S(2)}) collective-permute-start(bf16[4,6144]{1,0:T(4,128)(2,1)} %pack.1.refs_3_), channel_id=1, source_target_pairs={{0,2},{1,3},{2,0},{3,1},{4,6},{5,7},{6,4},{7,5},{8,10},{9,11},{10,... | collective-permute-start | bytes 147464 | tf_op jit(solution)/shard_map/ppermute | solution.py:31
  7.7 1.6 %collective-permute-start.1 = (bf16[4,6144]{1,0:T(4,128)(2,1)}, bf16[4,6144]{1,0:T(4,128)(2,1)S(1)}, u32[]{:S(2)}, u32[]{:S(2)}) collective-permute-start(bf16[4,6144]{1,0:T(4,128)(2,1)} %pack.1.refs_3_), channel_id=1, source_target_pairs={{0,4},{1,5},{2,6},{3,7},{4,0},{5,1},{6,2},{7,3},{8,12},{9,13},{10,... | collective-permute-start | bytes 147464 | tf_op jit(solution)/shard_map/ppermute | solution.py:31
  9.3 1.4 %collective-permute-start.2 = (bf16[4,6144]{1,0:T(4,128)(2,1)S(1)}, bf16[4,6144]{1,0:T(4,128)(2,1)S(1)}, u32[]{:S(2)}, u32[]{:S(2)}) collective-permute-start(bf16[4,6144]{1,0:T(4,128)(2,1)S(1)} %collective-permute-done.refs_4_), channel_id=1, source_target_pairs={{0,4},{1,5},{2,6},{3,7},{4,0},{5,1},{6,2},{7,3},{8,12},{9,13},{10,... | collective-permute-start | bytes 147464 | tf_op jit(solution)/shard_map/ppermute | solution.py:31
  10.7 1.3 %collective-permute-done.1.refs_5_ = bf16[4,6144]{1,0:T(4,128)(2,1)S(1)} collective-permute-done((bf16[4,6144]{1,0:T(4,128)(2,1)}, bf16[4,6144]{1,0:T(4,128)(2,1)S(1)}, u32[]{:S(2)}, u32[]{:S(2)}) %collective-permute-start.1) | collective-permute-done | bytes 49184 | tf_op jit(solution)/shard_map/ppermute | solution.py:31
  12.5 1.5 %collective-permute-start.4 = (bf16[4,6144]{1,0:T(4,128)(2,1)S(1)}, bf16[4,6144]{1,0:T(4,128)(2,1)S(1)}, u32[]{:S(2)}, u32[]{:S(2)}) collective-permute-start(bf16[4,6144]{1,0:T(4,128)(2,1)S(1)} %collective-permute-done.refs_4_), channel_id=1, source_target_pairs={{0,2},{1,3},{2,0},{3,1},{4,6},{5,7},{6,4},{7,5},{8,10},{9,11},{10,... | collective-permute-start | bytes 147464 | tf_op jit(solution)/shard_map/ppermute | solution.py:31
  14.0 0.8 %collective-permute-start.6 = (bf16[4,6144]{1,0:T(4,128)(2,1)S(1)}, bf16[4,6144]{1,0:T(4,128)(2,1)S(1)}, u32[]{:S(2)}, u32[]{:S(2)}) collective-permute-start(bf16[4,6144]{1,0:T(4,128)(2,1)S(1)} %collective-permute-done.2.refs_6_), channel_id=1, source_target_pairs={{0,2},{1,3},{2,0},{3,1},{4,6},{5,7},{6,4},{7,5},{8,10},{9,11},{10,... | collective-permute-start | bytes 147464 | tf_op jit(solution)/shard_map/ppermute | solution.py:31
  15.3 1.2 %collective-permute-done.5.refs_9_ = bf16[4,6144]{1,0:T(4,128)(2,1)S(1)} collective-permute-done((bf16[4,6144]{1,0:T(4,128)(2,1)S(1)}, bf16[4,6144]{1,0:T(4,128)(2,1)S(1)}, u32[]{:S(2)}, u32[]{:S(2)}) %collective-permute-start.5) | collective-permute-done | bytes 49184 | tf_op jit(solution)/shard_map/ppermute | solution.py:31
  16.5 1.0 %collective-permute-done.4.refs_8_ = bf16[4,6144]{1,0:T(4,128)(2,1)S(1)} collective-permute-done((bf16[4,6144]{1,0:T(4,128)(2,1)S(1)}, bf16[4,6144]{1,0:T(4,128)(2,1)S(1)}, u32[]{:S(2)}, u32[]{:S(2)}) %collective-permute-start.4) | collective-permute-done | bytes 49184 | tf_op jit(solution)/shard_map/ppermute | solution.py:31
  18.2 1.4 %copy.12 = s32[1,16,12]{2,1,0:T(8,128)} copy(s32[1,16,12]{1,0,2:T(1,128)} %param.19) | data formatting | bytes 1536 | tf_op args[9]
  20.3 7.3 %project.1 = (bf16[48,1024]{1,0:T(8,128)(2,1)}, s32[32,48]{1,0:T(8,128)}, s32[8,256]{1,0:T(8,128)}) custom-call(s32[1]{0:T(128)} %bitcast.refs_0_, s32[16,12]{1,0:T(8,128)} %bitcast.3, bf16[6144,1024]{1,0:T(8,128)(2,1)} %refs_2_.2, bf16[4,6144]{1,0:T(4,128)(2,1)} %pack.1.refs_3_, bf16[4,6144]{1,0:T(4,128)(2,1)} %copy-done.15, bf16[4,6144]{1,0:T(4,128)(2,1)} %copy-done.17, ...), custom_call_target="tpu_custom_call" | custom-call | flops 603979776 | bytes 12582912 | tf_op jit(solution)/shard_map/project/pallas_call | solution.py:150
  27.6 1.9 %collective-permute-start.15 = (bf16[48,1024]{1,0:T(8,128)(2,1)}, bf16[48,1024]{1,0:T(8,128)(2,1)S(1)}, u32[]{:S(2)}, u32[]{:S(2)}) collective-permute-start(bf16[48,1024]{1,0:T(8,128)(2,1)} %get-tuple-element.10.refs_5_), channel_id=1, source_target_pairs={{0,8},{1,9},{2,10},{3,11},{4,12},{5,13},{6,14},{7,15},{8,0},{9,1},... | collective-permute-start | bytes 294920 | tf_op jit(solution)/shard_map/ppermute | solution.py:31
  29.6 1.5 %collective-permute-start.18 = (bf16[48,1024]{1,0:T(8,128)(2,1)}, bf16[48,1024]{1,0:T(8,128)(2,1)S(1)}, u32[]{:S(2)}, u32[]{:S(2)}) collective-permute-start(bf16[48,1024]{1,0:T(8,128)(2,1)} %get-tuple-element.10.refs_5_), channel_id=1, source_target_pairs={{0,2},{1,3},{2,0},{3,1},{4,6},{5,7},{6,4},{7,5},{8,10},{9,11},{10,... | collective-permute-start | bytes 294920 | tf_op jit(solution)/shard_map/ppermute | solution.py:31
  31.0 1.5 %collective-permute-start.16 = (bf16[48,1024]{1,0:T(8,128)(2,1)}, bf16[48,1024]{1,0:T(8,128)(2,1)S(1)}, u32[]{:S(2)}, u32[]{:S(2)}) collective-permute-start(bf16[48,1024]{1,0:T(8,128)(2,1)} %get-tuple-element.10.refs_5_), channel_id=1, source_target_pairs={{0,4},{1,5},{2,6},{3,7},{4,0},{5,1},{6,2},{7,3},{8,12},{9,13},{10,... | collective-permute-start | bytes 294920 | tf_op jit(solution)/shard_map/ppermute | solution.py:31
  32.5 3.7 %collective-permute-done.15.refs_6_ = bf16[48,1024]{1,0:T(8,128)(2,1)S(1)} collective-permute-done((bf16[48,1024]{1,0:T(8,128)(2,1)}, bf16[48,1024]{1,0:T(8,128)(2,1)S(1)}, u32[]{:S(2)}, u32[]{:S(2)}) %collective-permute-start.15) | collective-permute-done | bytes 98336 | tf_op jit(solution)/shard_map/ppermute | solution.py:31
  36.9 1.3 %collective-permute-start.20 = (bf16[48,1024]{1,0:T(8,128)(2,1)S(1)}, bf16[48,1024]{1,0:T(8,128)(2,1)S(1)}, u32[]{:S(2)}, u32[]{:S(2)}) collective-permute-start(bf16[48,1024]{1,0:T(8,128)(2,1)S(1)} %collective-permute-done.16.refs_7_), channel_id=1, source_target_pairs={{0,2},{1,3},{2,0},{3,1},{4,6},{5,7},{6,4},{7,5},{8,10},{9,11},{10,... | collective-permute-start | bytes 294920 | tf_op jit(solution)/shard_map/ppermute | solution.py:31
  38.9 1.9 %collective-permute-done.17.refs_8_ = bf16[48,1024]{1,0:T(8,128)(2,1)S(1)} collective-permute-done((bf16[48,1024]{1,0:T(8,128)(2,1)S(1)}, bf16[48,1024]{1,0:T(8,128)(2,1)S(1)}, u32[]{:S(2)}, u32[]{:S(2)}) %collective-permute-start.17) | collective-permute-done | bytes 98336 | tf_op jit(solution)/shard_map/ppermute | solution.py:31
  42.5 2.1 %collective-permute-done.19.refs_10_ = bf16[48,1024]{1,0:T(8,128)(2,1)S(1)} collective-permute-done((bf16[48,1024]{1,0:T(8,128)(2,1)S(1)}, bf16[48,1024]{1,0:T(8,128)(2,1)S(1)}, u32[]{:S(2)}, u32[]{:S(2)}) %collective-permute-start.19) | collective-permute-done | bytes 98336 | tf_op jit(solution)/shard_map/ppermute | solution.py:31
  44.6 1.4 %collective-permute-done.21.refs_12_ = bf16[48,1024]{1,0:T(8,128)(2,1)S(1)} collective-permute-done((bf16[48,1024]{1,0:T(8,128)(2,1)S(1)}, bf16[48,1024]{1,0:T(8,128)(2,1)S(1)}, u32[]{:S(2)}, u32[]{:S(2)}) %collective-permute-start.21) | collective-permute-done | bytes 98336 | tf_op jit(solution)/shard_map/ppermute | solution.py:31
  46.0 1.2 %collective-permute-done.29.refs_20_ = bf16[48,1024]{1,0:T(8,128)(2,1)S(1)} collective-permute-done((bf16[48,1024]{1,0:T(8,128)(2,1)S(1)}, bf16[48,1024]{1,0:T(8,128)(2,1)S(1)}, u32[]{:S(2)}, u32[]{:S(2)}) %collective-permute-start.29) | collective-permute-done | bytes 98336 | tf_op jit(solution)/shard_map/ppermute | solution.py:31
  47.9 10.6 %advance.1 = (bf16[192,128]{1,0:T(8,128)(2,1)}, bf16[4,48,1024]{2,1,0:T(8,128)(2,1)}, bf16[168,128,128]{2,1,0:T(8,128)(2,1)}) custom-call(s32[1]{0:T(128)} %bitcast.refs_0_, s32[8,256]{1,0:T(8,128)} %get-tuple-element.9.refs_1_, f32[32]{0:T(128)} %refs_2_.3, f32[168]{0:T(256)} %refs_3_.1, bf16[168,128,128]{2,1,0:T(8,128)(2,1)} %refs_4_.2, ...), custom_call_target="tpu_custom_call" | custom-call | flops 11010048 | bytes 11010048 | tf_op jit(solution)/shard_map/advance/pallas_call | solution.py:277
  58.5 3.1 %collective-permute-start.30 = (bf16[192,128]{1,0:T(8,128)(2,1)}, bf16[192,128]{1,0:T(8,128)(2,1)S(1)}, u32[]{:S(2)}, u32[]{:S(2)}) collective-permute-start(bf16[192,128]{1,0:T(8,128)(2,1)} %get-tuple-element.12.refs_5_), channel_id=1, source_target_pairs={{0,8},{1,9},{2,10},{3,11},{4,12},{5,13},{6,14},{7,15},{8,0},{9,1},... | collective-permute-start | bytes 147464 | tf_op jit(solution)/shard_map/ppermute | solution.py:31
  61.7 1.5 %collective-permute-start.33 = (bf16[192,128]{1,0:T(8,128)(2,1)}, bf16[192,128]{1,0:T(8,128)(2,1)S(1)}, u32[]{:S(2)}, u32[]{:S(2)}) collective-permute-start(bf16[192,128]{1,0:T(8,128)(2,1)} %get-tuple-element.12.refs_5_), channel_id=1, source_target_pairs={{0,2},{1,3},{2,0},{3,1},{4,6},{5,7},{6,4},{7,5},{8,10},{9,11},{10,... | collective-permute-start | bytes 147464 | tf_op jit(solution)/shard_map/ppermute | solution.py:31
  63.5 1.0 %collective-permute-done.30.refs_6_ = bf16[192,128]{1,0:T(8,128)(2,1)S(1)} collective-permute-done((bf16[192,128]{1,0:T(8,128)(2,1)}, bf16[192,128]{1,0:T(8,128)(2,1)S(1)}, u32[]{:S(2)}, u32[]{:S(2)}) %collective-permute-start.30) | collective-permute-done | bytes 49184 | tf_op jit(solution)/shard_map/ppermute | solution.py:31
  64.5 1.1 %collective-permute-start.32 = (bf16[192,128]{1,0:T(8,128)(2,1)S(1)}, bf16[192,128]{1,0:T(8,128)(2,1)S(1)}, u32[]{:S(2)}, u32[]{:S(2)}) collective-permute-start(bf16[192,128]{1,0:T(8,128)(2,1)S(1)} %collective-permute-done.30.refs_6_), channel_id=1, source_target_pairs={{0,4},{1,5},{2,6},{3,7},{4,0},{5,1},{6,2},{7,3},{8,12},{9,13},{10,... | collective-permute-start | bytes 147464 | tf_op jit(solution)/shard_map/ppermute | solution.py:31
  66.0 1.7 %collective-permute-done.31.refs_7_ = bf16[192,128]{1,0:T(8,128)(2,1)S(1)} collective-permute-done((bf16[192,128]{1,0:T(8,128)(2,1)}, bf16[192,128]{1,0:T(8,128)(2,1)S(1)}, u32[]{:S(2)}, u32[]{:S(2)}) %collective-permute-start.31) | collective-permute-done | bytes 49184 | tf_op jit(solution)/shard_map/ppermute | solution.py:31
  68.0 1.7 %collective-permute-start.34 = (bf16[192,128]{1,0:T(8,128)(2,1)S(1)}, bf16[192,128]{1,0:T(8,128)(2,1)S(1)}, u32[]{:S(2)}, u32[]{:S(2)}) collective-permute-start(bf16[192,128]{1,0:T(8,128)(2,1)S(1)} %collective-permute-done.30.refs_6_), channel_id=1, source_target_pairs={{0,2},{1,3},{2,0},{3,1},{4,6},{5,7},{6,4},{7,5},{8,10},{9,11},{10,... | collective-permute-start | bytes 147464 | tf_op jit(solution)/shard_map/ppermute | solution.py:31
  69.7 0.9 %collective-permute-start.36 = (bf16[192,128]{1,0:T(8,128)(2,1)S(1)}, bf16[192,128]{1,0:T(8,128)(2,1)S(1)}, u32[]{:S(2)}, u32[]{:S(2)}) collective-permute-start(bf16[192,128]{1,0:T(8,128)(2,1)S(1)} %collective-permute-done.32.refs_8_), channel_id=1, source_target_pairs={{0,2},{1,3},{2,0},{3,1},{4,6},{5,7},{6,4},{7,5},{8,10},{9,11},{10,... | collective-permute-start | bytes 147464 | tf_op jit(solution)/shard_map/ppermute | solution.py:31
  71.1 1.1 %collective-permute-done.35.refs_11_ = bf16[192,128]{1,0:T(8,128)(2,1)S(1)} collective-permute-done((bf16[192,128]{1,0:T(8,128)(2,1)S(1)}, bf16[192,128]{1,0:T(8,128)(2,1)S(1)}, u32[]{:S(2)}, u32[]{:S(2)}) %collective-permute-start.35) | collective-permute-done | bytes 49184 | tf_op jit(solution)/shard_map/ppermute | solution.py:31
  72.2 1.0 %collective-permute-done.34.refs_10_ = bf16[192,128]{1,0:T(8,128)(2,1)S(1)} collective-permute-done((bf16[192,128]{1,0:T(8,128)(2,1)S(1)}, bf16[192,128]{1,0:T(8,128)(2,1)S(1)}, u32[]{:S(2)}, u32[]{:S(2)}) %collective-permute-start.34) | collective-permute-done | bytes 49184 | tf_op jit(solution)/shard_map/ppermute | solution.py:31
  75.8 4.4 %finish.1 = bf16[48,384]{1,0:T(8,128)(2,1)} custom-call(s32[1]{0:T(128)} %bitcast.refs_0_, s32[32,48]{1,0:T(8,128)} %get-tuple-element.8.refs_1_, bf16[4,48,1024]{2,1,0:T(8,128)(2,1)} %get-tuple-element.11.refs_2_, f32[32,128]{1,0:T(8,128)} %bitcast.4, bf16[4096,384]{1,0:T(8,128)(2,1)} %refs_4_.3, bf16[192,128]{1,0:T(8,128)(2,1)} %get-tuple-element.12.refs_5_, ...), custom_call_target="tpu_custom_call" | custom-call | flops 150994944 | bytes 3145728 | tf_op jit(solution)/shard_map/finish/pallas_call | solution.py:347
  (153 shorter events, 9.9 us)
Async XLA Ops:
  2.1 7.1 %collective-permute-start = (bf16[4,6144]{1,0:T(4,128)(2,1)}, bf16[4,6144]{1,0:T(4,128)(2,1)S(1)}, u32[]{:S(2)}, u32[]{:S(2)}) collective-permute-start(bf16[4,6144]{1,0:T(4,128)(2,1)} %pack.1.refs_3_), channel_id=1, source_target_pairs={{0,8},{1,9},{2,10},{3,11},{4,12},{5,13},{6,14},{7,15},{8,0},{9,1},... | collective-permute-start | bytes 147464 | tf_op jit(solution)/shard_map/ppermute | solution.py:31
  6.2 4.5 %collective-permute-start.3 = (bf16[4,6144]{1,0:T(4,128)(2,1)}, bf16[4,6144]{1,0:T(4,128)(2,1)S(1)}, u32[]{:S(2)}, u32[]{:S(2)}) collective-permute-start(bf16[4,6144]{1,0:T(4,128)(2,1)} %pack.1.refs_3_), channel_id=1, source_target_pairs={{0,2},{1,3},{2,0},{3,1},{4,6},{5,7},{6,4},{7,5},{8,10},{9,11},{10,... | collective-permute-start | bytes 147464 | tf_op jit(solution)/shard_map/ppermute | solution.py:31
  7.7 4.3 %collective-permute-start.1 = (bf16[4,6144]{1,0:T(4,128)(2,1)}, bf16[4,6144]{1,0:T(4,128)(2,1)S(1)}, u32[]{:S(2)}, u32[]{:S(2)}) collective-permute-start(bf16[4,6144]{1,0:T(4,128)(2,1)} %pack.1.refs_3_), channel_id=1, source_target_pairs={{0,4},{1,5},{2,6},{3,7},{4,0},{5,1},{6,2},{7,3},{8,12},{9,13},{10,... | collective-permute-start | bytes 147464 | tf_op jit(solution)/shard_map/ppermute | solution.py:31
  9.3 4.8 %collective-permute-start.2 = (bf16[4,6144]{1,0:T(4,128)(2,1)S(1)}, bf16[4,6144]{1,0:T(4,128)(2,1)S(1)}, u32[]{:S(2)}, u32[]{:S(2)}) collective-permute-start(bf16[4,6144]{1,0:T(4,128)(2,1)S(1)} %collective-permute-done.refs_4_), channel_id=1, source_target_pairs={{0,4},{1,5},{2,6},{3,7},{4,0},{5,1},{6,2},{7,3},{8,12},{9,13},{10,... | collective-permute-start | bytes 147464 | tf_op jit(solution)/shard_map/ppermute | solution.py:31
  10.7 4.2 %collective-permute-start.11 = (bf16[4,6144]{1,0:T(4,128)(2,1)S(1)}, bf16[4,6144]{1,0:T(4,128)(2,1)S(1)}, u32[]{:S(2)}, u32[]{:S(2)}) collective-permute-start(bf16[4,6144]{1,0:T(4,128)(2,1)S(1)} %collective-permute-done.3.refs_7_), channel_id=1, source_target_pairs={{0,1},{1,0},{2,3},{3,2},{4,5},{5,4},{6,7},{7,6},{8,9},{9,8},{10,11... | collective-permute-start | bytes 147464 | tf_op jit(solution)/shard_map/ppermute | solution.py:31
  12.0 4.5 %collective-permute-start.5 = (bf16[4,6144]{1,0:T(4,128)(2,1)S(1)}, bf16[4,6144]{1,0:T(4,128)(2,1)S(1)}, u32[]{:S(2)}, u32[]{:S(2)}) collective-permute-start(bf16[4,6144]{1,0:T(4,128)(2,1)S(1)} %collective-permute-done.1.refs_5_), channel_id=1, source_target_pairs={{0,2},{1,3},{2,0},{3,1},{4,6},{5,7},{6,4},{7,5},{8,10},{9,11},{10,... | collective-permute-start | bytes 147464 | tf_op jit(solution)/shard_map/ppermute | solution.py:31
  12.5 5.1 %collective-permute-start.4 = (bf16[4,6144]{1,0:T(4,128)(2,1)S(1)}, bf16[4,6144]{1,0:T(4,128)(2,1)S(1)}, u32[]{:S(2)}, u32[]{:S(2)}) collective-permute-start(bf16[4,6144]{1,0:T(4,128)(2,1)S(1)} %collective-permute-done.refs_4_), channel_id=1, source_target_pairs={{0,2},{1,3},{2,0},{3,1},{4,6},{5,7},{6,4},{7,5},{8,10},{9,11},{10,... | collective-permute-start | bytes 147464 | tf_op jit(solution)/shard_map/ppermute | solution.py:31
  14.0 4.2 %collective-permute-start.6 = (bf16[4,6144]{1,0:T(4,128)(2,1)S(1)}, bf16[4,6144]{1,0:T(4,128)(2,1)S(1)}, u32[]{:S(2)}, u32[]{:S(2)}) collective-permute-start(bf16[4,6144]{1,0:T(4,128)(2,1)S(1)} %collective-permute-done.2.refs_6_), channel_id=1, source_target_pairs={{0,2},{1,3},{2,0},{3,1},{4,6},{5,7},{6,4},{7,5},{8,10},{9,11},{10,... | collective-permute-start | bytes 147464 | tf_op jit(solution)/shard_map/ppermute | solution.py:31
  14.8 4.8 %collective-permute-start.8 = (bf16[4,6144]{1,0:T(4,128)(2,1)S(1)}, bf16[4,6144]{1,0:T(4,128)(2,1)S(1)}, u32[]{:S(2)}, u32[]{:S(2)}) collective-permute-start(bf16[4,6144]{1,0:T(4,128)(2,1)S(1)} %collective-permute-done.refs_4_), channel_id=1, source_target_pairs={{0,1},{1,0},{2,3},{3,2},{4,5},{5,4},{6,7},{7,6},{8,9},{9,8},{10,11... | collective-permute-start | bytes 147464 | tf_op jit(solution)/shard_map/ppermute | solution.py:31
  14.9 4.8 %collective-permute-start.10 = (bf16[4,6144]{1,0:T(4,128)(2,1)S(1)}, bf16[4,6144]{1,0:T(4,128)(2,1)S(1)}, u32[]{:S(2)}, u32[]{:S(2)}) collective-permute-start(bf16[4,6144]{1,0:T(4,128)(2,1)S(1)} %collective-permute-done.2.refs_6_), channel_id=1, source_target_pairs={{0,1},{1,0},{2,3},{3,2},{4,5},{5,4},{6,7},{7,6},{8,9},{9,8},{10,11... | collective-permute-start | bytes 147464 | tf_op jit(solution)/shard_map/ppermute | solution.py:31
  27.6 8.6 %collective-permute-start.15 = (bf16[48,1024]{1,0:T(8,128)(2,1)}, bf16[48,1024]{1,0:T(8,128)(2,1)S(1)}, u32[]{:S(2)}, u32[]{:S(2)}) collective-permute-start(bf16[48,1024]{1,0:T(8,128)(2,1)} %get-tuple-element.10.refs_5_), channel_id=1, source_target_pairs={{0,8},{1,9},{2,10},{3,11},{4,12},{5,13},{6,14},{7,15},{8,0},{9,1},... | collective-permute-start | bytes 294920 | tf_op jit(solution)/shard_map/ppermute | solution.py:31
  29.6 6.8 %collective-permute-start.18 = (bf16[48,1024]{1,0:T(8,128)(2,1)}, bf16[48,1024]{1,0:T(8,128)(2,1)S(1)}, u32[]{:S(2)}, u32[]{:S(2)}) collective-permute-start(bf16[48,1024]{1,0:T(8,128)(2,1)} %get-tuple-element.10.refs_5_), channel_id=1, source_target_pairs={{0,2},{1,3},{2,0},{3,1},{4,6},{5,7},{6,4},{7,5},{8,10},{9,11},{10,... | collective-permute-start | bytes 294920 | tf_op jit(solution)/shard_map/ppermute | solution.py:31
  31.0 5.5 %collective-permute-start.16 = (bf16[48,1024]{1,0:T(8,128)(2,1)}, bf16[48,1024]{1,0:T(8,128)(2,1)S(1)}, u32[]{:S(2)}, u32[]{:S(2)}) collective-permute-start(bf16[48,1024]{1,0:T(8,128)(2,1)} %get-tuple-element.10.refs_5_), channel_id=1, source_target_pairs={{0,4},{1,5},{2,6},{3,7},{4,0},{5,1},{6,2},{7,3},{8,12},{9,13},{10,... | collective-permute-start | bytes 294920 | tf_op jit(solution)/shard_map/ppermute | solution.py:31
  32.5 5.6 %collective-permute-start.22 = (bf16[48,1024]{1,0:T(8,128)(2,1)}, bf16[48,1024]{1,0:T(8,128)(2,1)S(1)}, u32[]{:S(2)}, u32[]{:S(2)}) collective-permute-start(bf16[48,1024]{1,0:T(8,128)(2,1)} %get-tuple-element.10.refs_5_), channel_id=1, source_target_pairs={{0,1},{1,0},{2,3},{3,2},{4,5},{5,4},{6,7},{7,6},{8,9},{9,8},{10,11... | collective-permute-start | bytes 294920 | tf_op jit(solution)/shard_map/ppermute | solution.py:31
  36.2 4.6 %collective-permute-start.17 = (bf16[48,1024]{1,0:T(8,128)(2,1)S(1)}, bf16[48,1024]{1,0:T(8,128)(2,1)S(1)}, u32[]{:S(2)}, u32[]{:S(2)}) collective-permute-start(bf16[48,1024]{1,0:T(8,128)(2,1)S(1)} %collective-permute-done.15.refs_6_), channel_id=1, source_target_pairs={{0,4},{1,5},{2,6},{3,7},{4,0},{5,1},{6,2},{7,3},{8,12},{9,13},{10,... | collective-permute-start | bytes 294920 | tf_op jit(solution)/shard_map/ppermute | solution.py:31
  36.3 5.2 %collective-permute-start.26 = (bf16[48,1024]{1,0:T(8,128)(2,1)S(1)}, bf16[48,1024]{1,0:T(8,128)(2,1)S(1)}, u32[]{:S(2)}, u32[]{:S(2)}) collective-permute-start(bf16[48,1024]{1,0:T(8,128)(2,1)S(1)} %collective-permute-done.18.refs_9_), channel_id=1, source_target_pairs={{0,1},{1,0},{2,3},{3,2},{4,5},{5,4},{6,7},{7,6},{8,9},{9,8},{10,11... | collective-permute-start | bytes 294920 | tf_op jit(solution)/shard_map/ppermute | solution.py:31
  36.5 5.0 %collective-permute-start.24 = (bf16[48,1024]{1,0:T(8,128)(2,1)S(1)}, bf16[48,1024]{1,0:T(8,128)(2,1)S(1)}, u32[]{:S(2)}, u32[]{:S(2)}) collective-permute-start(bf16[48,1024]{1,0:T(8,128)(2,1)S(1)} %collective-permute-done.16.refs_7_), channel_id=1, source_target_pairs={{0,1},{1,0},{2,3},{3,2},{4,5},{5,4},{6,7},{7,6},{8,9},{9,8},{10,11... | collective-permute-start | bytes 294920 | tf_op jit(solution)/shard_map/ppermute | solution.py:31
  36.9 5.6 %collective-permute-start.20 = (bf16[48,1024]{1,0:T(8,128)(2,1)S(1)}, bf16[48,1024]{1,0:T(8,128)(2,1)S(1)}, u32[]{:S(2)}, u32[]{:S(2)}) collective-permute-start(bf16[48,1024]{1,0:T(8,128)(2,1)S(1)} %collective-permute-done.16.refs_7_), channel_id=1, source_target_pairs={{0,2},{1,3},{2,0},{3,1},{4,6},{5,7},{6,4},{7,5},{8,10},{9,11},{10,... | collective-permute-start | bytes 294920 | tf_op jit(solution)/shard_map/ppermute | solution.py:31
  38.2 6.4 %collective-permute-start.19 = (bf16[48,1024]{1,0:T(8,128)(2,1)S(1)}, bf16[48,1024]{1,0:T(8,128)(2,1)S(1)}, u32[]{:S(2)}, u32[]{:S(2)}) collective-permute-start(bf16[48,1024]{1,0:T(8,128)(2,1)S(1)} %collective-permute-done.15.refs_6_), channel_id=1, source_target_pairs={{0,2},{1,3},{2,0},{3,1},{4,6},{5,7},{6,4},{7,5},{8,10},{9,11},{10,... | collective-permute-start | bytes 294920 | tf_op jit(solution)/shard_map/ppermute | solution.py:31
  40.8 5.1 %collective-permute-start.21 = (bf16[48,1024]{1,0:T(8,128)(2,1)S(1)}, bf16[48,1024]{1,0:T(8,128)(2,1)S(1)}, u32[]{:S(2)}, u32[]{:S(2)}) collective-permute-start(bf16[48,1024]{1,0:T(8,128)(2,1)S(1)} %collective-permute-done.17.refs_8_), channel_id=1, source_target_pairs={{0,2},{1,3},{2,0},{3,1},{4,6},{5,7},{6,4},{7,5},{8,10},{9,11},{10,... | collective-permute-start | bytes 294920 | tf_op jit(solution)/shard_map/ppermute | solution.py:31
  41.5 4.4 %collective-permute-start.23 = (bf16[48,1024]{1,0:T(8,128)(2,1)S(1)}, bf16[48,1024]{1,0:T(8,128)(2,1)S(1)}, u32[]{:S(2)}, u32[]{:S(2)}) collective-permute-start(bf16[48,1024]{1,0:T(8,128)(2,1)S(1)} %collective-permute-done.15.refs_6_), channel_id=1, source_target_pairs={{0,1},{1,0},{2,3},{3,2},{4,5},{5,4},{6,7},{7,6},{8,9},{9,8},{10,11... | collective-permute-start | bytes 294920 | tf_op jit(solution)/shard_map/ppermute | solution.py:31
  41.6 4.5 %collective-permute-start.25 = (bf16[48,1024]{1,0:T(8,128)(2,1)S(1)}, bf16[48,1024]{1,0:T(8,128)(2,1)S(1)}, u32[]{:S(2)}, u32[]{:S(2)}) collective-permute-start(bf16[48,1024]{1,0:T(8,128)(2,1)S(1)} %collective-permute-done.17.refs_8_), channel_id=1, source_target_pairs={{0,1},{1,0},{2,3},{3,2},{4,5},{5,4},{6,7},{7,6},{8,9},{9,8},{10,11... | collective-permute-start | bytes 294920 | tf_op jit(solution)/shard_map/ppermute | solution.py:31
  58.5 6.0 %collective-permute-start.30 = (bf16[192,128]{1,0:T(8,128)(2,1)}, bf16[192,128]{1,0:T(8,128)(2,1)S(1)}, u32[]{:S(2)}, u32[]{:S(2)}) collective-permute-start(bf16[192,128]{1,0:T(8,128)(2,1)} %get-tuple-element.12.refs_5_), channel_id=1, source_target_pairs={{0,8},{1,9},{2,10},{3,11},{4,12},{5,13},{6,14},{7,15},{8,0},{9,1},... | collective-permute-start | bytes 147464 | tf_op jit(solution)/shard_map/ppermute | solution.py:31
  61.7 4.3 %collective-permute-start.33 = (bf16[192,128]{1,0:T(8,128)(2,1)}, bf16[192,128]{1,0:T(8,128)(2,1)S(1)}, u32[]{:S(2)}, u32[]{:S(2)}) collective-permute-start(bf16[192,128]{1,0:T(8,128)(2,1)} %get-tuple-element.12.refs_5_), channel_id=1, source_target_pairs={{0,2},{1,3},{2,0},{3,1},{4,6},{5,7},{6,4},{7,5},{8,10},{9,11},{10,... | collective-permute-start | bytes 147464 | tf_op jit(solution)/shard_map/ppermute | solution.py:31
  63.1 4.5 %collective-permute-start.31 = (bf16[192,128]{1,0:T(8,128)(2,1)}, bf16[192,128]{1,0:T(8,128)(2,1)S(1)}, u32[]{:S(2)}, u32[]{:S(2)}) collective-permute-start(bf16[192,128]{1,0:T(8,128)(2,1)} %get-tuple-element.12.refs_5_), channel_id=1, source_target_pairs={{0,4},{1,5},{2,6},{3,7},{4,0},{5,1},{6,2},{7,3},{8,12},{9,13},{10,... | collective-permute-start | bytes 147464 | tf_op jit(solution)/shard_map/ppermute | solution.py:31
  63.5 4.5 %collective-permute-start.37 = (bf16[192,128]{1,0:T(8,128)(2,1)}, bf16[192,128]{1,0:T(8,128)(2,1)S(1)}, u32[]{:S(2)}, u32[]{:S(2)}) collective-permute-start(bf16[192,128]{1,0:T(8,128)(2,1)} %get-tuple-element.12.refs_5_), channel_id=1, source_target_pairs={{0,1},{1,0},{2,3},{3,2},{4,5},{5,4},{6,7},{7,6},{8,9},{9,8},{10,11... | collective-permute-start | bytes 147464 | tf_op jit(solution)/shard_map/ppermute | solution.py:31
  64.5 5.2 %collective-permute-start.32 = (bf16[192,128]{1,0:T(8,128)(2,1)S(1)}, bf16[192,128]{1,0:T(8,128)(2,1)S(1)}, u32[]{:S(2)}, u32[]{:S(2)}) collective-permute-start(bf16[192,128]{1,0:T(8,128)(2,1)S(1)} %collective-permute-done.30.refs_6_), channel_id=1, source_target_pairs={{0,4},{1,5},{2,6},{3,7},{4,0},{5,1},{6,2},{7,3},{8,12},{9,13},{10,... | collective-permute-start | bytes 147464 | tf_op jit(solution)/shard_map/ppermute | solution.py:31
  66.0 4.6 %collective-permute-start.41 = (bf16[192,128]{1,0:T(8,128)(2,1)S(1)}, bf16[192,128]{1,0:T(8,128)(2,1)S(1)}, u32[]{:S(2)}, u32[]{:S(2)}) collective-permute-start(bf16[192,128]{1,0:T(8,128)(2,1)S(1)} %collective-permute-done.33.refs_9_), channel_id=1, source_target_pairs={{0,1},{1,0},{2,3},{3,2},{4,5},{5,4},{6,7},{7,6},{8,9},{9,8},{10,11... | collective-permute-start | bytes 147464 | tf_op jit(solution)/shard_map/ppermute | solution.py:31
  67.7 4.5 %collective-permute-start.35 = (bf16[192,128]{1,0:T(8,128)(2,1)S(1)}, bf16[192,128]{1,0:T(8,128)(2,1)S(1)}, u32[]{:S(2)}, u32[]{:S(2)}) collective-permute-start(bf16[192,128]{1,0:T(8,128)(2,1)S(1)} %collective-permute-done.31.refs_7_), channel_id=1, source_target_pairs={{0,2},{1,3},{2,0},{3,1},{4,6},{5,7},{6,4},{7,5},{8,10},{9,11},{10,... | collective-permute-start | bytes 147464 | tf_op jit(solution)/shard_map/ppermute | solution.py:31
  68.0 5.2 %collective-permute-start.34 = (bf16[192,128]{1,0:T(8,128)(2,1)S(1)}, bf16[192,128]{1,0:T(8,128)(2,1)S(1)}, u32[]{:S(2)}, u32[]{:S(2)}) collective-permute-start(bf16[192,128]{1,0:T(8,128)(2,1)S(1)} %collective-permute-done.30.refs_6_), channel_id=1, source_target_pairs={{0,2},{1,3},{2,0},{3,1},{4,6},{5,7},{6,4},{7,5},{8,10},{9,11},{10,... | collective-permute-start | bytes 147464 | tf_op jit(solution)/shard_map/ppermute | solution.py:31
  69.7 4.2 %collective-permute-start.36 = (bf16[192,128]{1,0:T(8,128)(2,1)S(1)}, bf16[192,128]{1,0:T(8,128)(2,1)S(1)}, u32[]{:S(2)}, u32[]{:S(2)}) collective-permute-start(bf16[192,128]{1,0:T(8,128)(2,1)S(1)} %collective-permute-done.32.refs_8_), channel_id=1, source_target_pairs={{0,2},{1,3},{2,0},{3,1},{4,6},{5,7},{6,4},{7,5},{8,10},{9,11},{10,... | collective-permute-start | bytes 147464 | tf_op jit(solution)/shard_map/ppermute | solution.py:31
  70.6 3.9 %collective-permute-start.40 = (bf16[192,128]{1,0:T(8,128)(2,1)S(1)}, bf16[192,128]{1,0:T(8,128)(2,1)S(1)}, u32[]{:S(2)}, u32[]{:S(2)}) collective-permute-start(bf16[192,128]{1,0:T(8,128)(2,1)S(1)} %collective-permute-done.32.refs_8_), channel_id=1, source_target_pairs={{0,1},{1,0},{2,3},{3,2},{4,5},{5,4},{6,7},{7,6},{8,9},{9,8},{10,11... | collective-permute-start | bytes 147464 | tf_op jit(solution)/shard_map/ppermute | solution.py:31
  (58 other events, 224.8 us)

commit v3 on v2

v3 whole, which is shorter than its diff:
```python
import functools
import math

import jax
import jax.numpy as jnp
from jax import lax
from jax.experimental import pallas as pl
from jax.experimental.pallas import tpu as pltpu
from jax.sharding import PartitionSpec as P

BF16 = jnp.bfloat16
F32 = jnp.float32
I32 = jnp.int32
SMEM = pl.BlockSpec(memory_space=pltpu.SMEM)
VMEM = pl.BlockSpec(memory_space=pltpu.VMEM)
ANY = pl.BlockSpec(memory_space=pl.ANY)


def grant(*arrays):
    held = sum(math.prod(a.shape) * jnp.dtype(a.dtype).itemsize for a in arrays)
    most = 60 * 1024 * 1024
    return held + 6 * 1024 * 1024 if held < most // 2 else most


def block_order(devices):
    order, bit = [0], devices // 2
    while bit >= 1:
        order = order + [o ^ bit for o in order]
        bit //= 2
    return order


def place_of(crossed, devices):
    bits = devices.bit_length() - 1
    return sum(((crossed >> k) & 1) << (bits - 1 - k) for k in range(bits))


def gather_pieces(block, devices):
    held, bit = [block], devices // 2
    while bit >= 1:
        pairs = [(i, i ^ bit) for i in range(devices)]
        held = held + [lax.ppermute(piece, "batch", pairs) for piece in held]
        bit //= 2
    return held


def is_large(*arrays):
    return sum(math.prod(a.shape) * jnp.dtype(a.dtype).itemsize for a in arrays) > 6 * 1024 * 1024


def fetch(ref, stage):
    if not stage:
        return ref[...]
    copy = pltpu.make_async_copy(ref, *stage)
    copy.start()
    copy.wait()
    return stage[0][...]


def pack_kernel(heads, tokens_ref, holder_ref, rank_ref, out_ref):
    own, width = tokens_ref.shape
    parts = []
    for i in range(own):
        parts.append(holder_ref[i : i + 1, :].astype(F32))
        parts.append(rank_ref[i : i + 1, :].astype(F32))
        parts.append(jnp.zeros((1, 128 - 2 * heads), F32))
    parts.append(jnp.zeros((1, width - own * 128), F32))
    table = jnp.concatenate(parts, axis=1)
    block = jnp.concatenate([tokens_ref[...].astype(F32), table], axis=0)
    out_ref[...] = block.astype(BF16)


def pack(tokens, holder, rank):
    own, width = tokens.shape
    return pl.pallas_call(
        functools.partial(pack_kernel, holder.shape[1]),
        out_shape=jax.ShapeDtypeStruct((own + 1, width), BF16),
        in_specs=[VMEM] * 3,
        out_specs=VMEM,
        compiler_params=pltpu.CompilerParams(vmem_limit_bytes=grant(tokens)),
        cost_estimate=pl.CostEstimate(flops=20000000000, bytes_accessed=60000000, transcendentals=0),
        name="pack",
    )(tokens, holder, rank)


def project_kernel(devices, heads, slots, steps, *refs):
    send_ref, w_ref = refs[:2]
    pieces = refs[2 : 2 + devices]
    act_ref, pick_ref, slot_ref, rows = refs[2 + devices :]
    order = block_order(devices)
    sessions, cols = act_ref.shape
    per = cols // 128
    own = sessions // devices
    capacity = send_ref.shape[0]
    width = w_ref.shape[0]
    chunk = width // steps
    me = lax.axis_index("batch")
    lane = lax.broadcasted_iota(I32, (1, sessions), 1)
    target = jnp.zeros((1, sessions), I32)
    source = jnp.zeros((1, sessions), I32)
    indices = []
    for j in range(devices):
        block = pieces[j][...].astype(F32)
        rows[j * own : (j + 1) * own, :] = block[:own]
        for i in range(own):
            indices.append(block[own : own + 1, i * 128 : (i + 1) * 128])
        inside = (lane >= j * own) & (lane < (j + 1) * own)
        target = jnp.where(inside, lane + ((me ^ order[j]) - j) * own, target)
        source = jnp.where(inside, lane + (place_of(me ^ j, devices) - j) * own, source)
    grid_row = lax.broadcasted_iota(I32, (sessions, sessions), 0)
    place = (grid_row == target).astype(F32).astype(BF16)
    place_t = (grid_row == source).astype(F32).astype(BF16)

    table = jnp.concatenate(indices, axis=0)
    table = jnp.dot(table.T.astype(BF16), place_t, preferred_element_type=F32).astype(I32)
    holder = table[:heads]
    rank = table[heads : 2 * heads]
    owner = (lane * (65536 // own + 1)) >> 16
    pick_ref[...] = (place_of(holder ^ me, devices) * devices + owner) * capacity + rank

    owner_row = lax.broadcasted_iota(I32, (devices, sessions), 0)
    spread = (owner_row == owner).astype(F32).astype(BF16)
    sent = jnp.concatenate([send_ref[r].astype(F32) for r in range(capacity)], axis=0).astype(BF16)
    sent = jnp.dot(sent, spread, preferred_element_type=F32).astype(I32)
    slot = jnp.full((heads, sessions), -1, I32)
    for r in range(capacity):
        slot = jnp.where(rank == r, sent[r : r + 1, :], slot)
    slot = jnp.where(holder == me, slot, -1)
    entry = owner * capacity + rank
    padded = slot_ref.shape[1]
    slot_lane = lax.broadcasted_iota(I32, (heads, padded), 1)
    head_row = lax.broadcasted_iota(I32, (heads, padded), 0)
    piece = jnp.zeros((heads, padded), I32)
    for group in range(heads // per):
        inside = (head_row >= group * per) & (head_row < (group + 1) * per)
        piece = jnp.where(inside, place_of(me ^ group, devices), piece)
    found = jnp.zeros((heads, padded), I32)
    found_entry = jnp.zeros((heads, padded), I32)
    for s in range(sessions):
        same = slot[:, s : s + 1] == slot_lane
        found = jnp.where(same, s + 1, found)
        found_entry = jnp.where(same, entry[:, s : s + 1], found_entry)
    used = found > 0

    def only(x):
        return jnp.sum(jnp.where(used, x, 0).astype(F32), axis=0, keepdims=True).astype(I32)

    any_used = only(found) > 0
    head = only(head_row)
    piece = only(piece)
    inner = (head - only(head_row // per * per)) * sessions + only(found) - 1
    size = per * sessions
    unused = devices * size
    slot_ref[0:1, :] = jnp.where(any_used, piece * size + inner, unused)
    slot_ref[1:2, :] = jnp.where(any_used, (piece ^ 2) * size + inner, unused)
    slot_ref[2:3, :] = jnp.where(any_used, (piece ^ 1) * size + inner, unused)
    slot_ref[3:4, :] = jnp.where(any_used, head, -1)
    slot_ref[4:5, :] = jnp.where(any_used, only(found_entry), devices * capacity)
    slot_ref[5:8, :] = jnp.zeros((3, padded), I32)

    total = jnp.zeros(act_ref.shape, F32)
    for step in range(steps):
        part = slice(step * chunk, (step + 1) * chunk)
        total += jnp.dot(rows[:, part].astype(BF16), w_ref[part, :], preferred_element_type=F32)
    gate = jax.nn.sigmoid(total)
    is_gate = me * cols >= 3 * heads * 128
    active = jnp.where(is_gate, gate, total * gate).astype(BF16)
    act_ref[...] = jnp.dot(place, active, preferred_element_type=F32).astype(BF16)


def project(pieces, w, send, heads, slots):
    devices = len(pieces)
    own = pieces[0].shape[0] - 1
    sessions = own * devices
    width, cols = w.shape
    steps = 8
    padded = (slots + 127) // 128 * 128
    return pl.pallas_call(
        functools.partial(project_kernel, devices, heads, slots, steps),
        out_shape=(
            jax.ShapeDtypeStruct((sessions, cols), BF16),
            jax.ShapeDtypeStruct((heads, sessions), I32),
            jax.ShapeDtypeStruct((8, padded), I32),
        ),
        in_specs=[VMEM] * (2 + devices),
        out_specs=(VMEM, VMEM, VMEM),
        scratch_shapes=[
            pltpu.VMEM((sessions, width), F32),
        ],
        compiler_params=pltpu.CompilerParams(
            vmem_limit_bytes=grant(w, *pieces, jax.ShapeDtypeStruct((sessions, width), F32))
        ),
        cost_estimate=pl.CostEstimate(
            flops=2 * sessions * width * cols, bytes_accessed=2 * width * cols, transcendentals=0
        ),
        name="project",
    )(send, w, *pieces)


def advance_kernel(devices, chunks, *refs):
    slot_ref, rate_ref, scale_ref, cache_ref = refs[:4]
    pieces = refs[4 : 4 + devices]
    read_ref, flat_ref, out_ref, fresh, query, keys, values, reads, sems, *stage = refs[
        4 + devices :
    ]
    sessions, cols = pieces[0].shape
    per = cols // 128
    slots = cache_ref.shape[0]
    step = slots // chunks
    for j in range(devices):
        block = fetch(pieces[j], stage)
        for b in range(per):
            base = (j * per + b) * sessions
            flat_ref[base : base + sessions, :] = block[:, b * 128 : (b + 1) * 128].astype(F32)
    base = devices * per * sessions
    flat_ref[base : base + 8, :] = jnp.zeros((8, 128), F32)

    @pl.loop(0, slots // 8)
    def _(group):
        for u in range(8):
            e = group * 8 + u
            query[pl.ds(e, 1), :] = flat_ref[pl.ds(slot_ref[0, e], 1), :]
            keys[pl.ds(e, 1), :] = flat_ref[pl.ds(slot_ref[1, e], 1), :]
            values[pl.ds(e, 1), :] = flat_ref[pl.ds(slot_ref[2, e], 1), :]

    rows8 = lax.broadcasted_iota(I32, (8, 128), 0)

    def advance(base):
        q8 = query[base : base + 8, :]
        k8 = keys[base : base + 8, :]
        v8 = values[base : base + 8, :]
        rate = jnp.zeros((8, 128), F32)
        scale = jnp.ones((8, 128), F32)
        for u in range(8):
            head = slot_ref[3, base + u]
            one = jnp.where(head < 0, 0.0, rate_ref[jnp.maximum(head, 0)])
            rate = jnp.where(rows8 == u, one, rate)
            scale = jnp.where(rows8 == u, scale_ref[base + u], scale)
        decay = jnp.exp(-rate)
        scaled = v8 * (1.0 / scale)
        columns = k8.T
        wide = jnp.concatenate([cache_ref[base + u] for u in range(8)], axis=1)
        prod = jnp.dot(q8.astype(BF16), wide, preferred_element_type=F32)
        seen = jnp.zeros((8, 128), F32)
        for u in range(8):
            seen = jnp.where(rows8 == u, prod[:, u * 128 : (u + 1) * 128], seen)
            fresh[base + u] = (
                decay[u : u + 1, :] * cache_ref[base + u].astype(F32)
                + columns[:, u : u + 1] * scaled[u : u + 1, :]
            ).astype(BF16)
        near = jnp.sum(q8 * k8, axis=1, keepdims=True)
        result = seen * (decay * scale) + near * v8
        for u in range(8):
            reads[pl.ds(slot_ref[4, base + u], 1), :] = result[u : u + 1, :]

    backs = []
    for c in range(chunks):
        for base in range(c * step, (c + 1) * step, 8):
            advance(base)
        part = pl.ds(c * step, step)
        backs.append(pltpu.make_async_copy(fresh.at[part], out_ref.at[part], sems.at[c]))
        backs[-1].start()
    entries = read_ref.shape[0]
    read_ref[...] = reads[:entries, :].astype(BF16)
    for back in backs:
        back.wait()


def advance_tiles(pieces, cache, slot, rate, scale, capacity):
    devices = len(pieces)
    entries = devices * capacity
    sessions, cols = pieces[0].shape
    slots = cache.shape[0]
    chunks = 7 if slots % 56 == 0 else 1
    large = is_large(*pieces)
    flat = jax.ShapeDtypeStruct((devices * sessions * cols // 128 + 8, 128), F32)
    return pl.pallas_call(
        functools.partial(advance_kernel, devices, chunks),
        out_shape=(
            jax.ShapeDtypeStruct((entries, 128), BF16),
            flat,
            jax.ShapeDtypeStruct(cache.shape, BF16),
        ),
        in_specs=[SMEM] * 3 + [VMEM] + [ANY if large else VMEM] * devices,
        out_specs=(VMEM, VMEM, ANY),
        scratch_shapes=[
            pltpu.VMEM(cache.shape, BF16),
            pltpu.VMEM((slots, 128), F32),
            pltpu.VMEM((slots, 128), F32),
            pltpu.VMEM((slots, 128), F32),
            pltpu.VMEM((entries + 8, 128), F32),
            pltpu.SemaphoreType.DMA((chunks,)),
        ]
        + ([pltpu.VMEM((sessions, cols), BF16), pltpu.SemaphoreType.DMA] if large else []),
        compiler_params=pltpu.CompilerParams(
            vmem_limit_bytes=grant(cache, cache, flat, *([] if large else pieces))
        ),
        cost_estimate=pl.CostEstimate(
            flops=4 * cache.size, bytes_accessed=4 * cache.size, transcendentals=0
        ),
        name="advance",
    )(slot, rate, scale, cache, *pieces)


def finish_kernel(devices, per, *refs):
    pick_ref, act_ref, gain_ref, w_ref = refs[:4]
    pieces = refs[4 : 4 + devices]
    out_ref, flat, hidden, merged, *stages = refs[4 + devices :]
    entries = pieces[0].shape[0]
    sessions = merged.shape[0]
    heads = merged.shape[1] // 128
    me = lax.axis_index("batch")
    for j in range(devices):
        flat[j * entries : (j + 1) * entries, :] = fetch(pieces[j], stages[:2]).astype(F32)

    @pl.loop(0, heads)
    def _(h):
        base = pl.multiple_of(h * sessions, 8)
        for s in range(sessions):
            hidden[pl.ds(base + s, 1), :] = flat[pl.ds(pick_ref[h, s], 1), :]

    squares = jnp.zeros((sessions, 128), F32)
    for h in range(heads):
        block = hidden[h * sessions : (h + 1) * sessions, :]
        squares += block * block
    mean = jnp.sum(squares, axis=1, keepdims=True) * (1.0 / (heads * 128))
    norm = lax.rsqrt(mean + 1e-6)
    for h in range(heads):
        block = hidden[h * sessions : (h + 1) * sessions, :]
        piece = place_of(me ^ (3 * devices // 4 + h // per), devices)
        base = pl.multiple_of((piece * per + h % per) * sessions, 8)
        gate = fetch(act_ref.at[pl.ds(base, sessions)], stages[2:])
        block = block * norm * gain_ref[h : h + 1, :] * gate
        merged[:, h * 128 : (h + 1) * 128] = block.astype(BF16)
    out_ref[...] = jnp.dot(merged[...], w_ref[...], preferred_element_type=F32).astype(BF16)


def finish(pieces, gates, pick, gain, w_out):
    devices = len(pieces)
    entries = pieces[0].shape[0]
    heads, sessions = pick.shape
    per = gates.shape[0] // (devices * sessions)
    large = is_large(gates)
    width = w_out.shape[0]
    return pl.pallas_call(
        functools.partial(finish_kernel, devices, per),
        out_shape=jax.ShapeDtypeStruct((sessions, w_out.shape[1]), BF16),
        in_specs=[SMEM, ANY if large else VMEM, VMEM, VMEM] + [ANY if large else VMEM] * devices,
        out_specs=VMEM,
        scratch_shapes=[
            pltpu.VMEM((devices * entries, 128), F32),
            pltpu.VMEM((sessions * width // 128, 128), F32),
            pltpu.VMEM((sessions, width), BF16),
        ]
        + (
            [
                pltpu.VMEM((entries, 128), BF16),
                pltpu.SemaphoreType.DMA,
                pltpu.VMEM((sessions, 128), F32),
                pltpu.SemaphoreType.DMA,
            ]
            if large
            else []
        ),
        compiler_params=pltpu.CompilerParams(
            vmem_limit_bytes=grant(
                w_out,
                *([] if large else [gates, *pieces]),
                jax.ShapeDtypeStruct((devices * entries, 128), F32),
                jax.ShapeDtypeStruct((sessions * width // 128, 192), F32),
            )
        ),
        cost_estimate=pl.CostEstimate(
            flops=2 * sessions * w_out.size, bytes_accessed=2 * w_out.size, transcendentals=0
        ),
        name="finish",
    )(pick, gates, gain, w_out, *pieces)


def on_device(
    tokens,
    w_proj,
    w_out,
    decay_rate,
    norm_gain,
    cache_tiles,
    tile_scales,
    tile_holder,
    tile_rank,
    send_slot,
):
    devices = lax.axis_size("batch")
    heads = decay_rate.shape[0]
    capacity = send_slot.shape[-1]
    slots = cache_tiles.shape[0]

    tokens_all = gather_pieces(pack(tokens, tile_holder, tile_rank), devices)
    act, pick, slot = project(
        tokens_all, w_proj, jnp.transpose(send_slot, (2, 0, 1)), heads, slots
    )
    act_all = gather_pieces(act, devices)
    read, gates, new_cache = advance_tiles(
        act_all, cache_tiles, slot, decay_rate, tile_scales, capacity
    )
    read_all = gather_pieces(read, devices)
    mixed_out = finish(read_all, gates, pick, norm_gain.reshape(heads, 128), w_out)
    return (mixed_out, new_cache)


def solution(mesh):
    return jax.shard_map(
        on_device,
        mesh=mesh,
        in_specs=(
            P(("groups", "batch"), None),
            P(None, "batch"),
            P(None, "batch"),
            P(),
            P(),
            P(("groups", "batch"), None, None),
            P(("groups", "batch")),
            P(("groups", "batch"), None),
            P(("groups", "batch"), None),
            P(("groups", "batch"), None, None),
        ),
        out_specs=(P("groups", "batch"), P(("groups", "batch"), None, None)),
        check_vma=False,
    )
```

time: 80.6 us -> 69.8 us (0.87)
  Pallas kernels: 23.8 us -> 13.9 us
  waiting for transfers between devices: 22.2 us -> 23.1 us
  local copies, waits for them, and re-layouts: 3.07 us -> 2.19 us
    pallas_call x1, Pallas kernels: 7.29 us -> 2.5 us  [project(): pl.pallas_call(functools.partial(project_kernel, devices, heads, slots, s...]
    pallas_call x2, Pallas kernels: 15 us -> 11.3 us  [the longest x1 7.64 us: advance_tiles(): pl.pallas_call(functools.partial(advance_kernel, devices, chunks), out_sh...]
    pallas_call x1, Pallas kernels: 1.51 us -> 0.08 us  [pack(): pl.pallas_call(functools.partial(pack_kernel, holder.shape[1]), out_shape...]
    ppermute x45, waiting for transfers between devices: 22.2 us -> 23.1 us  [gather_pieces(): held = held + [lax.ppermute(piece, 'batch', pairs) for piece in held]]
    unnamed x91 -> x20, local copies, waits for them, and re-layouts: 3.07 us -> 2.19 us
  transfers between devices with their start and end apart: 45 -> 45, of which waited for: 19 -> 21; matrix products, arithmetic and copies ran while one was open for 2% -> 0% of each run, Pallas kernels for 0% -> 0%
where the time goes in v3:
time: 69.8 us; the launch traced here: 69.6 us
  starting transfers between devices  29.7 us (43%)
  waiting for transfers between devices  23.1 us (33%)
  Pallas kernels  13.9 us (20%)
  local copies, waits for them, and re-layouts  2.19 us (3%)
  between operations  0.76 us (1%)
    ppermute x45, starting transfers between devices, gather_pieces(): held = held + [lax.ppermute(piece, 'batch', pairs) for piece in held]  29.7 us
    ppermute x45, waiting for transfers between devices, gather_pieces(): held = held + [lax.ppermute(piece, 'batch', pairs) for piece in held]  23.1 us
    pallas_call x1, Pallas kernels, advance_tiles(): pl.pallas_call(functools.partial(advance_kernel, devices, chunks), out_sh...  7.64 us
    pallas_call x1, Pallas kernels, finish(): pl.pallas_call(functools.partial(finish_kernel, devices, per), out_shape=...  3.66 us
    pallas_call x1, Pallas kernels, project(): pl.pallas_call(functools.partial(project_kernel, devices, heads, slots, s...  2.5 us
    unnamed x20, local copies, waits for them, and re-layouts  2.19 us
  transfers between devices with their start and end apart: 45, of which 21 were waited for; matrix products, arithmetic and copies ran while one was open for 0% of the time, Pallas kernels for 0%

profile of v3, /device:TPU:0, one launch (start us, length us, event | category | flops | bytes accessed | tf_op | source)
XLA Modules:
  0.0 69.6 jit_solution(627597472677789818)
XLA Ops:
  0.7 0.8 %copy-done.7 = bf16[3,6144]{1,0:T(4,128)(2,1)S(1)} copy-done((bf16[3,6144]{1,0:T(4,128)(2,1)S(1)}, bf16[3,6144]{1,0:T(4,128)(2,1)}, u32[]{:S(2)}) %copy-start.7) | copy-done | bytes 36888
  2.9 4.1 %collective-permute-start = (bf16[4,6144]{1,0:T(4,128)(2,1)S(1)}, bf16[4,6144]{1,0:T(4,128)(2,1)S(1)}, u32[]{:S(2)}, u32[]{:S(2)}) collective-permute-start(bf16[4,6144]{1,0:T(4,128)(2,1)S(1)} %pack.1.refs_2_), channel_id=1, source_target_pairs={{0,8},{1,9},{2,10},{3,11},{4,12},{5,13},{6,14},{7,15},{8,0},{9,1},... | collective-permute-start | bytes 147464 | tf_op jit(solution)/shard_map/ppermute | solution.py:42
  6.9 1.5 %collective-permute-start.3 = (bf16[4,6144]{1,0:T(4,128)(2,1)S(1)}, bf16[4,6144]{1,0:T(4,128)(2,1)S(1)}, u32[]{:S(2)}, u32[]{:S(2)}) collective-permute-start(bf16[4,6144]{1,0:T(4,128)(2,1)S(1)} %pack.1.refs_2_), channel_id=1, source_target_pairs={{0,2},{1,3},{2,0},{3,1},{4,6},{5,7},{6,4},{7,5},{8,10},{9,11},{10,... | collective-permute-start | bytes 147464 | tf_op jit(solution)/shard_map/ppermute | solution.py:42
  8.4 1.6 %collective-permute-start.1 = (bf16[4,6144]{1,0:T(4,128)(2,1)S(1)}, bf16[4,6144]{1,0:T(4,128)(2,1)S(1)}, u32[]{:S(2)}, u32[]{:S(2)}) collective-permute-start(bf16[4,6144]{1,0:T(4,128)(2,1)S(1)} %pack.1.refs_2_), channel_id=1, source_target_pairs={{0,4},{1,5},{2,6},{3,7},{4,0},{5,1},{6,2},{7,3},{8,12},{9,13},{10,... | collective-permute-start | bytes 147464 | tf_op jit(solution)/shard_map/ppermute | solution.py:42
  10.0 1.2 %collective-permute-start.2 = (bf16[4,6144]{1,0:T(4,128)(2,1)S(1)}, bf16[4,6144]{1,0:T(4,128)(2,1)S(1)}, u32[]{:S(2)}, u32[]{:S(2)}) collective-permute-start(bf16[4,6144]{1,0:T(4,128)(2,1)S(1)} %collective-permute-done.refs_3_), channel_id=1, source_target_pairs={{0,4},{1,5},{2,6},{3,7},{4,0},{5,1},{6,2},{7,3},{8,12},{9,13},{10,... | collective-permute-start | bytes 147464 | tf_op jit(solution)/shard_map/ppermute | solution.py:42
  11.2 1.3 %collective-permute-done.1.refs_4_ = bf16[4,6144]{1,0:T(4,128)(2,1)S(1)} collective-permute-done((bf16[4,6144]{1,0:T(4,128)(2,1)S(1)}, bf16[4,6144]{1,0:T(4,128)(2,1)S(1)}, u32[]{:S(2)}, u32[]{:S(2)}) %collective-permute-start.1) | collective-permute-done | bytes 49184 | tf_op jit(solution)/shard_map/ppermute | solution.py:42
  13.1 1.5 %collective-permute-start.4 = (bf16[4,6144]{1,0:T(4,128)(2,1)S(1)}, bf16[4,6144]{1,0:T(4,128)(2,1)S(1)}, u32[]{:S(2)}, u32[]{:S(2)}) collective-permute-start(bf16[4,6144]{1,0:T(4,128)(2,1)S(1)} %collective-permute-done.refs_3_), channel_id=1, source_target_pairs={{0,2},{1,3},{2,0},{3,1},{4,6},{5,7},{6,4},{7,5},{8,10},{9,11},{10,... | collective-permute-start | bytes 147464 | tf_op jit(solution)/shard_map/ppermute | solution.py:42
  14.6 0.8 %collective-permute-start.6 = (bf16[4,6144]{1,0:T(4,128)(2,1)S(1)}, bf16[4,6144]{1,0:T(4,128)(2,1)S(1)}, u32[]{:S(2)}, u32[]{:S(2)}) collective-permute-start(bf16[4,6144]{1,0:T(4,128)(2,1)S(1)} %collective-permute-done.2.refs_5_), channel_id=1, source_target_pairs={{0,2},{1,3},{2,0},{3,1},{4,6},{5,7},{6,4},{7,5},{8,10},{9,11},{10,... | collective-permute-start | bytes 147464 | tf_op jit(solution)/shard_map/ppermute | solution.py:42
  15.9 1.2 %collective-permute-done.5.refs_8_ = bf16[4,6144]{1,0:T(4,128)(2,1)S(1)} collective-permute-done((bf16[4,6144]{1,0:T(4,128)(2,1)S(1)}, bf16[4,6144]{1,0:T(4,128)(2,1)S(1)}, u32[]{:S(2)}, u32[]{:S(2)}) %collective-permute-start.5) | collective-permute-done | bytes 49184 | tf_op jit(solution)/shard_map/ppermute | solution.py:42
  17.1 1.1 %collective-permute-done.4.refs_7_ = bf16[4,6144]{1,0:T(4,128)(2,1)S(1)} collective-permute-done((bf16[4,6144]{1,0:T(4,128)(2,1)S(1)}, bf16[4,6144]{1,0:T(4,128)(2,1)S(1)}, u32[]{:S(2)}, u32[]{:S(2)}) %collective-permute-start.4) | collective-permute-done | bytes 49184 | tf_op jit(solution)/shard_map/ppermute | solution.py:42
  20.1 2.5 %project.1 = (bf16[48,1024]{1,0:T(8,128)(2,1)S(1)}, s32[32,48]{1,0:T(8,128)S(1)}, s32[8,256]{1,0:T(8,128)S(1)}) custom-call(s32[12,1,16]{2,1,0:T(1,128)S(1)} %bitcast.3, bf16[6144,1024]{1,0:T(8,128)(2,1)S(1)} %copy-done, bf16[4,6144]{1,0:T(4,128)(2,1)S(1)} %pack.1.refs_2_, bf16[4,6144]{1,0:T(4,128)(2,1)S(1)} %collective-permute-done.refs_3_, ...), custom_call_target="tpu_custom_call" | custom-call | flops 603979776 | bytes 12582912 | tf_op jit(solution)/shard_map/project/pallas_call | solution.py:178
  22.6 1.9 %collective-permute-start.15 = (bf16[48,1024]{1,0:T(8,128)(2,1)S(1)}, bf16[48,1024]{1,0:T(8,128)(2,1)S(1)}, u32[]{:S(2)}, u32[]{:S(2)}) collective-permute-start(bf16[48,1024]{1,0:T(8,128)(2,1)S(1)} %get-tuple-element.10.refs_4_), channel_id=1, source_target_pairs={{0,8},{1,9},{2,10},{3,11},{4,12},{5,13},{6,14},{7,15},{8,0},{9,1},... | collective-permute-start | bytes 294920 | tf_op jit(solution)/shard_map/ppermute | solution.py:42
  24.5 1.5 %collective-permute-start.18 = (bf16[48,1024]{1,0:T(8,128)(2,1)S(1)}, bf16[48,1024]{1,0:T(8,128)(2,1)S(1)}, u32[]{:S(2)}, u32[]{:S(2)}) collective-permute-start(bf16[48,1024]{1,0:T(8,128)(2,1)S(1)} %get-tuple-element.10.refs_4_), channel_id=1, source_target_pairs={{0,2},{1,3},{2,0},{3,1},{4,6},{5,7},{6,4},{7,5},{8,10},{9,11},{10,... | collective-permute-start | bytes 294920 | tf_op jit(solution)/shard_map/ppermute | solution.py:42
  25.9 1.5 %collective-permute-start.16 = (bf16[48,1024]{1,0:T(8,128)(2,1)S(1)}, bf16[48,1024]{1,0:T(8,128)(2,1)S(1)}, u32[]{:S(2)}, u32[]{:S(2)}) collective-permute-start(bf16[48,1024]{1,0:T(8,128)(2,1)S(1)} %get-tuple-element.10.refs_4_), channel_id=1, source_target_pairs={{0,4},{1,5},{2,6},{3,7},{4,0},{5,1},{6,2},{7,3},{8,12},{9,13},{10,... | collective-permute-start | bytes 294920 | tf_op jit(solution)/shard_map/ppermute | solution.py:42
  27.5 2.8 %collective-permute-done.15.refs_5_ = bf16[48,1024]{1,0:T(8,128)(2,1)S(1)} collective-permute-done((bf16[48,1024]{1,0:T(8,128)(2,1)S(1)}, bf16[48,1024]{1,0:T(8,128)(2,1)S(1)}, u32[]{:S(2)}, u32[]{:S(2)}) %collective-permute-start.15) | collective-permute-done | bytes 98336 | tf_op jit(solution)/shard_map/ppermute | solution.py:42
  30.3 1.1 %collective-permute-start.17 = (bf16[48,1024]{1,0:T(8,128)(2,1)S(1)}, bf16[48,1024]{1,0:T(8,128)(2,1)S(1)}, u32[]{:S(2)}, u32[]{:S(2)}) collective-permute-start(bf16[48,1024]{1,0:T(8,128)(2,1)S(1)} %collective-permute-done.15.refs_5_), channel_id=1, source_target_pairs={{0,4},{1,5},{2,6},{3,7},{4,0},{5,1},{6,2},{7,3},{8,12},{9,13},{10,... | collective-permute-start | bytes 294920 | tf_op jit(solution)/shard_map/ppermute | solution.py:42
  31.8 0.7 %collective-permute-start.20 = (bf16[48,1024]{1,0:T(8,128)(2,1)S(1)}, bf16[48,1024]{1,0:T(8,128)(2,1)S(1)}, u32[]{:S(2)}, u32[]{:S(2)}) collective-permute-start(bf16[48,1024]{1,0:T(8,128)(2,1)S(1)} %collective-permute-done.16.refs_6_), channel_id=1, source_target_pairs={{0,2},{1,3},{2,0},{3,1},{4,6},{5,7},{6,4},{7,5},{8,10},{9,11},{10,... | collective-permute-start | bytes 294920 | tf_op jit(solution)/shard_map/ppermute | solution.py:42
  32.5 1.3 %collective-permute-start.19 = (bf16[48,1024]{1,0:T(8,128)(2,1)S(1)}, bf16[48,1024]{1,0:T(8,128)(2,1)S(1)}, u32[]{:S(2)}, u32[]{:S(2)}) collective-permute-start(bf16[48,1024]{1,0:T(8,128)(2,1)S(1)} %collective-permute-done.15.refs_5_), channel_id=1, source_target_pairs={{0,2},{1,3},{2,0},{3,1},{4,6},{5,7},{6,4},{7,5},{8,10},{9,11},{10,... | collective-permute-start | bytes 294920 | tf_op jit(solution)/shard_map/ppermute | solution.py:42
  33.9 1.0 %collective-permute-done.17.refs_7_ = bf16[48,1024]{1,0:T(8,128)(2,1)S(1)} collective-permute-done((bf16[48,1024]{1,0:T(8,128)(2,1)S(1)}, bf16[48,1024]{1,0:T(8,128)(2,1)S(1)}, u32[]{:S(2)}, u32[]{:S(2)}) %collective-permute-start.17) | collective-permute-done | bytes 98336 | tf_op jit(solution)/shard_map/ppermute | solution.py:42
  36.1 1.4 %collective-permute-done.20.refs_10_ = bf16[48,1024]{1,0:T(8,128)(2,1)S(1)} collective-permute-done((bf16[48,1024]{1,0:T(8,128)(2,1)S(1)}, bf16[48,1024]{1,0:T(8,128)(2,1)S(1)}, u32[]{:S(2)}, u32[]{:S(2)}) %collective-permute-start.20) | collective-permute-done | bytes 98336 | tf_op jit(solution)/shard_map/ppermute | solution.py:42
  37.5 2.1 %collective-permute-done.19.refs_9_ = bf16[48,1024]{1,0:T(8,128)(2,1)S(1)} collective-permute-done((bf16[48,1024]{1,0:T(8,128)(2,1)S(1)}, bf16[48,1024]{1,0:T(8,128)(2,1)S(1)}, u32[]{:S(2)}, u32[]{:S(2)}) %collective-permute-start.19) | collective-permute-done | bytes 98336 | tf_op jit(solution)/shard_map/ppermute | solution.py:42
  39.6 1.2 %collective-permute-done.21.refs_11_ = bf16[48,1024]{1,0:T(8,128)(2,1)S(1)} collective-permute-done((bf16[48,1024]{1,0:T(8,128)(2,1)S(1)}, bf16[48,1024]{1,0:T(8,128)(2,1)S(1)}, u32[]{:S(2)}, u32[]{:S(2)}) %collective-permute-start.21) | collective-permute-done | bytes 98336 | tf_op jit(solution)/shard_map/ppermute | solution.py:42
  40.9 1.2 %collective-permute-done.29.refs_19_ = bf16[48,1024]{1,0:T(8,128)(2,1)S(1)} collective-permute-done((bf16[48,1024]{1,0:T(8,128)(2,1)S(1)}, bf16[48,1024]{1,0:T(8,128)(2,1)S(1)}, u32[]{:S(2)}, u32[]{:S(2)}) %collective-permute-start.29) | collective-permute-done | bytes 98336 | tf_op jit(solution)/shard_map/ppermute | solution.py:42
  42.1 7.6 %advance.1 = (bf16[192,128]{1,0:T(8,128)(2,1)S(1)}, f32[6152,128]{1,0:T(8,128)S(1)}, bf16[168,128,128]{2,1,0:T(8,128)(2,1)}) custom-call(s32[8,256]{1,0:T(8,128)S(1)} %get-tuple-element.9.refs_0_, f32[32]{0:T(128)S(1)} %copy-done.6, f32[168]{0:T(256)S(1)} %copy-done.5, bf16[168,128,128]{2,1,0:T(8,128)(2,1)S(1)} %copy-done.1, ...), custom_call_target="tpu_custom_call" | custom-call | flops 11010048 | bytes 11010048 | tf_op jit(solution)/shard_map/advance/pallas_call | solution.py:277
  49.8 2.7 %collective-permute-start.30 = (bf16[192,128]{1,0:T(8,128)(2,1)S(1)}, bf16[192,128]{1,0:T(8,128)(2,1)S(1)}, u32[]{:S(2)}, u32[]{:S(2)}) collective-permute-start(bf16[192,128]{1,0:T(8,128)(2,1)S(1)} %get-tuple-element.12.refs_4_), channel_id=1, source_target_pairs={{0,8},{1,9},{2,10},{3,11},{4,12},{5,13},{6,14},{7,15},{8,0},{9,1},... | collective-permute-start | bytes 147464 | tf_op jit(solution)/shard_map/ppermute | solution.py:42
  52.4 1.5 %collective-permute-start.33 = (bf16[192,128]{1,0:T(8,128)(2,1)S(1)}, bf16[192,128]{1,0:T(8,128)(2,1)S(1)}, u32[]{:S(2)}, u32[]{:S(2)}) collective-permute-start(bf16[192,128]{1,0:T(8,128)(2,1)S(1)} %get-tuple-element.12.refs_4_), channel_id=1, source_target_pairs={{0,2},{1,3},{2,0},{3,1},{4,6},{5,7},{6,4},{7,5},{8,10},{9,11},{10,... | collective-permute-start | bytes 147464 | tf_op jit(solution)/shard_map/ppermute | solution.py:42
  54.5 1.1 %collective-permute-done.30.refs_5_ = bf16[192,128]{1,0:T(8,128)(2,1)S(1)} collective-permute-done((bf16[192,128]{1,0:T(8,128)(2,1)S(1)}, bf16[192,128]{1,0:T(8,128)(2,1)S(1)}, u32[]{:S(2)}, u32[]{:S(2)}) %collective-permute-start.30) | collective-permute-done | bytes 49184 | tf_op jit(solution)/shard_map/ppermute | solution.py:42
  56.5 1.9 %collective-permute-done.31.refs_6_ = bf16[192,128]{1,0:T(8,128)(2,1)S(1)} collective-permute-done((bf16[192,128]{1,0:T(8,128)(2,1)S(1)}, bf16[192,128]{1,0:T(8,128)(2,1)S(1)}, u32[]{:S(2)}, u32[]{:S(2)}) %collective-permute-start.31) | collective-permute-done | bytes 49184 | tf_op jit(solution)/shard_map/ppermute | solution.py:42
  58.6 1.9 %collective-permute-start.34 = (bf16[192,128]{1,0:T(8,128)(2,1)S(1)}, bf16[192,128]{1,0:T(8,128)(2,1)S(1)}, u32[]{:S(2)}, u32[]{:S(2)}) collective-permute-start(bf16[192,128]{1,0:T(8,128)(2,1)S(1)} %collective-permute-done.30.refs_5_), channel_id=1, source_target_pairs={{0,2},{1,3},{2,0},{3,1},{4,6},{5,7},{6,4},{7,5},{8,10},{9,11},{10,... | collective-permute-start | bytes 147464 | tf_op jit(solution)/shard_map/ppermute | solution.py:42
  61.7 1.3 %collective-permute-done.35.refs_10_ = bf16[192,128]{1,0:T(8,128)(2,1)S(1)} collective-permute-done((bf16[192,128]{1,0:T(8,128)(2,1)S(1)}, bf16[192,128]{1,0:T(8,128)(2,1)S(1)}, u32[]{:S(2)}, u32[]{:S(2)}) %collective-permute-start.35) | collective-permute-done | bytes 49184 | tf_op jit(solution)/shard_map/ppermute | solution.py:42
  63.0 1.1 %collective-permute-done.34.refs_9_ = bf16[192,128]{1,0:T(8,128)(2,1)S(1)} collective-permute-done((bf16[192,128]{1,0:T(8,128)(2,1)S(1)}, bf16[192,128]{1,0:T(8,128)(2,1)S(1)}, u32[]{:S(2)}, u32[]{:S(2)}) %collective-permute-start.34) | collective-permute-done | bytes 49184 | tf_op jit(solution)/shard_map/ppermute | solution.py:42
  65.9 3.7 %finish.1 = bf16[48,384]{1,0:T(8,128)(2,1)} custom-call(s32[32,48]{1,0:T(8,128)S(1)} %get-tuple-element.8.refs_0_, f32[6152,128]{1,0:T(8,128)S(1)} %get-tuple-element.11.refs_1_, f32[32,128]{1,0:T(8,128)S(1)} %bitcast.2, bf16[4096,384]{1,0:T(8,128)(2,1)S(1)} %copy-done.2, bf16[192,128]{1,0:T(8,128)(2,1)S(1)} %get-tuple-element.12.refs_4_, ...), custom_call_target="tpu_custom_call" | custom-call | flops 150994944 | bytes 3145728 | tf_op jit(solution)/shard_map/finish/pallas_call | solution.py:345
  (82 shorter events, 11.0 us)
Async XLA Ops:
  2.9 7.1 %collective-permute-start = (bf16[4,6144]{1,0:T(4,128)(2,1)S(1)}, bf16[4,6144]{1,0:T(4,128)(2,1)S(1)}, u32[]{:S(2)}, u32[]{:S(2)}) collective-permute-start(bf16[4,6144]{1,0:T(4,128)(2,1)S(1)} %pack.1.refs_2_), channel_id=1, source_target_pairs={{0,8},{1,9},{2,10},{3,11},{4,12},{5,13},{6,14},{7,15},{8,0},{9,1},... | collective-permute-start | bytes 147464 | tf_op jit(solution)/shard_map/ppermute | solution.py:42
  6.9 4.2 %collective-permute-start.3 = (bf16[4,6144]{1,0:T(4,128)(2,1)S(1)}, bf16[4,6144]{1,0:T(4,128)(2,1)S(1)}, u32[]{:S(2)}, u32[]{:S(2)}) collective-permute-start(bf16[4,6144]{1,0:T(4,128)(2,1)S(1)} %pack.1.refs_2_), channel_id=1, source_target_pairs={{0,2},{1,3},{2,0},{3,1},{4,6},{5,7},{6,4},{7,5},{8,10},{9,11},{10,... | collective-permute-start | bytes 147464 | tf_op jit(solution)/shard_map/ppermute | solution.py:42
  8.4 4.1 %collective-permute-start.1 = (bf16[4,6144]{1,0:T(4,128)(2,1)S(1)}, bf16[4,6144]{1,0:T(4,128)(2,1)S(1)}, u32[]{:S(2)}, u32[]{:S(2)}) collective-permute-start(bf16[4,6144]{1,0:T(4,128)(2,1)S(1)} %pack.1.refs_2_), channel_id=1, source_target_pairs={{0,4},{1,5},{2,6},{3,7},{4,0},{5,1},{6,2},{7,3},{8,12},{9,13},{10,... | collective-permute-start | bytes 147464 | tf_op jit(solution)/shard_map/ppermute | solution.py:42
  10.0 4.5 %collective-permute-start.2 = (bf16[4,6144]{1,0:T(4,128)(2,1)S(1)}, bf16[4,6144]{1,0:T(4,128)(2,1)S(1)}, u32[]{:S(2)}, u32[]{:S(2)}) collective-permute-start(bf16[4,6144]{1,0:T(4,128)(2,1)S(1)} %collective-permute-done.refs_3_), channel_id=1, source_target_pairs={{0,4},{1,5},{2,6},{3,7},{4,0},{5,1},{6,2},{7,3},{8,12},{9,13},{10,... | collective-permute-start | bytes 147464 | tf_op jit(solution)/shard_map/ppermute | solution.py:42
  11.2 4.2 %collective-permute-start.11 = (bf16[4,6144]{1,0:T(4,128)(2,1)S(1)}, bf16[4,6144]{1,0:T(4,128)(2,1)S(1)}, u32[]{:S(2)}, u32[]{:S(2)}) collective-permute-start(bf16[4,6144]{1,0:T(4,128)(2,1)S(1)} %collective-permute-done.3.refs_6_), channel_id=1, source_target_pairs={{0,1},{1,0},{2,3},{3,2},{4,5},{5,4},{6,7},{7,6},{8,9},{9,8},{10,11... | collective-permute-start | bytes 147464 | tf_op jit(solution)/shard_map/ppermute | solution.py:42
  12.5 4.5 %collective-permute-start.5 = (bf16[4,6144]{1,0:T(4,128)(2,1)S(1)}, bf16[4,6144]{1,0:T(4,128)(2,1)S(1)}, u32[]{:S(2)}, u32[]{:S(2)}) collective-permute-start(bf16[4,6144]{1,0:T(4,128)(2,1)S(1)} %collective-permute-done.1.refs_4_), channel_id=1, source_target_pairs={{0,2},{1,3},{2,0},{3,1},{4,6},{5,7},{6,4},{7,5},{8,10},{9,11},{10,... | collective-permute-start | bytes 147464 | tf_op jit(solution)/shard_map/ppermute | solution.py:42
  13.1 5.1 %collective-permute-start.4 = (bf16[4,6144]{1,0:T(4,128)(2,1)S(1)}, bf16[4,6144]{1,0:T(4,128)(2,1)S(1)}, u32[]{:S(2)}, u32[]{:S(2)}) collective-permute-start(bf16[4,6144]{1,0:T(4,128)(2,1)S(1)} %collective-permute-done.refs_3_), channel_id=1, source_target_pairs={{0,2},{1,3},{2,0},{3,1},{4,6},{5,7},{6,4},{7,5},{8,10},{9,11},{10,... | collective-permute-start | bytes 147464 | tf_op jit(solution)/shard_map/ppermute | solution.py:42
  14.6 4.2 %collective-permute-start.6 = (bf16[4,6144]{1,0:T(4,128)(2,1)S(1)}, bf16[4,6144]{1,0:T(4,128)(2,1)S(1)}, u32[]{:S(2)}, u32[]{:S(2)}) collective-permute-start(bf16[4,6144]{1,0:T(4,128)(2,1)S(1)} %collective-permute-done.2.refs_5_), channel_id=1, source_target_pairs={{0,2},{1,3},{2,0},{3,1},{4,6},{5,7},{6,4},{7,5},{8,10},{9,11},{10,... | collective-permute-start | bytes 147464 | tf_op jit(solution)/shard_map/ppermute | solution.py:42
  15.4 4.0 %collective-permute-start.10 = (bf16[4,6144]{1,0:T(4,128)(2,1)S(1)}, bf16[4,6144]{1,0:T(4,128)(2,1)S(1)}, u32[]{:S(2)}, u32[]{:S(2)}) collective-permute-start(bf16[4,6144]{1,0:T(4,128)(2,1)S(1)} %collective-permute-done.2.refs_5_), channel_id=1, source_target_pairs={{0,1},{1,0},{2,3},{3,2},{4,5},{5,4},{6,7},{7,6},{8,9},{9,8},{10,11... | collective-permute-start | bytes 147464 | tf_op jit(solution)/shard_map/ppermute | solution.py:42
  22.6 7.7 %collective-permute-start.15 = (bf16[48,1024]{1,0:T(8,128)(2,1)S(1)}, bf16[48,1024]{1,0:T(8,128)(2,1)S(1)}, u32[]{:S(2)}, u32[]{:S(2)}) collective-permute-start(bf16[48,1024]{1,0:T(8,128)(2,1)S(1)} %get-tuple-element.10.refs_4_), channel_id=1, source_target_pairs={{0,8},{1,9},{2,10},{3,11},{4,12},{5,13},{6,14},{7,15},{8,0},{9,1},... | collective-permute-start | bytes 294920 | tf_op jit(solution)/shard_map/ppermute | solution.py:42
  24.5 6.8 %collective-permute-start.18 = (bf16[48,1024]{1,0:T(8,128)(2,1)S(1)}, bf16[48,1024]{1,0:T(8,128)(2,1)S(1)}, u32[]{:S(2)}, u32[]{:S(2)}) collective-permute-start(bf16[48,1024]{1,0:T(8,128)(2,1)S(1)} %get-tuple-element.10.refs_4_), channel_id=1, source_target_pairs={{0,2},{1,3},{2,0},{3,1},{4,6},{5,7},{6,4},{7,5},{8,10},{9,11},{10,... | collective-permute-start | bytes 294920 | tf_op jit(solution)/shard_map/ppermute | solution.py:42
  25.9 5.4 %collective-permute-start.16 = (bf16[48,1024]{1,0:T(8,128)(2,1)S(1)}, bf16[48,1024]{1,0:T(8,128)(2,1)S(1)}, u32[]{:S(2)}, u32[]{:S(2)}) collective-permute-start(bf16[48,1024]{1,0:T(8,128)(2,1)S(1)} %get-tuple-element.10.refs_4_), channel_id=1, source_target_pairs={{0,4},{1,5},{2,6},{3,7},{4,0},{5,1},{6,2},{7,3},{8,12},{9,13},{10,... | collective-permute-start | bytes 294920 | tf_op jit(solution)/shard_map/ppermute | solution.py:42
  27.5 5.1 %collective-permute-start.22 = (bf16[48,1024]{1,0:T(8,128)(2,1)S(1)}, bf16[48,1024]{1,0:T(8,128)(2,1)S(1)}, u32[]{:S(2)}, u32[]{:S(2)}) collective-permute-start(bf16[48,1024]{1,0:T(8,128)(2,1)S(1)} %get-tuple-element.10.refs_4_), channel_id=1, source_target_pairs={{0,1},{1,0},{2,3},{3,2},{4,5},{5,4},{6,7},{7,6},{8,9},{9,8},{10,11... | collective-permute-start | bytes 294920 | tf_op jit(solution)/shard_map/ppermute | solution.py:42
  30.3 4.6 %collective-permute-start.17 = (bf16[48,1024]{1,0:T(8,128)(2,1)S(1)}, bf16[48,1024]{1,0:T(8,128)(2,1)S(1)}, u32[]{:S(2)}, u32[]{:S(2)}) collective-permute-start(bf16[48,1024]{1,0:T(8,128)(2,1)S(1)} %collective-permute-done.15.refs_5_), channel_id=1, source_target_pairs={{0,4},{1,5},{2,6},{3,7},{4,0},{5,1},{6,2},{7,3},{8,12},{9,13},{10,... | collective-permute-start | bytes 294920 | tf_op jit(solution)/shard_map/ppermute | solution.py:42
  31.3 4.2 %collective-permute-start.26 = (bf16[48,1024]{1,0:T(8,128)(2,1)S(1)}, bf16[48,1024]{1,0:T(8,128)(2,1)S(1)}, u32[]{:S(2)}, u32[]{:S(2)}) collective-permute-start(bf16[48,1024]{1,0:T(8,128)(2,1)S(1)} %collective-permute-done.18.refs_8_), channel_id=1, source_target_pairs={{0,1},{1,0},{2,3},{3,2},{4,5},{5,4},{6,7},{7,6},{8,9},{9,8},{10,11... | collective-permute-start | bytes 294920 | tf_op jit(solution)/shard_map/ppermute | solution.py:42
  31.3 4.2 %collective-permute-start.24 = (bf16[48,1024]{1,0:T(8,128)(2,1)S(1)}, bf16[48,1024]{1,0:T(8,128)(2,1)S(1)}, u32[]{:S(2)}, u32[]{:S(2)}) collective-permute-start(bf16[48,1024]{1,0:T(8,128)(2,1)S(1)} %collective-permute-done.16.refs_6_), channel_id=1, source_target_pairs={{0,1},{1,0},{2,3},{3,2},{4,5},{5,4},{6,7},{7,6},{8,9},{9,8},{10,11... | collective-permute-start | bytes 294920 | tf_op jit(solution)/shard_map/ppermute | solution.py:42
  31.8 5.7 %collective-permute-start.20 = (bf16[48,1024]{1,0:T(8,128)(2,1)S(1)}, bf16[48,1024]{1,0:T(8,128)(2,1)S(1)}, u32[]{:S(2)}, u32[]{:S(2)}) collective-permute-start(bf16[48,1024]{1,0:T(8,128)(2,1)S(1)} %collective-permute-done.16.refs_6_), channel_id=1, source_target_pairs={{0,2},{1,3},{2,0},{3,1},{4,6},{5,7},{6,4},{7,5},{8,10},{9,11},{10,... | collective-permute-start | bytes 294920 | tf_op jit(solution)/shard_map/ppermute | solution.py:42
  32.5 7.1 %collective-permute-start.19 = (bf16[48,1024]{1,0:T(8,128)(2,1)S(1)}, bf16[48,1024]{1,0:T(8,128)(2,1)S(1)}, u32[]{:S(2)}, u32[]{:S(2)}) collective-permute-start(bf16[48,1024]{1,0:T(8,128)(2,1)S(1)} %collective-permute-done.15.refs_5_), channel_id=1, source_target_pairs={{0,2},{1,3},{2,0},{3,1},{4,6},{5,7},{6,4},{7,5},{8,10},{9,11},{10,... | collective-permute-start | bytes 294920 | tf_op jit(solution)/shard_map/ppermute | solution.py:42
  34.9 6.0 %collective-permute-start.21 = (bf16[48,1024]{1,0:T(8,128)(2,1)S(1)}, bf16[48,1024]{1,0:T(8,128)(2,1)S(1)}, u32[]{:S(2)}, u32[]{:S(2)}) collective-permute-start(bf16[48,1024]{1,0:T(8,128)(2,1)S(1)} %collective-permute-done.17.refs_7_), channel_id=1, source_target_pairs={{0,2},{1,3},{2,0},{3,1},{4,6},{5,7},{6,4},{7,5},{8,10},{9,11},{10,... | collective-permute-start | bytes 294920 | tf_op jit(solution)/shard_map/ppermute | solution.py:42
  35.6 5.3 %collective-permute-start.23 = (bf16[48,1024]{1,0:T(8,128)(2,1)S(1)}, bf16[48,1024]{1,0:T(8,128)(2,1)S(1)}, u32[]{:S(2)}, u32[]{:S(2)}) collective-permute-start(bf16[48,1024]{1,0:T(8,128)(2,1)S(1)} %collective-permute-done.15.refs_5_), channel_id=1, source_target_pairs={{0,1},{1,0},{2,3},{3,2},{4,5},{5,4},{6,7},{7,6},{8,9},{9,8},{10,11... | collective-permute-start | bytes 294920 | tf_op jit(solution)/shard_map/ppermute | solution.py:42
  35.6 5.3 %collective-permute-start.25 = (bf16[48,1024]{1,0:T(8,128)(2,1)S(1)}, bf16[48,1024]{1,0:T(8,128)(2,1)S(1)}, u32[]{:S(2)}, u32[]{:S(2)}) collective-permute-start(bf16[48,1024]{1,0:T(8,128)(2,1)S(1)} %collective-permute-done.17.refs_7_), channel_id=1, source_target_pairs={{0,1},{1,0},{2,3},{3,2},{4,5},{5,4},{6,7},{7,6},{8,9},{9,8},{10,11... | collective-permute-start | bytes 294920 | tf_op jit(solution)/shard_map/ppermute | solution.py:42
  49.8 5.8 %collective-permute-start.30 = (bf16[192,128]{1,0:T(8,128)(2,1)S(1)}, bf16[192,128]{1,0:T(8,128)(2,1)S(1)}, u32[]{:S(2)}, u32[]{:S(2)}) collective-permute-start(bf16[192,128]{1,0:T(8,128)(2,1)S(1)} %get-tuple-element.12.refs_4_), channel_id=1, source_target_pairs={{0,8},{1,9},{2,10},{3,11},{4,12},{5,13},{6,14},{7,15},{8,0},{9,1},... | collective-permute-start | bytes 147464 | tf_op jit(solution)/shard_map/ppermute | solution.py:42
  52.4 4.1 %collective-permute-start.33 = (bf16[192,128]{1,0:T(8,128)(2,1)S(1)}, bf16[192,128]{1,0:T(8,128)(2,1)S(1)}, u32[]{:S(2)}, u32[]{:S(2)}) collective-permute-start(bf16[192,128]{1,0:T(8,128)(2,1)S(1)} %get-tuple-element.12.refs_4_), channel_id=1, source_target_pairs={{0,2},{1,3},{2,0},{3,1},{4,6},{5,7},{6,4},{7,5},{8,10},{9,11},{10,... | collective-permute-start | bytes 147464 | tf_op jit(solution)/shard_map/ppermute | solution.py:42
  53.9 4.5 %collective-permute-start.31 = (bf16[192,128]{1,0:T(8,128)(2,1)S(1)}, bf16[192,128]{1,0:T(8,128)(2,1)S(1)}, u32[]{:S(2)}, u32[]{:S(2)}) collective-permute-start(bf16[192,128]{1,0:T(8,128)(2,1)S(1)} %get-tuple-element.12.refs_4_), channel_id=1, source_target_pairs={{0,4},{1,5},{2,6},{3,7},{4,0},{5,1},{6,2},{7,3},{8,12},{9,13},{10,... | collective-permute-start | bytes 147464 | tf_op jit(solution)/shard_map/ppermute | solution.py:42
  54.5 4.1 %collective-permute-start.37 = (bf16[192,128]{1,0:T(8,128)(2,1)S(1)}, bf16[192,128]{1,0:T(8,128)(2,1)S(1)}, u32[]{:S(2)}, u32[]{:S(2)}) collective-permute-start(bf16[192,128]{1,0:T(8,128)(2,1)S(1)} %get-tuple-element.12.refs_4_), channel_id=1, source_target_pairs={{0,1},{1,0},{2,3},{3,2},{4,5},{5,4},{6,7},{7,6},{8,9},{9,8},{10,11... | collective-permute-start | bytes 147464 | tf_op jit(solution)/shard_map/ppermute | solution.py:42
  55.6 4.9 %collective-permute-start.32 = (bf16[192,128]{1,0:T(8,128)(2,1)S(1)}, bf16[192,128]{1,0:T(8,128)(2,1)S(1)}, u32[]{:S(2)}, u32[]{:S(2)}) collective-permute-start(bf16[192,128]{1,0:T(8,128)(2,1)S(1)} %collective-permute-done.30.refs_5_), channel_id=1, source_target_pairs={{0,4},{1,5},{2,6},{3,7},{4,0},{5,1},{6,2},{7,3},{8,12},{9,13},{10,... | collective-permute-start | bytes 147464 | tf_op jit(solution)/shard_map/ppermute | solution.py:42
  56.5 4.6 %collective-permute-start.41 = (bf16[192,128]{1,0:T(8,128)(2,1)S(1)}, bf16[192,128]{1,0:T(8,128)(2,1)S(1)}, u32[]{:S(2)}, u32[]{:S(2)}) collective-permute-start(bf16[192,128]{1,0:T(8,128)(2,1)S(1)} %collective-permute-done.33.refs_8_), channel_id=1, source_target_pairs={{0,1},{1,0},{2,3},{3,2},{4,5},{5,4},{6,7},{7,6},{8,9},{9,8},{10,11... | collective-permute-start | bytes 147464 | tf_op jit(solution)/shard_map/ppermute | solution.py:42
  58.4 4.5 %collective-permute-start.35 = (bf16[192,128]{1,0:T(8,128)(2,1)S(1)}, bf16[192,128]{1,0:T(8,128)(2,1)S(1)}, u32[]{:S(2)}, u32[]{:S(2)}) collective-permute-start(bf16[192,128]{1,0:T(8,128)(2,1)S(1)} %collective-permute-done.31.refs_6_), channel_id=1, source_target_pairs={{0,2},{1,3},{2,0},{3,1},{4,6},{5,7},{6,4},{7,5},{8,10},{9,11},{10,... | collective-permute-start | bytes 147464 | tf_op jit(solution)/shard_map/ppermute | solution.py:42
  58.6 5.4 %collective-permute-start.34 = (bf16[192,128]{1,0:T(8,128)(2,1)S(1)}, bf16[192,128]{1,0:T(8,128)(2,1)S(1)}, u32[]{:S(2)}, u32[]{:S(2)}) collective-permute-start(bf16[192,128]{1,0:T(8,128)(2,1)S(1)} %collective-permute-done.30.refs_5_), channel_id=1, source_target_pairs={{0,2},{1,3},{2,0},{3,1},{4,6},{5,7},{6,4},{7,5},{8,10},{9,11},{10,... | collective-permute-start | bytes 147464 | tf_op jit(solution)/shard_map/ppermute | solution.py:42
  60.4 4.2 %collective-permute-start.36 = (bf16[192,128]{1,0:T(8,128)(2,1)S(1)}, bf16[192,128]{1,0:T(8,128)(2,1)S(1)}, u32[]{:S(2)}, u32[]{:S(2)}) collective-permute-start(bf16[192,128]{1,0:T(8,128)(2,1)S(1)} %collective-permute-done.32.refs_7_), channel_id=1, source_target_pairs={{0,2},{1,3},{2,0},{3,1},{4,6},{5,7},{6,4},{7,5},{8,10},{9,11},{10,... | collective-permute-start | bytes 147464 | tf_op jit(solution)/shard_map/ppermute | solution.py:42
  61.1 3.5 %collective-permute-start.38 = (bf16[192,128]{1,0:T(8,128)(2,1)S(1)}, bf16[192,128]{1,0:T(8,128)(2,1)S(1)}, u32[]{:S(2)}, u32[]{:S(2)}) collective-permute-start(bf16[192,128]{1,0:T(8,128)(2,1)S(1)} %collective-permute-done.30.refs_5_), channel_id=1, source_target_pairs={{0,1},{1,0},{2,3},{3,2},{4,5},{5,4},{6,7},{7,6},{8,9},{9,8},{10,11... | collective-permute-start | bytes 147464 | tf_op jit(solution)/shard_map/ppermute | solution.py:42
  61.1 4.1 %collective-permute-start.40 = (bf16[192,128]{1,0:T(8,128)(2,1)S(1)}, bf16[192,128]{1,0:T(8,128)(2,1)S(1)}, u32[]{:S(2)}, u32[]{:S(2)}) collective-permute-start(bf16[192,128]{1,0:T(8,128)(2,1)S(1)} %collective-permute-done.32.refs_7_), channel_id=1, source_target_pairs={{0,1},{1,0},{2,3},{3,2},{4,5},{5,4},{6,7},{7,6},{8,9},{9,8},{10,11... | collective-permute-start | bytes 147464 | tf_op jit(solution)/shard_map/ppermute | solution.py:42
  (23 other events, 218.2 us)

commit v4 on v3

--- a/solution.py
+++ b/solution.py
@@ -35,11 +35,14 @@
     return sum(((crossed >> k) & 1) << (bits - 1 - k) for k in range(bits))
 
 
+def cross(piece, bit, devices):
+    return lax.ppermute(piece, "batch", [(i, i ^ bit) for i in range(devices)])
+
+
 def gather_pieces(block, devices):
     held, bit = [block], devices // 2
     while bit >= 1:
-        pairs = [(i, i ^ bit) for i in range(devices)]
-        held = held + [lax.ppermute(piece, "batch", pairs) for piece in held]
+        held = held + [cross(piece, bit, devices) for piece in held]
         bit //= 2
     return held
 
@@ -197,16 +200,13 @@
     )(send, w, *pieces)
 
 
-def advance_kernel(devices, chunks, *refs):
+def readout_kernel(devices, *refs):
     slot_ref, rate_ref, scale_ref, cache_ref = refs[:4]
     pieces = refs[4 : 4 + devices]
-    read_ref, flat_ref, out_ref, fresh, query, keys, values, reads, sems, *stage = refs[
-        4 + devices :
-    ]
+    read_ref, flat_ref, key_ref, value_ref, query, reads, *stage = refs[4 + devices :]
     sessions, cols = pieces[0].shape
     per = cols // 128
     slots = cache_ref.shape[0]
-    step = slots // chunks
     for j in range(devices):
         block = fetch(pieces[j], stage)
         for b in range(per):
@@ -220,86 +220,118 @@
         for u in range(8):
             e = group * 8 + u
             query[pl.ds(e, 1), :] = flat_ref[pl.ds(slot_ref[0, e], 1), :]
-            keys[pl.ds(e, 1), :] = flat_ref[pl.ds(slot_ref[1, e], 1), :]
-            values[pl.ds(e, 1), :] = flat_ref[pl.ds(slot_ref[2, e], 1), :]
+            key_ref[pl.ds(e, 1), :] = flat_ref[pl.ds(slot_ref[1, e], 1), :]
+            value_ref[pl.ds(e, 1), :] = flat_ref[pl.ds(slot_ref[2, e], 1), :]
 
     rows8 = lax.broadcasted_iota(I32, (8, 128), 0)
-
-    def advance(base):
+    for base in range(0, slots, 8):
         q8 = query[base : base + 8, :]
-        k8 = keys[base : base + 8, :]
-        v8 = values[base : base + 8, :]
-        rate = jnp.zeros((8, 128), F32)
-        scale = jnp.ones((8, 128), F32)
-        for u in range(8):
-            head = slot_ref[3, base + u]
-            one = jnp.where(head < 0, 0.0, rate_ref[jnp.maximum(head, 0)])
-            rate = jnp.where(rows8 == u, one, rate)
-            scale = jnp.where(rows8 == u, scale_ref[base + u], scale)
-        decay = jnp.exp(-rate)
-        scaled = v8 * (1.0 / scale)
-        columns = k8.T
+        decay, scale = factors(slot_ref, rate_ref, scale_ref, base)
         wide = jnp.concatenate([cache_ref[base + u] for u in range(8)], axis=1)
         prod = jnp.dot(q8.astype(BF16), wide, preferred_element_type=F32)
         seen = jnp.zeros((8, 128), F32)
         for u in range(8):
             seen = jnp.where(rows8 == u, prod[:, u * 128 : (u + 1) * 128], seen)
-            fresh[base + u] = (
-                decay[u : u + 1, :] * cache_ref[base + u].astype(F32)
-                + columns[:, u : u + 1] * scaled[u : u + 1, :]
-            ).astype(BF16)
-        near = jnp.sum(q8 * k8, axis=1, keepdims=True)
-        result = seen * (decay * scale) + near * v8
+        near = jnp.sum(q8 * key_ref[base : base + 8, :], axis=1, keepdims=True)
+        result = seen * (decay * scale) + near * value_ref[base : base + 8, :]
         for u in range(8):
             reads[pl.ds(slot_ref[4, base + u], 1), :] = result[u : u + 1, :]
-
-    backs = []
-    for c in range(chunks):
-        for base in range(c * step, (c + 1) * step, 8):
-            advance(base)
-        part = pl.ds(c * step, step)
-        backs.append(pltpu.make_async_copy(fresh.at[part], out_ref.at[part], sems.at[c]))
-        backs[-1].start()
     entries = read_ref.shape[0]
     read_ref[...] = reads[:entries, :].astype(BF16)
-    for back in backs:
-        back.wait()
-
-
-def advance_tiles(pieces, cache, slot, rate, scale, capacity):
+
+
+def factors(slot_ref, rate_ref, scale_ref, base):
+    rows8 = lax.broadcasted_iota(I32, (8, 128), 0)
+    rate = jnp.zeros((8, 128), F32)
+    scale = jnp.ones((8, 128), F32)
+    for u in range(8):
+        head = slot_ref[3, base + u]
+        one = jnp.where(head < 0, 0.0, rate_ref[jnp.maximum(head, 0)])
+        rate = jnp.where(rows8 == u, one, rate)
+        scale = jnp.where(rows8 == u, scale_ref[base + u], scale)
+    return jnp.exp(-rate), scale
+
+
+def read_states(pieces, cache, slot, rate, scale, capacity):
     devices = len(pieces)
     entries = devices * capacity
     sessions, cols = pieces[0].shape
     slots = cache.shape[0]
-    chunks = 7 if slots % 56 == 0 else 1
     large = is_large(*pieces)
     flat = jax.ShapeDtypeStruct((devices * sessions * cols // 128 + 8, 128), F32)
+    rows = jax.ShapeDtypeStruct((slots, 128), F32)
     return pl.pallas_call(
-        functools.partial(advance_kernel, devices, chunks),
-        out_shape=(
-            jax.ShapeDtypeStruct((entries, 128), BF16),
-            flat,
-            jax.ShapeDtypeStruct(cache.shape, BF16),
-        ),
+        functools.partial(readout_kernel, devices),
+        out_shape=(jax.ShapeDtypeStruct((entries, 128), BF16), flat, rows, rows),
         in_specs=[SMEM] * 3 + [VMEM] + [ANY if large else VMEM] * devices,
-        out_specs=(VMEM, VMEM, ANY),
+        out_specs=(VMEM, VMEM, VMEM, VMEM),
         scratch_shapes=[
-            pltpu.VMEM(cache.shape, BF16),
-            pltpu.VMEM((slots, 128), F32),
-            pltpu.VMEM((slots, 128), F32),
             pltpu.VMEM((slots, 128), F32),
             pltpu.VMEM((entries + 8, 128), F32),
-            pltpu.SemaphoreType.DMA((chunks,)),
         ]
         + ([pltpu.VMEM((sessions, cols), BF16), pltpu.SemaphoreType.DMA] if large else []),
         compiler_params=pltpu.CompilerParams(
-            vmem_limit_bytes=grant(cache, cache, flat, *([] if large else pieces))
+            vmem_limit_bytes=grant(cache, flat, *([] if large else pieces))
         ),
         cost_estimate=pl.CostEstimate(
-            flops=4 * cache.size, bytes_accessed=4 * cache.size, transcendentals=0
-        ),
-        name="advance",
+            flops=2 * cache.size, bytes_accessed=8 * cache.size, transcendentals=0
+        ),
+        name="readout",
     )(slot, rate, scale, cache, *pieces)
+
+
+def update_kernel(first, count, *refs):
+    slot_ref, rate_ref, scale_ref, cache_ref, key_ref, value_ref = refs[:6]
+    out_ref, fresh, sems = refs[-3:]
+    rows8 = lax.broadcasted_iota(I32, (8, 128), 0)
+    backs = []
+    for base in range(first, first + count, 8):
+        decay, scale = factors(slot_ref, rate_ref, scale_ref, base)
+        scaled = value_ref[base : base + 8, :] * (1.0 / scale)
+        high = scaled.astype(BF16).astype(F32)
+        spread = jnp.concatenate(
+            [
+                jnp.concatenate([jnp.where(rows8 == u, term, 0.0) for u in range(8)], axis=1)
+                for term in (high, scaled - high)
+            ],
+            axis=0,
+        ).astype(BF16)
+        columns = jnp.concatenate([key_ref[base : base + 8, :]] * 2, axis=0).T.astype(BF16)
+        outer = jnp.dot(columns, spread, preferred_element_type=F32)
+        for u in range(8):
+            fresh[base - first + u] = (
+                decay[u : u + 1, :] * cache_ref[base + u].astype(F32)
+                + outer[:, u * 128 : (u + 1) * 128]
+            ).astype(BF16)
+        backs.append(
+            pltpu.make_async_copy(
+                fresh.at[pl.ds(base - first, 8)],
+                out_ref.at[pl.ds(base, 8)],
+                sems.at[(base - first) // 8],
+            )
+        )
+        backs[-1].start()
+    for back in backs:
+        back.wait()
+
+
+def update_tiles(cache, key_rows, values, slot, rate, scale, first, count, begun):
+    return pl.pallas_call(
+        functools.partial(update_kernel, first, count),
+        out_shape=jax.ShapeDtypeStruct(cache.shape, BF16),
+        in_specs=[SMEM] * 3 + [VMEM] * 3 + [ANY] * len(begun),
+        out_specs=ANY,
+        scratch_shapes=[
+            pltpu.VMEM((count, 128, 128), BF16),
+            pltpu.SemaphoreType.DMA((count // 8,)),
+        ],
+        input_output_aliases={6: 0} if begun else {},
+        compiler_params=pltpu.CompilerParams(vmem_limit_bytes=grant(cache, cache)),
+        cost_estimate=pl.CostEstimate(
+            flops=0, bytes_accessed=4 * count * 128 * 128, transcendentals=0
+        ),
+        name="update",
+    )(slot, rate, scale, cache, key_rows, values, *begun)
 
 
 def finish_kernel(devices, per, *refs):
@@ -399,10 +431,25 @@
         tokens_all, w_proj, jnp.transpose(send_slot, (2, 0, 1)), heads, slots
     )
     act_all = gather_pieces(act, devices)
-    read, gates, new_cache = advance_tiles(
+    read, gates, key_rows, values = read_states(
         act_all, cache_tiles, slot, decay_rate, tile_scales, capacity
     )
-    read_all = gather_pieces(read, devices)
+    half = slots // 16 * 8
+    update = functools.partial(
+        update_tiles, cache_tiles, key_rows, values, slot, decay_rate, tile_scales
+    )
+    bits = [1 << k for k in reversed(range(1, devices.bit_length() - 1))]
+    first = [cross(read, bit, devices) for bit in bits]
+    new_cache = update(0, half, [])
+    *first, new_cache = lax.optimization_barrier((*first, new_cache))
+    held = [read]
+    for own_piece, bit in zip(first, bits):
+        last = [cross(piece, bit, devices) for piece in held[1:]]
+        held = held + [own_piece] + last
+    new_cache = update(half, slots - half, [new_cache])
+    *last, new_cache = lax.optimization_barrier((*last, new_cache))
+    held = held[: len(held) - len(last)] + last
+    read_all = held + [cross(piece, 1, devices) for piece in held]
     mixed_out = finish(read_all, gates, pick, norm_gain.reshape(heads, 128), w_out)
     return (mixed_out, new_cache)
 

time: 69.8 us -> 66.2 us (0.948)
  waiting for transfers between devices: 23.1 us -> 14.1 us
  starting transfers between devices: 29.7 us -> 35 us
    ppermute x45, waiting for transfers between devices: 23.1 us -> 14.1 us  [cross(): return lax.ppermute(piece, 'batch', [(i, i ^ bit) for i in range(devices)])]
    ppermute x45, starting transfers between devices: 29.7 us -> 35 us  [cross(): return lax.ppermute(piece, 'batch', [(i, i ^ bit) for i in range(devices)])]
    pallas_call x1 -> x3, Pallas kernels: 7.64 us -> 7.69 us  [the longest x2 5.14 us: update_tiles(): pl.pallas_call(functools.partial(update_kernel, first, count), out_shape=...]
  transfers between devices with their start and end apart: 45 -> 45, of which waited for: 21 -> 19; matrix products, arithmetic and copies ran while one was open for 0% -> 0% of each run, Pallas kernels for 0% -> 8%
where the time goes in v4:
time: 66.2 us; the launch traced here: 66 us
  starting transfers between devices  35 us (53%)
  waiting for transfers between devices  14.1 us (21%)
  Pallas kernels  13.9 us (21%)
  local copies, waits for them, and re-layouts  2.19 us (3%)
  between operations  0.8 us (1%)
    ppermute x45, starting transfers between devices, cross(): return lax.ppermute(piece, 'batch', [(i, i ^ bit) for i in range(devices)])  35 us
    ppermute x45, waiting for transfers between devices, cross(): return lax.ppermute(piece, 'batch', [(i, i ^ bit) for i in range(devices)])  14.1 us
    pallas_call x2, Pallas kernels, update_tiles(): pl.pallas_call(functools.partial(update_kernel, first, count), out_shape=...  5.14 us
    pallas_call x1, Pallas kernels, finish(): pl.pallas_call(functools.partial(finish_kernel, devices, per), out_shape=...  3.66 us
    pallas_call x1, Pallas kernels, read_states(): pl.pallas_call(functools.partial(readout_kernel, devices), out_shape=(jax...  2.55 us
    pallas_call x1, Pallas kernels, project(): pl.pallas_call(functools.partial(project_kernel, devices, heads, slots, s...  2.49 us
    unnamed x20, local copies, waits for them, and re-layouts  2.19 us
  transfers between devices with their start and end apart: 45, of which 19 were waited for; matrix products, arithmetic and copies ran while one was open for 0% of the time, Pallas kernels for 8%

profile of v4, /device:TPU:0, one launch (start us, length us, event | category | flops | bytes accessed | tf_op | source)
XLA Modules:
  0.0 66.0 jit_solution(13495309326023660916)
XLA Ops:
  0.7 0.8 %copy-done.7 = bf16[3,6144]{1,0:T(4,128)(2,1)S(1)} copy-done((bf16[3,6144]{1,0:T(4,128)(2,1)S(1)}, bf16[3,6144]{1,0:T(4,128)(2,1)}, u32[]{:S(2)}) %copy-start.7) | copy-done | bytes 36888
  1.4 0.7 %copy-done.8 = s32[3,32]{1,0:T(4,128)S(1)} copy-done((s32[3,32]{1,0:T(4,128)S(1)}, s32[3,32]{1,0:T(4,128)}, u32[]{:S(2)}) %copy-start.8) | copy-done | bytes 408
  2.1 0.7 %copy-done.9 = s32[3,32]{1,0:T(4,128)S(1)} copy-done((s32[3,32]{1,0:T(4,128)S(1)}, s32[3,32]{1,0:T(4,128)}, u32[]{:S(2)}) %copy-start.9) | copy-done | bytes 408
  2.9 4.1 %collective-permute-start = (bf16[4,6144]{1,0:T(4,128)(2,1)S(1)}, bf16[4,6144]{1,0:T(4,128)(2,1)S(1)}, u32[]{:S(2)}, u32[]{:S(2)}) collective-permute-start(bf16[4,6144]{1,0:T(4,128)(2,1)S(1)} %pack.1.refs_2_), channel_id=1, source_target_pairs={{0,8},{1,9},{2,10},{3,11},{4,12},{5,13},{6,14},{7,15},{8,0},{9,1},... | collective-permute-start | bytes 147464 | tf_op jit(solution)/shard_map/ppermute | solution.py:39
  6.9 1.6 %collective-permute-start.1 = (bf16[4,6144]{1,0:T(4,128)(2,1)S(1)}, bf16[4,6144]{1,0:T(4,128)(2,1)S(1)}, u32[]{:S(2)}, u32[]{:S(2)}) collective-permute-start(bf16[4,6144]{1,0:T(4,128)(2,1)S(1)} %pack.1.refs_2_), channel_id=1, source_target_pairs={{0,4},{1,5},{2,6},{3,7},{4,0},{5,1},{6,2},{7,3},{8,12},{9,13},{10,... | collective-permute-start | bytes 147464 | tf_op jit(solution)/shard_map/ppermute | solution.py:39
  8.5 1.5 %collective-permute-start.3 = (bf16[4,6144]{1,0:T(4,128)(2,1)S(1)}, bf16[4,6144]{1,0:T(4,128)(2,1)S(1)}, u32[]{:S(2)}, u32[]{:S(2)}) collective-permute-start(bf16[4,6144]{1,0:T(4,128)(2,1)S(1)} %pack.1.refs_2_), channel_id=1, source_target_pairs={{0,2},{1,3},{2,0},{3,1},{4,6},{5,7},{6,4},{7,5},{8,10},{9,11},{10,... | collective-permute-start | bytes 147464 | tf_op jit(solution)/shard_map/ppermute | solution.py:39
  10.0 0.9 %collective-permute-start.2 = (bf16[4,6144]{1,0:T(4,128)(2,1)S(1)}, bf16[4,6144]{1,0:T(4,128)(2,1)S(1)}, u32[]{:S(2)}, u32[]{:S(2)}) collective-permute-start(bf16[4,6144]{1,0:T(4,128)(2,1)S(1)} %collective-permute-done.refs_3_), channel_id=1, source_target_pairs={{0,4},{1,5},{2,6},{3,7},{4,0},{5,1},{6,2},{7,3},{8,12},{9,13},{10,... | collective-permute-start | bytes 147464 | tf_op jit(solution)/shard_map/ppermute | solution.py:39
  10.9 1.5 %collective-permute-start.4 = (bf16[4,6144]{1,0:T(4,128)(2,1)S(1)}, bf16[4,6144]{1,0:T(4,128)(2,1)S(1)}, u32[]{:S(2)}, u32[]{:S(2)}) collective-permute-start(bf16[4,6144]{1,0:T(4,128)(2,1)S(1)} %collective-permute-done.refs_3_), channel_id=1, source_target_pairs={{0,2},{1,3},{2,0},{3,1},{4,6},{5,7},{6,4},{7,5},{8,10},{9,11},{10,... | collective-permute-start | bytes 147464 | tf_op jit(solution)/shard_map/ppermute | solution.py:39
  13.5 0.7 %collective-permute-done.2.refs_5_ = bf16[4,6144]{1,0:T(4,128)(2,1)S(1)} collective-permute-done((bf16[4,6144]{1,0:T(4,128)(2,1)S(1)}, bf16[4,6144]{1,0:T(4,128)(2,1)S(1)}, u32[]{:S(2)}, u32[]{:S(2)}) %collective-permute-start.2) | collective-permute-done | bytes 49184 | tf_op jit(solution)/shard_map/ppermute | solution.py:39
  14.2 1.3 %collective-permute-start.6 = (bf16[4,6144]{1,0:T(4,128)(2,1)S(1)}, bf16[4,6144]{1,0:T(4,128)(2,1)S(1)}, u32[]{:S(2)}, u32[]{:S(2)}) collective-permute-start(bf16[4,6144]{1,0:T(4,128)(2,1)S(1)} %collective-permute-done.2.refs_5_), channel_id=1, source_target_pairs={{0,2},{1,3},{2,0},{3,1},{4,6},{5,7},{6,4},{7,5},{8,10},{9,11},{10,... | collective-permute-start | bytes 147464 | tf_op jit(solution)/shard_map/ppermute | solution.py:39
  15.4 1.1 %collective-permute-done.5.refs_8_ = bf16[4,6144]{1,0:T(4,128)(2,1)S(1)} collective-permute-done((bf16[4,6144]{1,0:T(4,128)(2,1)S(1)}, bf16[4,6144]{1,0:T(4,128)(2,1)S(1)}, u32[]{:S(2)}, u32[]{:S(2)}) %collective-permute-start.5) | collective-permute-done | bytes 49184 | tf_op jit(solution)/shard_map/ppermute | solution.py:39
  17.2 1.1 %collective-permute-done.6.refs_9_ = bf16[4,6144]{1,0:T(4,128)(2,1)S(1)} collective-permute-done((bf16[4,6144]{1,0:T(4,128)(2,1)S(1)}, bf16[4,6144]{1,0:T(4,128)(2,1)S(1)}, u32[]{:S(2)}, u32[]{:S(2)}) %collective-permute-start.6) | collective-permute-done | bytes 49184 | tf_op jit(solution)/shard_map/ppermute | solution.py:39
  18.3 1.2 %collective-permute-done.14.refs_17_ = bf16[4,6144]{1,0:T(4,128)(2,1)S(1)} collective-permute-done((bf16[4,6144]{1,0:T(4,128)(2,1)S(1)}, bf16[4,6144]{1,0:T(4,128)(2,1)S(1)}, u32[]{:S(2)}, u32[]{:S(2)}) %collective-permute-start.14) | collective-permute-done | bytes 49184 | tf_op jit(solution)/shard_map/ppermute | solution.py:39
  19.5 2.5 %project.1 = (bf16[48,1024]{1,0:T(8,128)(2,1)S(1)}, s32[32,48]{1,0:T(8,128)S(1)}, s32[8,256]{1,0:T(8,128)S(1)}) custom-call(s32[12,1,16]{2,1,0:T(1,128)S(1)} %bitcast.3, bf16[6144,1024]{1,0:T(8,128)(2,1)S(1)} %copy-done.1, bf16[4,6144]{1,0:T(4,128)(2,1)S(1)} %pack.1.refs_2_, bf16[4,6144]{1,0:T(4,128)(2,1)S(1)} %collective-permute-done.refs_3_, ...), custom_call_target="tpu_custom_call" | custom-call | flops 603979776 | bytes 12582912 | tf_op jit(solution)/shard_map/project/pallas_call | solution.py:181
  22.0 2.4 %collective-permute-start.15 = (bf16[48,1024]{1,0:T(8,128)(2,1)S(1)}, bf16[48,1024]{1,0:T(8,128)(2,1)S(1)}, u32[]{:S(2)}, u32[]{:S(2)}) collective-permute-start(bf16[48,1024]{1,0:T(8,128)(2,1)S(1)} %get-tuple-element.19.refs_4_), channel_id=1, source_target_pairs={{0,8},{1,9},{2,10},{3,11},{4,12},{5,13},{6,14},{7,15},{8,0},{9,1},... | collective-permute-start | bytes 294920 | tf_op jit(solution)/shard_map/ppermute | solution.py:39
  24.4 1.5 %collective-permute-start.16 = (bf16[48,1024]{1,0:T(8,128)(2,1)S(1)}, bf16[48,1024]{1,0:T(8,128)(2,1)S(1)}, u32[]{:S(2)}, u32[]{:S(2)}) collective-permute-start(bf16[48,1024]{1,0:T(8,128)(2,1)S(1)} %get-tuple-element.19.refs_4_), channel_id=1, source_target_pairs={{0,4},{1,5},{2,6},{3,7},{4,0},{5,1},{6,2},{7,3},{8,12},{9,13},{10,... | collective-permute-start | bytes 294920 | tf_op jit(solution)/shard_map/ppermute | solution.py:39
  25.9 1.5 %collective-permute-start.18 = (bf16[48,1024]{1,0:T(8,128)(2,1)S(1)}, bf16[48,1024]{1,0:T(8,128)(2,1)S(1)}, u32[]{:S(2)}, u32[]{:S(2)}) collective-permute-start(bf16[48,1024]{1,0:T(8,128)(2,1)S(1)} %get-tuple-element.19.refs_4_), channel_id=1, source_target_pairs={{0,2},{1,3},{2,0},{3,1},{4,6},{5,7},{6,4},{7,5},{8,10},{9,11},{10,... | collective-permute-start | bytes 294920 | tf_op jit(solution)/shard_map/ppermute | solution.py:39
  27.4 2.6 %collective-permute-done.15.refs_5_ = bf16[48,1024]{1,0:T(8,128)(2,1)S(1)} collective-permute-done((bf16[48,1024]{1,0:T(8,128)(2,1)S(1)}, bf16[48,1024]{1,0:T(8,128)(2,1)S(1)}, u32[]{:S(2)}, u32[]{:S(2)}) %collective-permute-start.15) | collective-permute-done | bytes 98336 | tf_op jit(solution)/shard_map/ppermute | solution.py:39
  30.4 1.4 %collective-permute-start.19 = (bf16[48,1024]{1,0:T(8,128)(2,1)S(1)}, bf16[48,1024]{1,0:T(8,128)(2,1)S(1)}, u32[]{:S(2)}, u32[]{:S(2)}) collective-permute-start(bf16[48,1024]{1,0:T(8,128)(2,1)S(1)} %collective-permute-done.15.refs_5_), channel_id=1, source_target_pairs={{0,2},{1,3},{2,0},{3,1},{4,6},{5,7},{6,4},{7,5},{8,10},{9,11},{10,... | collective-permute-start | bytes 294920 | tf_op jit(solution)/shard_map/ppermute | solution.py:39
  33.0 1.7 %collective-permute-done.17.refs_7_ = bf16[48,1024]{1,0:T(8,128)(2,1)S(1)} collective-permute-done((bf16[48,1024]{1,0:T(8,128)(2,1)S(1)}, bf16[48,1024]{1,0:T(8,128)(2,1)S(1)}, u32[]{:S(2)}, u32[]{:S(2)}) %collective-permute-start.17) | collective-permute-done | bytes 98336 | tf_op jit(solution)/shard_map/ppermute | solution.py:39
  34.7 1.3 %collective-permute-start.21 = (bf16[48,1024]{1,0:T(8,128)(2,1)S(1)}, bf16[48,1024]{1,0:T(8,128)(2,1)S(1)}, u32[]{:S(2)}, u32[]{:S(2)}) collective-permute-start(bf16[48,1024]{1,0:T(8,128)(2,1)S(1)} %collective-permute-done.17.refs_7_), channel_id=1, source_target_pairs={{0,2},{1,3},{2,0},{3,1},{4,6},{5,7},{6,4},{7,5},{8,10},{9,11},{10,... | collective-permute-start | bytes 294920 | tf_op jit(solution)/shard_map/ppermute | solution.py:39
  36.1 2.0 %collective-permute-done.20.refs_10_ = bf16[48,1024]{1,0:T(8,128)(2,1)S(1)} collective-permute-done((bf16[48,1024]{1,0:T(8,128)(2,1)S(1)}, bf16[48,1024]{1,0:T(8,128)(2,1)S(1)}, u32[]{:S(2)}, u32[]{:S(2)}) %collective-permute-start.20) | collective-permute-done | bytes 98336 | tf_op jit(solution)/shard_map/ppermute | solution.py:39
  40.6 2.5 %readout.1 = (bf16[192,128]{1,0:T(8,128)(2,1)S(1)}, f32[6152,128]{1,0:T(8,128)S(1)}, f32[168,128]{1,0:T(8,128)S(1)}, f32[168,128]{1,0:T(8,128)S(1)}) custom-call(s32[8,256]{1,0:T(8,128)S(1)} %get-tuple-element.18.refs_0_, f32[32]{0:T(128)S(1)} %copy-done.6, f32[168]{0:T(256)S(1)} %copy-done.4, bf16[168,128,128]{2,1,0:T(8,128)(2,1)S(1)} %copy-done, ...), custom_call_target="tpu_custom_call" | custom-call | flops 5505024 | bytes 22020096 | tf_op jit(solution)/shard_map/readout/pallas_call | solution.py:263
  43.2 3.3 %collective-permute-start.30 = (bf16[192,128]{1,0:T(8,128)(2,1)S(1)}, bf16[192,128]{1,0:T(8,128)(2,1)S(1)}, u32[]{:S(2)}, u32[]{:S(2)}) collective-permute-start(bf16[192,128]{1,0:T(8,128)(2,1)S(1)} %get-tuple-element.21.refs_4_), channel_id=1, source_target_pairs={{0,8},{1,9},{2,10},{3,11},{4,12},{5,13},{6,14},{7,15},{8,0},{9,1},... | collective-permute-start | bytes 147464 | tf_op jit(solution)/shard_map/ppermute | solution.py:39
  47.0 1.5 %collective-permute-start.32 = (bf16[192,128]{1,0:T(8,128)(2,1)S(1)}, bf16[192,128]{1,0:T(8,128)(2,1)S(1)}, u32[]{:S(2)}, u32[]{:S(2)}) collective-permute-start(bf16[192,128]{1,0:T(8,128)(2,1)S(1)} %get-tuple-element.21.refs_4_), channel_id=1, source_target_pairs={{0,2},{1,3},{2,0},{3,1},{4,6},{5,7},{6,4},{7,5},{8,10},{9,11},{10,... | collective-permute-start | bytes 147464 | tf_op jit(solution)/shard_map/ppermute | solution.py:39
  48.5 2.5 %update.2.refs_6_ = bf16[168,128,128]{2,1,0:T(8,128)(2,1)} custom-call(s32[8,256]{1,0:T(8,128)S(1)} %get-tuple-element.18.refs_0_, f32[32]{0:T(128)S(1)} %copy-done.6, f32[168]{0:T(256)S(1)} %copy-done.4, bf16[168,128,128]{2,1,0:T(8,128)(2,1)S(1)} %copy-done, f32[168,128]{1,0:T(8,128)S(1)} %get-tuple-element.22.refs_4_, f32[168,128]{1,0:T(8,128)S(1)} %get-tuple-element.23.refs_5_), custom_call_target="tpu_custom_call" | custom-call | bytes 5242880 | tf_op jit(solution)/shard_map/update/pallas_call | solution.py:319
  51.1 1.5 %collective-permute-start.33 = (bf16[192,128]{1,0:T(8,128)(2,1)S(1)}, bf16[192,128]{1,0:T(8,128)(2,1)S(1)}, u32[]{:S(2)}, u32[]{:S(2)}) collective-permute-start(bf16[192,128]{1,0:T(8,128)(2,1)S(1)} %collective-permute-done.30.refs_5_), channel_id=1, source_target_pairs={{0,4},{1,5},{2,6},{3,7},{4,0},{5,1},{6,2},{7,3},{8,12},{9,13},{10,... | collective-permute-start | bytes 147464 | tf_op jit(solution)/shard_map/ppermute | solution.py:39
  52.6 1.3 %collective-permute-start.34 = (bf16[192,128]{1,0:T(8,128)(2,1)S(1)}, bf16[192,128]{1,0:T(8,128)(2,1)S(1)}, u32[]{:S(2)}, u32[]{:S(2)}) collective-permute-start(bf16[192,128]{1,0:T(8,128)(2,1)S(1)} %collective-permute-done.30.refs_5_), channel_id=1, source_target_pairs={{0,2},{1,3},{2,0},{3,1},{4,6},{5,7},{6,4},{7,5},{8,10},{9,11},{10,... | collective-permute-start | bytes 147464 | tf_op jit(solution)/shard_map/ppermute | solution.py:39
  53.9 0.7 %collective-permute-start.35 = (bf16[192,128]{1,0:T(8,128)(2,1)S(1)}, bf16[192,128]{1,0:T(8,128)(2,1)S(1)}, u32[]{:S(2)}, u32[]{:S(2)}) collective-permute-start(bf16[192,128]{1,0:T(8,128)(2,1)S(1)} %collective-permute-done.31.refs_6_), channel_id=1, source_target_pairs={{0,2},{1,3},{2,0},{3,1},{4,6},{5,7},{6,4},{7,5},{8,10},{9,11},{10,... | collective-permute-start | bytes 147464 | tf_op jit(solution)/shard_map/ppermute | solution.py:39
  55.2 1.4 %collective-permute-start.36 = (bf16[192,128]{1,0:T(8,128)(2,1)S(1)}, bf16[192,128]{1,0:T(8,128)(2,1)S(1)}, u32[]{:S(2)}, u32[]{:S(2)}) collective-permute-start(bf16[192,128]{1,0:T(8,128)(2,1)S(1)} %collective-permute-done.33.refs_7_), channel_id=1, source_target_pairs={{0,2},{1,3},{2,0},{3,1},{4,6},{5,7},{6,4},{7,5},{8,10},{9,11},{10,... | collective-permute-start | bytes 147464 | tf_op jit(solution)/shard_map/ppermute | solution.py:39
  57.2 2.6 %update.3 = bf16[168,128,128]{2,1,0:T(8,128)(2,1)} custom-call(s32[8,256]{1,0:T(8,128)S(1)} %get-tuple-element.18.refs_0_, f32[32]{0:T(128)S(1)} %copy-done.6, f32[168]{0:T(256)S(1)} %copy-done.4, bf16[168,128,128]{2,1,0:T(8,128)(2,1)S(1)} %copy-done, f32[168,128]{1,0:T(8,128)S(1)} %get-tuple-element.22.refs_4_, ...), custom_call_target="tpu_custom_call", output_to_operand_aliasing={{}: (6, {})} | custom-call | bytes 5767168 | tf_op jit(solution)/shard_map/update/pallas_call | solution.py:319
  62.3 3.7 %finish.1 = bf16[48,384]{1,0:T(8,128)(2,1)} custom-call(s32[32,48]{1,0:T(8,128)S(1)} %get-tuple-element.17.refs_0_, f32[6152,128]{1,0:T(8,128)S(1)} %get-tuple-element.20.refs_1_, f32[32,128]{1,0:T(8,128)S(1)} %bitcast.2, bf16[4096,384]{1,0:T(8,128)(2,1)S(1)} %copy-done.2, bf16[192,128]{1,0:T(8,128)(2,1)S(1)} %get-tuple-element.21.refs_4_, ...), custom_call_target="tpu_custom_call" | custom-call | flops 150994944 | bytes 3145728 | tf_op jit(solution)/shard_map/finish/pallas_call | solution.py:377
  (84 shorter events, 10.0 us)
Async XLA Ops:
  2.9 7.1 %collective-permute-start = (bf16[4,6144]{1,0:T(4,128)(2,1)S(1)}, bf16[4,6144]{1,0:T(4,128)(2,1)S(1)}, u32[]{:S(2)}, u32[]{:S(2)}) collective-permute-start(bf16[4,6144]{1,0:T(4,128)(2,1)S(1)} %pack.1.refs_2_), channel_id=1, source_target_pairs={{0,8},{1,9},{2,10},{3,11},{4,12},{5,13},{6,14},{7,15},{8,0},{9,1},... | collective-permute-start | bytes 147464 | tf_op jit(solution)/shard_map/ppermute | solution.py:39
  6.9 5.5 %collective-permute-start.1 = (bf16[4,6144]{1,0:T(4,128)(2,1)S(1)}, bf16[4,6144]{1,0:T(4,128)(2,1)S(1)}, u32[]{:S(2)}, u32[]{:S(2)}) collective-permute-start(bf16[4,6144]{1,0:T(4,128)(2,1)S(1)} %pack.1.refs_2_), channel_id=1, source_target_pairs={{0,4},{1,5},{2,6},{3,7},{4,0},{5,1},{6,2},{7,3},{8,12},{9,13},{10,... | collective-permute-start | bytes 147464 | tf_op jit(solution)/shard_map/ppermute | solution.py:39
  8.5 4.4 %collective-permute-start.3 = (bf16[4,6144]{1,0:T(4,128)(2,1)S(1)}, bf16[4,6144]{1,0:T(4,128)(2,1)S(1)}, u32[]{:S(2)}, u32[]{:S(2)}) collective-permute-start(bf16[4,6144]{1,0:T(4,128)(2,1)S(1)} %pack.1.refs_2_), channel_id=1, source_target_pairs={{0,2},{1,3},{2,0},{3,1},{4,6},{5,7},{6,4},{7,5},{8,10},{9,11},{10,... | collective-permute-start | bytes 147464 | tf_op jit(solution)/shard_map/ppermute | solution.py:39
  10.0 2.9 %collective-permute-start.7 = (bf16[4,6144]{1,0:T(4,128)(2,1)S(1)}, bf16[4,6144]{1,0:T(4,128)(2,1)S(1)}, u32[]{:S(2)}, u32[]{:S(2)}) collective-permute-start(bf16[4,6144]{1,0:T(4,128)(2,1)S(1)} %pack.1.refs_2_), channel_id=1, source_target_pairs={{0,1},{1,0},{2,3},{3,2},{4,5},{5,4},{6,7},{7,6},{8,9},{9,8},{10,11... | collective-permute-start | bytes 147464 | tf_op jit(solution)/shard_map/ppermute | solution.py:39
  10.0 4.2 %collective-permute-start.2 = (bf16[4,6144]{1,0:T(4,128)(2,1)S(1)}, bf16[4,6144]{1,0:T(4,128)(2,1)S(1)}, u32[]{:S(2)}, u32[]{:S(2)}) collective-permute-start(bf16[4,6144]{1,0:T(4,128)(2,1)S(1)} %collective-permute-done.refs_3_), channel_id=1, source_target_pairs={{0,4},{1,5},{2,6},{3,7},{4,0},{5,1},{6,2},{7,3},{8,12},{9,13},{10,... | collective-permute-start | bytes 147464 | tf_op jit(solution)/shard_map/ppermute | solution.py:39
  10.9 4.5 %collective-permute-start.4 = (bf16[4,6144]{1,0:T(4,128)(2,1)S(1)}, bf16[4,6144]{1,0:T(4,128)(2,1)S(1)}, u32[]{:S(2)}, u32[]{:S(2)}) collective-permute-start(bf16[4,6144]{1,0:T(4,128)(2,1)S(1)} %collective-permute-done.refs_3_), channel_id=1, source_target_pairs={{0,2},{1,3},{2,0},{3,1},{4,6},{5,7},{6,4},{7,5},{8,10},{9,11},{10,... | collective-permute-start | bytes 147464 | tf_op jit(solution)/shard_map/ppermute | solution.py:39
  12.4 4.2 %collective-permute-start.5 = (bf16[4,6144]{1,0:T(4,128)(2,1)S(1)}, bf16[4,6144]{1,0:T(4,128)(2,1)S(1)}, u32[]{:S(2)}, u32[]{:S(2)}) collective-permute-start(bf16[4,6144]{1,0:T(4,128)(2,1)S(1)} %collective-permute-done.1.refs_4_), channel_id=1, source_target_pairs={{0,2},{1,3},{2,0},{3,1},{4,6},{5,7},{6,4},{7,5},{8,10},{9,11},{10,... | collective-permute-start | bytes 147464 | tf_op jit(solution)/shard_map/ppermute | solution.py:39
  13.0 3.6 %collective-permute-start.8 = (bf16[4,6144]{1,0:T(4,128)(2,1)S(1)}, bf16[4,6144]{1,0:T(4,128)(2,1)S(1)}, u32[]{:S(2)}, u32[]{:S(2)}) collective-permute-start(bf16[4,6144]{1,0:T(4,128)(2,1)S(1)} %collective-permute-done.refs_3_), channel_id=1, source_target_pairs={{0,1},{1,0},{2,3},{3,2},{4,5},{5,4},{6,7},{7,6},{8,9},{9,8},{10,11... | collective-permute-start | bytes 147464 | tf_op jit(solution)/shard_map/ppermute | solution.py:39
  13.0 4.1 %collective-permute-start.9 = (bf16[4,6144]{1,0:T(4,128)(2,1)S(1)}, bf16[4,6144]{1,0:T(4,128)(2,1)S(1)}, u32[]{:S(2)}, u32[]{:S(2)}) collective-permute-start(bf16[4,6144]{1,0:T(4,128)(2,1)S(1)} %collective-permute-done.1.refs_4_), channel_id=1, source_target_pairs={{0,1},{1,0},{2,3},{3,2},{4,5},{5,4},{6,7},{7,6},{8,9},{9,8},{10,11... | collective-permute-start | bytes 147464 | tf_op jit(solution)/shard_map/ppermute | solution.py:39
  14.2 4.1 %collective-permute-start.6 = (bf16[4,6144]{1,0:T(4,128)(2,1)S(1)}, bf16[4,6144]{1,0:T(4,128)(2,1)S(1)}, u32[]{:S(2)}, u32[]{:S(2)}) collective-permute-start(bf16[4,6144]{1,0:T(4,128)(2,1)S(1)} %collective-permute-done.2.refs_5_), channel_id=1, source_target_pairs={{0,2},{1,3},{2,0},{3,1},{4,6},{5,7},{6,4},{7,5},{8,10},{9,11},{10,... | collective-permute-start | bytes 147464 | tf_op jit(solution)/shard_map/ppermute | solution.py:39
  15.4 2.8 %collective-permute-start.11 = (bf16[4,6144]{1,0:T(4,128)(2,1)S(1)}, bf16[4,6144]{1,0:T(4,128)(2,1)S(1)}, u32[]{:S(2)}, u32[]{:S(2)}) collective-permute-start(bf16[4,6144]{1,0:T(4,128)(2,1)S(1)} %collective-permute-done.3.refs_6_), channel_id=1, source_target_pairs={{0,1},{1,0},{2,3},{3,2},{4,5},{5,4},{6,7},{7,6},{8,9},{9,8},{10,11... | collective-permute-start | bytes 147464 | tf_op jit(solution)/shard_map/ppermute | solution.py:39
  22.0 8.0 %collective-permute-start.15 = (bf16[48,1024]{1,0:T(8,128)(2,1)S(1)}, bf16[48,1024]{1,0:T(8,128)(2,1)S(1)}, u32[]{:S(2)}, u32[]{:S(2)}) collective-permute-start(bf16[48,1024]{1,0:T(8,128)(2,1)S(1)} %get-tuple-element.19.refs_4_), channel_id=1, source_target_pairs={{0,8},{1,9},{2,10},{3,11},{4,12},{5,13},{6,14},{7,15},{8,0},{9,1},... | collective-permute-start | bytes 294920 | tf_op jit(solution)/shard_map/ppermute | solution.py:39
  24.4 7.4 %collective-permute-start.16 = (bf16[48,1024]{1,0:T(8,128)(2,1)S(1)}, bf16[48,1024]{1,0:T(8,128)(2,1)S(1)}, u32[]{:S(2)}, u32[]{:S(2)}) collective-permute-start(bf16[48,1024]{1,0:T(8,128)(2,1)S(1)} %get-tuple-element.19.refs_4_), channel_id=1, source_target_pairs={{0,4},{1,5},{2,6},{3,7},{4,0},{5,1},{6,2},{7,3},{8,12},{9,13},{10,... | collective-permute-start | bytes 294920 | tf_op jit(solution)/shard_map/ppermute | solution.py:39
  25.9 6.5 %collective-permute-start.18 = (bf16[48,1024]{1,0:T(8,128)(2,1)S(1)}, bf16[48,1024]{1,0:T(8,128)(2,1)S(1)}, u32[]{:S(2)}, u32[]{:S(2)}) collective-permute-start(bf16[48,1024]{1,0:T(8,128)(2,1)S(1)} %get-tuple-element.19.refs_4_), channel_id=1, source_target_pairs={{0,2},{1,3},{2,0},{3,1},{4,6},{5,7},{6,4},{7,5},{8,10},{9,11},{10,... | collective-permute-start | bytes 294920 | tf_op jit(solution)/shard_map/ppermute | solution.py:39
  27.4 5.0 %collective-permute-start.22 = (bf16[48,1024]{1,0:T(8,128)(2,1)S(1)}, bf16[48,1024]{1,0:T(8,128)(2,1)S(1)}, u32[]{:S(2)}, u32[]{:S(2)}) collective-permute-start(bf16[48,1024]{1,0:T(8,128)(2,1)S(1)} %get-tuple-element.19.refs_4_), channel_id=1, source_target_pairs={{0,1},{1,0},{2,3},{3,2},{4,5},{5,4},{6,7},{7,6},{8,9},{9,8},{10,11... | collective-permute-start | bytes 294920 | tf_op jit(solution)/shard_map/ppermute | solution.py:39
  30.1 4.6 %collective-permute-start.17 = (bf16[48,1024]{1,0:T(8,128)(2,1)S(1)}, bf16[48,1024]{1,0:T(8,128)(2,1)S(1)}, u32[]{:S(2)}, u32[]{:S(2)}) collective-permute-start(bf16[48,1024]{1,0:T(8,128)(2,1)S(1)} %collective-permute-done.15.refs_5_), channel_id=1, source_target_pairs={{0,4},{1,5},{2,6},{3,7},{4,0},{5,1},{6,2},{7,3},{8,12},{9,13},{10,... | collective-permute-start | bytes 294920 | tf_op jit(solution)/shard_map/ppermute | solution.py:39
  30.4 5.7 %collective-permute-start.19 = (bf16[48,1024]{1,0:T(8,128)(2,1)S(1)}, bf16[48,1024]{1,0:T(8,128)(2,1)S(1)}, u32[]{:S(2)}, u32[]{:S(2)}) collective-permute-start(bf16[48,1024]{1,0:T(8,128)(2,1)S(1)} %collective-permute-done.15.refs_5_), channel_id=1, source_target_pairs={{0,2},{1,3},{2,0},{3,1},{4,6},{5,7},{6,4},{7,5},{8,10},{9,11},{10,... | collective-permute-start | bytes 294920 | tf_op jit(solution)/shard_map/ppermute | solution.py:39
  31.8 6.3 %collective-permute-start.20 = (bf16[48,1024]{1,0:T(8,128)(2,1)S(1)}, bf16[48,1024]{1,0:T(8,128)(2,1)S(1)}, u32[]{:S(2)}, u32[]{:S(2)}) collective-permute-start(bf16[48,1024]{1,0:T(8,128)(2,1)S(1)} %collective-permute-done.16.refs_6_), channel_id=1, source_target_pairs={{0,2},{1,3},{2,0},{3,1},{4,6},{5,7},{6,4},{7,5},{8,10},{9,11},{10,... | collective-permute-start | bytes 294920 | tf_op jit(solution)/shard_map/ppermute | solution.py:39
  32.4 5.7 %collective-permute-start.23 = (bf16[48,1024]{1,0:T(8,128)(2,1)S(1)}, bf16[48,1024]{1,0:T(8,128)(2,1)S(1)}, u32[]{:S(2)}, u32[]{:S(2)}) collective-permute-start(bf16[48,1024]{1,0:T(8,128)(2,1)S(1)} %collective-permute-done.15.refs_5_), channel_id=1, source_target_pairs={{0,1},{1,0},{2,3},{3,2},{4,5},{5,4},{6,7},{7,6},{8,9},{9,8},{10,11... | collective-permute-start | bytes 294920 | tf_op jit(solution)/shard_map/ppermute | solution.py:39
  32.5 6.2 %collective-permute-start.24 = (bf16[48,1024]{1,0:T(8,128)(2,1)S(1)}, bf16[48,1024]{1,0:T(8,128)(2,1)S(1)}, u32[]{:S(2)}, u32[]{:S(2)}) collective-permute-start(bf16[48,1024]{1,0:T(8,128)(2,1)S(1)} %collective-permute-done.16.refs_6_), channel_id=1, source_target_pairs={{0,1},{1,0},{2,3},{3,2},{4,5},{5,4},{6,7},{7,6},{8,9},{9,8},{10,11... | collective-permute-start | bytes 294920 | tf_op jit(solution)/shard_map/ppermute | solution.py:39
  34.7 4.6 %collective-permute-start.21 = (bf16[48,1024]{1,0:T(8,128)(2,1)S(1)}, bf16[48,1024]{1,0:T(8,128)(2,1)S(1)}, u32[]{:S(2)}, u32[]{:S(2)}) collective-permute-start(bf16[48,1024]{1,0:T(8,128)(2,1)S(1)} %collective-permute-done.17.refs_7_), channel_id=1, source_target_pairs={{0,2},{1,3},{2,0},{3,1},{4,6},{5,7},{6,4},{7,5},{8,10},{9,11},{10,... | collective-permute-start | bytes 294920 | tf_op jit(solution)/shard_map/ppermute | solution.py:39
  36.1 3.2 %collective-permute-start.26 = (bf16[48,1024]{1,0:T(8,128)(2,1)S(1)}, bf16[48,1024]{1,0:T(8,128)(2,1)S(1)}, u32[]{:S(2)}, u32[]{:S(2)}) collective-permute-start(bf16[48,1024]{1,0:T(8,128)(2,1)S(1)} %collective-permute-done.18.refs_8_), channel_id=1, source_target_pairs={{0,1},{1,0},{2,3},{3,2},{4,5},{5,4},{6,7},{7,6},{8,9},{9,8},{10,11... | collective-permute-start | bytes 294920 | tf_op jit(solution)/shard_map/ppermute | solution.py:39
  43.2 7.9 %collective-permute-start.30 = (bf16[192,128]{1,0:T(8,128)(2,1)S(1)}, bf16[192,128]{1,0:T(8,128)(2,1)S(1)}, u32[]{:S(2)}, u32[]{:S(2)}) collective-permute-start(bf16[192,128]{1,0:T(8,128)(2,1)S(1)} %get-tuple-element.21.refs_4_), channel_id=1, source_target_pairs={{0,8},{1,9},{2,10},{3,11},{4,12},{5,13},{6,14},{7,15},{8,0},{9,1},... | collective-permute-start | bytes 147464 | tf_op jit(solution)/shard_map/ppermute | solution.py:39
  46.5 4.6 %collective-permute-start.31 = (bf16[192,128]{1,0:T(8,128)(2,1)S(1)}, bf16[192,128]{1,0:T(8,128)(2,1)S(1)}, u32[]{:S(2)}, u32[]{:S(2)}) collective-permute-start(bf16[192,128]{1,0:T(8,128)(2,1)S(1)} %get-tuple-element.21.refs_4_), channel_id=1, source_target_pairs={{0,4},{1,5},{2,6},{3,7},{4,0},{5,1},{6,2},{7,3},{8,12},{9,13},{10,... | collective-permute-start | bytes 147464 | tf_op jit(solution)/shard_map/ppermute | solution.py:39
  47.0 4.1 %collective-permute-start.32 = (bf16[192,128]{1,0:T(8,128)(2,1)S(1)}, bf16[192,128]{1,0:T(8,128)(2,1)S(1)}, u32[]{:S(2)}, u32[]{:S(2)}) collective-permute-start(bf16[192,128]{1,0:T(8,128)(2,1)S(1)} %get-tuple-element.21.refs_4_), channel_id=1, source_target_pairs={{0,2},{1,3},{2,0},{3,1},{4,6},{5,7},{6,4},{7,5},{8,10},{9,11},{10,... | collective-permute-start | bytes 147464 | tf_op jit(solution)/shard_map/ppermute | solution.py:39
  51.1 4.2 %collective-permute-start.33 = (bf16[192,128]{1,0:T(8,128)(2,1)S(1)}, bf16[192,128]{1,0:T(8,128)(2,1)S(1)}, u32[]{:S(2)}, u32[]{:S(2)}) collective-permute-start(bf16[192,128]{1,0:T(8,128)(2,1)S(1)} %collective-permute-done.30.refs_5_), channel_id=1, source_target_pairs={{0,4},{1,5},{2,6},{3,7},{4,0},{5,1},{6,2},{7,3},{8,12},{9,13},{10,... | collective-permute-start | bytes 147464 | tf_op jit(solution)/shard_map/ppermute | solution.py:39
  52.6 4.6 %collective-permute-start.34 = (bf16[192,128]{1,0:T(8,128)(2,1)S(1)}, bf16[192,128]{1,0:T(8,128)(2,1)S(1)}, u32[]{:S(2)}, u32[]{:S(2)}) collective-permute-start(bf16[192,128]{1,0:T(8,128)(2,1)S(1)} %collective-permute-done.30.refs_5_), channel_id=1, source_target_pairs={{0,2},{1,3},{2,0},{3,1},{4,6},{5,7},{6,4},{7,5},{8,10},{9,11},{10,... | collective-permute-start | bytes 147464 | tf_op jit(solution)/shard_map/ppermute | solution.py:39
  53.9 5.9 %collective-permute-start.35 = (bf16[192,128]{1,0:T(8,128)(2,1)S(1)}, bf16[192,128]{1,0:T(8,128)(2,1)S(1)}, u32[]{:S(2)}, u32[]{:S(2)}) collective-permute-start(bf16[192,128]{1,0:T(8,128)(2,1)S(1)} %collective-permute-done.31.refs_6_), channel_id=1, source_target_pairs={{0,2},{1,3},{2,0},{3,1},{4,6},{5,7},{6,4},{7,5},{8,10},{9,11},{10,... | collective-permute-start | bytes 147464 | tf_op jit(solution)/shard_map/ppermute | solution.py:39
  55.2 5.2 %collective-permute-start.36 = (bf16[192,128]{1,0:T(8,128)(2,1)S(1)}, bf16[192,128]{1,0:T(8,128)(2,1)S(1)}, u32[]{:S(2)}, u32[]{:S(2)}) collective-permute-start(bf16[192,128]{1,0:T(8,128)(2,1)S(1)} %collective-permute-done.33.refs_7_), channel_id=1, source_target_pairs={{0,2},{1,3},{2,0},{3,1},{4,6},{5,7},{6,4},{7,5},{8,10},{9,11},{10,... | collective-permute-start | bytes 147464 | tf_op jit(solution)/shard_map/ppermute | solution.py:39
  56.7 3.8 %collective-permute-start.37 = (bf16[192,128]{1,0:T(8,128)(2,1)S(1)}, bf16[192,128]{1,0:T(8,128)(2,1)S(1)}, u32[]{:S(2)}, u32[]{:S(2)}) collective-permute-start(bf16[192,128]{1,0:T(8,128)(2,1)S(1)} %get-tuple-element.21.refs_4_), channel_id=1, source_target_pairs={{0,1},{1,0},{2,3},{3,2},{4,5},{5,4},{6,7},{7,6},{8,9},{9,8},{10,11... | collective-permute-start | bytes 147464 | tf_op jit(solution)/shard_map/ppermute | solution.py:39
  56.7 4.2 %collective-permute-start.38 = (bf16[192,128]{1,0:T(8,128)(2,1)S(1)}, bf16[192,128]{1,0:T(8,128)(2,1)S(1)}, u32[]{:S(2)}, u32[]{:S(2)}) collective-permute-start(bf16[192,128]{1,0:T(8,128)(2,1)S(1)} %collective-permute-done.30.refs_5_), channel_id=1, source_target_pairs={{0,1},{1,0},{2,3},{3,2},{4,5},{5,4},{6,7},{7,6},{8,9},{9,8},{10,11... | collective-permute-start | bytes 147464 | tf_op jit(solution)/shard_map/ppermute | solution.py:39
  57.2 3.8 %collective-permute-start.39 = (bf16[192,128]{1,0:T(8,128)(2,1)S(1)}, bf16[192,128]{1,0:T(8,128)(2,1)S(1)}, u32[]{:S(2)}, u32[]{:S(2)}) collective-permute-start(bf16[192,128]{1,0:T(8,128)(2,1)S(1)} %collective-permute-done.31.refs_6_), channel_id=1, source_target_pairs={{0,1},{1,0},{2,3},{3,2},{4,5},{5,4},{6,7},{7,6},{8,9},{9,8},{10,11... | collective-permute-start | bytes 147464 | tf_op jit(solution)/shard_map/ppermute | solution.py:39
  (23 other events, 141.5 us)

commit v5 on v4

--- a/solution.py
+++ b/solution.py
@@ -39,8 +39,7 @@
     return lax.ppermute(piece, "batch", [(i, i ^ bit) for i in range(devices)])
 
 
-def gather_pieces(block, devices):
-    held, bit = [block], devices // 2
+def gather_pieces(held, bit, devices):
     while bit >= 1:
         held = held + [cross(piece, bit, devices) for piece in held]
         bit //= 2
@@ -60,30 +59,30 @@
     return stage[0][...]
 
 
-def pack_kernel(heads, tokens_ref, holder_ref, rank_ref, out_ref):
+def pack_kernel(tokens_ref, origin_ref, out_ref):
     own, width = tokens_ref.shape
+    heads = origin_ref.shape[1]
     parts = []
     for i in range(own):
-        parts.append(holder_ref[i : i + 1, :].astype(F32))
-        parts.append(rank_ref[i : i + 1, :].astype(F32))
-        parts.append(jnp.zeros((1, 128 - 2 * heads), F32))
+        parts.append(origin_ref[i : i + 1, :].astype(F32))
+        parts.append(jnp.zeros((1, 128 - heads), F32))
     parts.append(jnp.zeros((1, width - own * 128), F32))
     table = jnp.concatenate(parts, axis=1)
     block = jnp.concatenate([tokens_ref[...].astype(F32), table], axis=0)
     out_ref[...] = block.astype(BF16)
 
 
-def pack(tokens, holder, rank):
+def pack(tokens, origin):
     own, width = tokens.shape
     return pl.pallas_call(
-        functools.partial(pack_kernel, holder.shape[1]),
+        pack_kernel,
         out_shape=jax.ShapeDtypeStruct((own + 1, width), BF16),
-        in_specs=[VMEM] * 3,
+        in_specs=[VMEM] * 2,
         out_specs=VMEM,
         compiler_params=pltpu.CompilerParams(vmem_limit_bytes=grant(tokens)),
         cost_estimate=pl.CostEstimate(flops=20000000000, bytes_accessed=60000000, transcendentals=0),
         name="pack",
-    )(tokens, holder, rank)
+    )(tokens, origin)
 
 
 def project_kernel(devices, heads, slots, steps, *refs):
@@ -116,8 +115,9 @@
 
     table = jnp.concatenate(indices, axis=0)
     table = jnp.dot(table.T.astype(BF16), place_t, preferred_element_type=F32).astype(I32)
-    holder = table[:heads]
-    rank = table[heads : 2 * heads]
+    origin = table[:heads]
+    holder = (origin * (65536 // capacity + 1)) >> 16
+    rank = origin - holder * capacity
     owner = (lane * (65536 // own + 1)) >> 16
     pick_ref[...] = (place_of(holder ^ me, devices) * devices + owner) * capacity + rank
 
@@ -426,11 +426,14 @@
     capacity = send_slot.shape[-1]
     slots = cache_tiles.shape[0]
 
-    tokens_all = gather_pieces(pack(tokens, tile_holder, tile_rank), devices)
+    sent = pack(tokens, tile_holder * capacity + tile_rank)
+    high, low = devices // 2, devices // 4
+    direct = [cross(sent, bit, devices) for bit in (high, low, high ^ low)]
+    tokens_all = gather_pieces([sent] + direct, devices // 8, devices)
     act, pick, slot = project(
         tokens_all, w_proj, jnp.transpose(send_slot, (2, 0, 1)), heads, slots
     )
-    act_all = gather_pieces(act, devices)
+    act_all = gather_pieces([act], devices // 2, devices)
     read, gates, key_rows, values = read_states(
         act_all, cache_tiles, slot, decay_rate, tile_scales, capacity
     )
@@ -438,18 +441,21 @@
     update = functools.partial(
         update_tiles, cache_tiles, key_rows, values, slot, decay_rate, tile_scales
     )
-    bits = [1 << k for k in reversed(range(1, devices.bit_length() - 1))]
-    first = [cross(read, bit, devices) for bit in bits]
+    high, low = devices // 2, devices // 4
+    bits = [1 << k for k in reversed(range(1, devices.bit_length() - 3))]
+    first = [cross(read, bit, devices) for bit in (high, low, high ^ low, *bits)]
     new_cache = update(0, half, [])
     *first, new_cache = lax.optimization_barrier((*first, new_cache))
-    held = [read]
-    for own_piece, bit in zip(first, bits):
+    held = [read] + first[:3]
+    for own_piece, bit in zip(first[3:], bits):
         last = [cross(piece, bit, devices) for piece in held[1:]]
         held = held + [own_piece] + last
+    early = [cross(piece, 1, devices) for piece in held[: len(held) - len(last)]]
+    *early, new_cache = lax.optimization_barrier((*early, new_cache))
     new_cache = update(half, slots - half, [new_cache])
     *last, new_cache = lax.optimization_barrier((*last, new_cache))
     held = held[: len(held) - len(last)] + last
-    read_all = held + [cross(piece, 1, devices) for piece in held]
+    read_all = held + early + [cross(piece, 1, devices) for piece in last]
     mixed_out = finish(read_all, gates, pick, norm_gain.reshape(heads, 128), w_out)
     return (mixed_out, new_cache)
 

time: 66.2 us -> 64.5 us (0.974)
  starting transfers between devices: 35 us -> 32.5 us
  waiting for transfers between devices: 14.1 us -> 15.3 us
  local copies, waits for them, and re-layouts: 2.19 us -> 1.04 us
  other arithmetic: 0 us -> 0.85 us
    ppermute x45, starting transfers between devices: 35 us -> 32.5 us  [cross(): return lax.ppermute(piece, 'batch', [(i, i ^ bit) for i in range(devices)])]
    ppermute x45, waiting for transfers between devices: 14.1 us -> 15.3 us  [cross(): return lax.ppermute(piece, 'batch', [(i, i ^ bit) for i in range(devices)])]
    unnamed x20, local copies, waits for them, and re-layouts: 2.19 us -> 1.04 us
    add x0 -> x1, other arithmetic: none -> 0.85 us  [on_device(): sent = pack(tokens, tile_holder * capacity + tile_rank)]
  transfers between devices with their start and end apart: 45 -> 45, of which waited for: 19 -> 14; matrix products, arithmetic and copies ran while one was open for 0% -> 0% of each run, Pallas kernels for 8% -> 8%
where the time goes in v5:
time: 64.5 us; the launch traced here: 64.3 us
  starting transfers between devices  32.5 us (50%)
  waiting for transfers between devices  15.3 us (24%)
  Pallas kernels  13.9 us (22%)
  local copies, waits for them, and re-layouts  1.04 us (2%)
  other arithmetic  0.85 us (1%)
  between operations  0.84 us (1%)
    ppermute x45, starting transfers between devices, cross(): return lax.ppermute(piece, 'batch', [(i, i ^ bit) for i in range(devices)])  32.5 us
    ppermute x45, waiting for transfers between devices, cross(): return lax.ppermute(piece, 'batch', [(i, i ^ bit) for i in range(devices)])  15.3 us
    pallas_call x2, Pallas kernels, update_tiles(): pl.pallas_call(functools.partial(update_kernel, first, count), out_shape=...  5.14 us
    pallas_call x1, Pallas kernels, finish(): pl.pallas_call(functools.partial(finish_kernel, devices, per), out_shape=...  3.66 us
    pallas_call x1, Pallas kernels, read_states(): pl.pallas_call(functools.partial(readout_kernel, devices), out_shape=(jax...  2.55 us
    pallas_call x1, Pallas kernels, project(): pl.pallas_call(functools.partial(project_kernel, devices, heads, slots, s...  2.49 us
  transfers between devices with their start and end apart: 45, of which 14 were waited for; matrix products, arithmetic and copies ran while one was open for 0% of the time, Pallas kernels for 8%

profile of v5, /device:TPU:0, one launch (start us, length us, event | category | flops | bytes accessed | tf_op | source)
XLA Modules:
  0.0 64.3 jit_solution(1286306005814771930)
XLA Ops:
  0.6 0.9 %multiply_add_fusion.origin_ref = s32[3,32]{1,0:T(4,128)S(1)} fusion(s32[3,32]{1,0:T(4,128)} %param.18, s32[3,32]{1,0:T(4,128)} %param.17), kind=kLoop, calls=%fused_computation | loop fusion | flops 192 | bytes 1152 | tf_op jit(solution)/shard_map/add | solution.py:429
  1.5 1.0 %copy-done.6 = bf16[3,6144]{1,0:T(4,128)(2,1)S(1)} copy-done((bf16[3,6144]{1,0:T(4,128)(2,1)S(1)}, bf16[3,6144]{1,0:T(4,128)(2,1)}, u32[]{:S(2)}) %copy-start.6) | copy-done | bytes 36888
  2.5 4.1 %collective-permute-start = (bf16[4,6144]{1,0:T(4,128)(2,1)S(1)}, bf16[4,6144]{1,0:T(4,128)(2,1)S(1)}, u32[]{:S(2)}, u32[]{:S(2)}) collective-permute-start(bf16[4,6144]{1,0:T(4,128)(2,1)S(1)} %pack.1.refs_2_), channel_id=1, source_target_pairs={{0,8},{1,9},{2,10},{3,11},{4,12},{5,13},{6,14},{7,15},{8,0},{9,1},... | collective-permute-start | bytes 147464 | tf_op jit(solution)/shard_map/ppermute | solution.py:39
  6.6 1.6 %collective-permute-start.1 = (bf16[4,6144]{1,0:T(4,128)(2,1)S(1)}, bf16[4,6144]{1,0:T(4,128)(2,1)S(1)}, u32[]{:S(2)}, u32[]{:S(2)}) collective-permute-start(bf16[4,6144]{1,0:T(4,128)(2,1)S(1)} %pack.1.refs_2_), channel_id=1, source_target_pairs={{0,4},{1,5},{2,6},{3,7},{4,0},{5,1},{6,2},{7,3},{8,12},{9,13},{10,... | collective-permute-start | bytes 147464 | tf_op jit(solution)/shard_map/ppermute | solution.py:39
  8.2 1.7 %collective-permute-start.3 = (bf16[4,6144]{1,0:T(4,128)(2,1)S(1)}, bf16[4,6144]{1,0:T(4,128)(2,1)S(1)}, u32[]{:S(2)}, u32[]{:S(2)}) collective-permute-start(bf16[4,6144]{1,0:T(4,128)(2,1)S(1)} %pack.1.refs_2_), channel_id=1, source_target_pairs={{0,2},{1,3},{2,0},{3,1},{4,6},{5,7},{6,4},{7,5},{8,10},{9,11},{10,... | collective-permute-start | bytes 147464 | tf_op jit(solution)/shard_map/ppermute | solution.py:39
  9.9 1.1 %collective-permute-start.4 = (bf16[4,6144]{1,0:T(4,128)(2,1)S(1)}, bf16[4,6144]{1,0:T(4,128)(2,1)S(1)}, u32[]{:S(2)}, u32[]{:S(2)}) collective-permute-start(bf16[4,6144]{1,0:T(4,128)(2,1)S(1)} %collective-permute-done.refs_3_), channel_id=1, source_target_pairs={{0,2},{1,3},{2,0},{3,1},{4,6},{5,7},{6,4},{7,5},{8,10},{9,11},{10,... | collective-permute-start | bytes 147464 | tf_op jit(solution)/shard_map/ppermute | solution.py:39
  11.0 1.2 %collective-permute-start.5 = (bf16[4,6144]{1,0:T(4,128)(2,1)S(1)}, bf16[4,6144]{1,0:T(4,128)(2,1)S(1)}, u32[]{:S(2)}, u32[]{:S(2)}) collective-permute-start(bf16[4,6144]{1,0:T(4,128)(2,1)S(1)} %collective-permute-done.1.refs_4_), channel_id=1, source_target_pairs={{0,2},{1,3},{2,0},{3,1},{4,6},{5,7},{6,4},{7,5},{8,10},{9,11},{10,... | collective-permute-start | bytes 147464 | tf_op jit(solution)/shard_map/ppermute | solution.py:39
  12.2 1.9 %collective-permute-done.2.refs_5_ = bf16[4,6144]{1,0:T(4,128)(2,1)S(1)} collective-permute-done((bf16[4,6144]{1,0:T(4,128)(2,1)S(1)}, bf16[4,6144]{1,0:T(4,128)(2,1)S(1)}, u32[]{:S(2)}, u32[]{:S(2)}) %collective-permute-start.2) | collective-permute-done | bytes 49184 | tf_op jit(solution)/shard_map/ppermute | solution.py:39
  14.1 1.5 %collective-permute-start.6 = (bf16[4,6144]{1,0:T(4,128)(2,1)S(1)}, bf16[4,6144]{1,0:T(4,128)(2,1)S(1)}, u32[]{:S(2)}, u32[]{:S(2)}) collective-permute-start(bf16[4,6144]{1,0:T(4,128)(2,1)S(1)} %collective-permute-done.2.refs_5_), channel_id=1, source_target_pairs={{0,2},{1,3},{2,0},{3,1},{4,6},{5,7},{6,4},{7,5},{8,10},{9,11},{10,... | collective-permute-start | bytes 147464 | tf_op jit(solution)/shard_map/ppermute | solution.py:39
  16.6 1.6 %collective-permute-done.6.refs_9_ = bf16[4,6144]{1,0:T(4,128)(2,1)S(1)} collective-permute-done((bf16[4,6144]{1,0:T(4,128)(2,1)S(1)}, bf16[4,6144]{1,0:T(4,128)(2,1)S(1)}, u32[]{:S(2)}, u32[]{:S(2)}) %collective-permute-start.6) | collective-permute-done | bytes 49184 | tf_op jit(solution)/shard_map/ppermute | solution.py:39
  18.8 0.6 collective-permute-done.12.refs_15_
  20.0 2.5 %project.1 = (bf16[48,1024]{1,0:T(8,128)(2,1)S(1)}, s32[32,48]{1,0:T(8,128)S(1)}, s32[8,256]{1,0:T(8,128)S(1)}) custom-call(s32[12,1,16]{2,1,0:T(1,128)S(1)} %bitcast.5, bf16[6144,1024]{1,0:T(8,128)(2,1)S(1)} %bitcast.3, bf16[4,6144]{1,0:T(4,128)(2,1)S(1)} %pack.1.refs_2_, bf16[4,6144]{1,0:T(4,128)(2,1)S(1)} %collective-permute-done.refs_3_, ...), custom_call_target="tpu_custom_call" | custom-call | flops 603979776 | bytes 12582912 | tf_op jit(solution)/shard_map/project/pallas_call | solution.py:181
  22.6 2.4 %collective-permute-start.16 = (bf16[48,1024]{1,0:T(8,128)(2,1)S(1)}, bf16[48,1024]{1,0:T(8,128)(2,1)S(1)}, u32[]{:S(2)}, u32[]{:S(2)}) collective-permute-start(bf16[48,1024]{1,0:T(8,128)(2,1)S(1)} %get-tuple-element.26.refs_4_), channel_id=1, source_target_pairs={{0,4},{1,5},{2,6},{3,7},{4,0},{5,1},{6,2},{7,3},{8,12},{9,13},{10,... | collective-permute-start | bytes 294920 | tf_op jit(solution)/shard_map/ppermute | solution.py:39
  25.1 1.5 %collective-permute-start.18 = (bf16[48,1024]{1,0:T(8,128)(2,1)S(1)}, bf16[48,1024]{1,0:T(8,128)(2,1)S(1)}, u32[]{:S(2)}, u32[]{:S(2)}) collective-permute-start(bf16[48,1024]{1,0:T(8,128)(2,1)S(1)} %get-tuple-element.26.refs_4_), channel_id=1, source_target_pairs={{0,2},{1,3},{2,0},{3,1},{4,6},{5,7},{6,4},{7,5},{8,10},{9,11},{10,... | collective-permute-start | bytes 294920 | tf_op jit(solution)/shard_map/ppermute | solution.py:39
  26.6 3.3 %collective-permute-done.15.refs_5_ = bf16[48,1024]{1,0:T(8,128)(2,1)S(1)} collective-permute-done((bf16[48,1024]{1,0:T(8,128)(2,1)S(1)}, bf16[48,1024]{1,0:T(8,128)(2,1)S(1)}, u32[]{:S(2)}, u32[]{:S(2)}) %collective-permute-start.15) | collective-permute-done | bytes 98336 | tf_op jit(solution)/shard_map/ppermute | solution.py:39
  29.8 1.5 %collective-permute-start.19 = (bf16[48,1024]{1,0:T(8,128)(2,1)S(1)}, bf16[48,1024]{1,0:T(8,128)(2,1)S(1)}, u32[]{:S(2)}, u32[]{:S(2)}) collective-permute-start(bf16[48,1024]{1,0:T(8,128)(2,1)S(1)} %collective-permute-done.15.refs_5_), channel_id=1, source_target_pairs={{0,2},{1,3},{2,0},{3,1},{4,6},{5,7},{6,4},{7,5},{8,10},{9,11},{10,... | collective-permute-start | bytes 294920 | tf_op jit(solution)/shard_map/ppermute | solution.py:39
  32.4 2.1 %collective-permute-done.17.refs_7_ = bf16[48,1024]{1,0:T(8,128)(2,1)S(1)} collective-permute-done((bf16[48,1024]{1,0:T(8,128)(2,1)S(1)}, bf16[48,1024]{1,0:T(8,128)(2,1)S(1)}, u32[]{:S(2)}, u32[]{:S(2)}) %collective-permute-start.17) | collective-permute-done | bytes 98336 | tf_op jit(solution)/shard_map/ppermute | solution.py:39
  34.5 1.5 %collective-permute-start.21 = (bf16[48,1024]{1,0:T(8,128)(2,1)S(1)}, bf16[48,1024]{1,0:T(8,128)(2,1)S(1)}, u32[]{:S(2)}, u32[]{:S(2)}) collective-permute-start(bf16[48,1024]{1,0:T(8,128)(2,1)S(1)} %collective-permute-done.17.refs_7_), channel_id=1, source_target_pairs={{0,2},{1,3},{2,0},{3,1},{4,6},{5,7},{6,4},{7,5},{8,10},{9,11},{10,... | collective-permute-start | bytes 294920 | tf_op jit(solution)/shard_map/ppermute | solution.py:39
  36.0 0.9 %collective-permute-done.20.refs_10_ = bf16[48,1024]{1,0:T(8,128)(2,1)S(1)} collective-permute-done((bf16[48,1024]{1,0:T(8,128)(2,1)S(1)}, bf16[48,1024]{1,0:T(8,128)(2,1)S(1)}, u32[]{:S(2)}, u32[]{:S(2)}) %collective-permute-start.20) | collective-permute-done | bytes 98336 | tf_op jit(solution)/shard_map/ppermute | solution.py:39
  37.5 1.6 %collective-permute-done.21.refs_11_ = bf16[48,1024]{1,0:T(8,128)(2,1)S(1)} collective-permute-done((bf16[48,1024]{1,0:T(8,128)(2,1)S(1)}, bf16[48,1024]{1,0:T(8,128)(2,1)S(1)}, u32[]{:S(2)}, u32[]{:S(2)}) %collective-permute-start.21) | collective-permute-done | bytes 98336 | tf_op jit(solution)/shard_map/ppermute | solution.py:39
  39.2 1.3 %collective-permute-done.29.refs_19_ = bf16[48,1024]{1,0:T(8,128)(2,1)S(1)} collective-permute-done((bf16[48,1024]{1,0:T(8,128)(2,1)S(1)}, bf16[48,1024]{1,0:T(8,128)(2,1)S(1)}, u32[]{:S(2)}, u32[]{:S(2)}) %collective-permute-start.29) | collective-permute-done | bytes 98336 | tf_op jit(solution)/shard_map/ppermute | solution.py:39
  40.4 2.5 %readout.1 = (bf16[192,128]{1,0:T(8,128)(2,1)S(1)}, f32[6152,128]{1,0:T(8,128)S(1)}, f32[168,128]{1,0:T(8,128)S(1)}, f32[168,128]{1,0:T(8,128)S(1)}) custom-call(s32[8,256]{1,0:T(8,128)S(1)} %get-tuple-element.25.refs_0_, f32[32]{0:T(128)S(1)} %copy-done.5, f32[168]{0:T(256)S(1)} %copy-done.3, bf16[168,128,128]{2,1,0:T(8,128)(2,1)S(1)} %copy-done, ...), custom_call_target="tpu_custom_call" | custom-call | flops 5505024 | bytes 22020096 | tf_op jit(solution)/shard_map/readout/pallas_call | solution.py:263
  43.0 2.0 %collective-permute-start.30 = (bf16[192,128]{1,0:T(8,128)(2,1)S(1)}, bf16[192,128]{1,0:T(8,128)(2,1)S(1)}, u32[]{:S(2)}, u32[]{:S(2)}) collective-permute-start(bf16[192,128]{1,0:T(8,128)(2,1)S(1)} %get-tuple-element.28.refs_4_), channel_id=1, source_target_pairs={{0,8},{1,9},{2,10},{3,11},{4,12},{5,13},{6,14},{7,15},{8,0},{9,1},... | collective-permute-start | bytes 147464 | tf_op jit(solution)/shard_map/ppermute | solution.py:39
  45.5 2.0 %collective-permute-start.32 = (bf16[192,128]{1,0:T(8,128)(2,1)S(1)}, bf16[192,128]{1,0:T(8,128)(2,1)S(1)}, u32[]{:S(2)}, u32[]{:S(2)}) collective-permute-start(bf16[192,128]{1,0:T(8,128)(2,1)S(1)} %get-tuple-element.28.refs_4_), channel_id=1, source_target_pairs={{0,12},{1,13},{2,14},{3,15},{4,8},{5,9},{6,10},{7,11},{8,4},{9,5},... | collective-permute-start | bytes 147464 | tf_op jit(solution)/shard_map/ppermute | solution.py:39
  47.4 1.5 %collective-permute-start.33 = (bf16[192,128]{1,0:T(8,128)(2,1)S(1)}, bf16[192,128]{1,0:T(8,128)(2,1)S(1)}, u32[]{:S(2)}, u32[]{:S(2)}) collective-permute-start(bf16[192,128]{1,0:T(8,128)(2,1)S(1)} %get-tuple-element.28.refs_4_), channel_id=1, source_target_pairs={{0,2},{1,3},{2,0},{3,1},{4,6},{5,7},{6,4},{7,5},{8,10},{9,11},{10,... | collective-permute-start | bytes 147464 | tf_op jit(solution)/shard_map/ppermute | solution.py:39
  48.9 2.5 %update.2.refs_6_ = bf16[168,128,128]{2,1,0:T(8,128)(2,1)} custom-call(s32[8,256]{1,0:T(8,128)S(1)} %get-tuple-element.25.refs_0_, f32[32]{0:T(128)S(1)} %copy-done.5, f32[168]{0:T(256)S(1)} %copy-done.3, bf16[168,128,128]{2,1,0:T(8,128)(2,1)S(1)} %copy-done, f32[168,128]{1,0:T(8,128)S(1)} %get-tuple-element.29.refs_4_, f32[168,128]{1,0:T(8,128)S(1)} %get-tuple-element.30.refs_5_), custom_call_target="tpu_custom_call" | custom-call | bytes 5242880 | tf_op jit(solution)/shard_map/update/pallas_call | solution.py:319
  52.7 1.4 %collective-permute-start.34 = (bf16[192,128]{1,0:T(8,128)(2,1)S(1)}, bf16[192,128]{1,0:T(8,128)(2,1)S(1)}, u32[]{:S(2)}, u32[]{:S(2)}) collective-permute-start(bf16[192,128]{1,0:T(8,128)(2,1)S(1)} %collective-permute-done.30.refs_5_), channel_id=1, source_target_pairs={{0,2},{1,3},{2,0},{3,1},{4,6},{5,7},{6,4},{7,5},{8,10},{9,11},{10,... | collective-permute-start | bytes 147464 | tf_op jit(solution)/shard_map/ppermute | solution.py:39
  54.1 0.7 %collective-permute-start.35 = (bf16[192,128]{1,0:T(8,128)(2,1)S(1)}, bf16[192,128]{1,0:T(8,128)(2,1)S(1)}, u32[]{:S(2)}, u32[]{:S(2)}) collective-permute-start(bf16[192,128]{1,0:T(8,128)(2,1)S(1)} %collective-permute-done.31.refs_6_), channel_id=1, source_target_pairs={{0,2},{1,3},{2,0},{3,1},{4,6},{5,7},{6,4},{7,5},{8,10},{9,11},{10,... | collective-permute-start | bytes 147464 | tf_op jit(solution)/shard_map/ppermute | solution.py:39
  54.7 1.4 %collective-permute-start.36 = (bf16[192,128]{1,0:T(8,128)(2,1)S(1)}, bf16[192,128]{1,0:T(8,128)(2,1)S(1)}, u32[]{:S(2)}, u32[]{:S(2)}) collective-permute-start(bf16[192,128]{1,0:T(8,128)(2,1)S(1)} %collective-permute-done.32.refs_7_), channel_id=1, source_target_pairs={{0,2},{1,3},{2,0},{3,1},{4,6},{5,7},{6,4},{7,5},{8,10},{9,11},{10,... | collective-permute-start | bytes 147464 | tf_op jit(solution)/shard_map/ppermute | solution.py:39
  56.1 2.6 %update.3 = bf16[168,128,128]{2,1,0:T(8,128)(2,1)} custom-call(s32[8,256]{1,0:T(8,128)S(1)} %get-tuple-element.25.refs_0_, f32[32]{0:T(128)S(1)} %copy-done.5, f32[168]{0:T(256)S(1)} %copy-done.3, bf16[168,128,128]{2,1,0:T(8,128)(2,1)S(1)} %copy-done, f32[168,128]{1,0:T(8,128)S(1)} %get-tuple-element.29.refs_4_, ...), custom_call_target="tpu_custom_call", output_to_operand_aliasing={{}: (6, {})} | custom-call | bytes 5767168 | tf_op jit(solution)/shard_map/update/pallas_call | solution.py:319
  59.4 0.7 %collective-permute-done.42.refs_17_ = bf16[192,128]{1,0:T(8,128)(2,1)S(1)} collective-permute-done((bf16[192,128]{1,0:T(8,128)(2,1)S(1)}, bf16[192,128]{1,0:T(8,128)(2,1)S(1)}, u32[]{:S(2)}, u32[]{:S(2)}) %collective-permute-start.42) | collective-permute-done | bytes 49184 | tf_op jit(solution)/shard_map/ppermute | solution.py:39
  60.6 3.7 %finish.1 = bf16[48,384]{1,0:T(8,128)(2,1)} custom-call(s32[32,48]{1,0:T(8,128)S(1)} %get-tuple-element.24.refs_0_, f32[6152,128]{1,0:T(8,128)S(1)} %get-tuple-element.27.refs_1_, f32[32,128]{1,0:T(8,128)S(1)} %bitcast.4, bf16[4096,384]{1,0:T(8,128)(2,1)S(1)} %copy-done.1, bf16[192,128]{1,0:T(8,128)(2,1)S(1)} %get-tuple-element.28.refs_4_, ...), custom_call_target="tpu_custom_call" | custom-call | flops 150994944 | bytes 3145728 | tf_op jit(solution)/shard_map/finish/pallas_call | solution.py:377
  (86 shorter events, 6.9 us)
Async XLA Ops:
  2.5 7.4 %collective-permute-start = (bf16[4,6144]{1,0:T(4,128)(2,1)S(1)}, bf16[4,6144]{1,0:T(4,128)(2,1)S(1)}, u32[]{:S(2)}, u32[]{:S(2)}) collective-permute-start(bf16[4,6144]{1,0:T(4,128)(2,1)S(1)} %pack.1.refs_2_), channel_id=1, source_target_pairs={{0,8},{1,9},{2,10},{3,11},{4,12},{5,13},{6,14},{7,15},{8,0},{9,1},... | collective-permute-start | bytes 147464 | tf_op jit(solution)/shard_map/ppermute | solution.py:39
  6.6 4.4 %collective-permute-start.1 = (bf16[4,6144]{1,0:T(4,128)(2,1)S(1)}, bf16[4,6144]{1,0:T(4,128)(2,1)S(1)}, u32[]{:S(2)}, u32[]{:S(2)}) collective-permute-start(bf16[4,6144]{1,0:T(4,128)(2,1)S(1)} %pack.1.refs_2_), channel_id=1, source_target_pairs={{0,4},{1,5},{2,6},{3,7},{4,0},{5,1},{6,2},{7,3},{8,12},{9,13},{10,... | collective-permute-start | bytes 147464 | tf_op jit(solution)/shard_map/ppermute | solution.py:39
  8.2 5.9 %collective-permute-start.2 = (bf16[4,6144]{1,0:T(4,128)(2,1)S(1)}, bf16[4,6144]{1,0:T(4,128)(2,1)S(1)}, u32[]{:S(2)}, u32[]{:S(2)}) collective-permute-start(bf16[4,6144]{1,0:T(4,128)(2,1)S(1)} %pack.1.refs_2_), channel_id=1, source_target_pairs={{0,12},{1,13},{2,14},{3,15},{4,8},{5,9},{6,10},{7,11},{8,4},{9,5},... | collective-permute-start | bytes 147464 | tf_op jit(solution)/shard_map/ppermute | solution.py:39
  8.2 7.4 %collective-permute-start.3 = (bf16[4,6144]{1,0:T(4,128)(2,1)S(1)}, bf16[4,6144]{1,0:T(4,128)(2,1)S(1)}, u32[]{:S(2)}, u32[]{:S(2)}) collective-permute-start(bf16[4,6144]{1,0:T(4,128)(2,1)S(1)} %pack.1.refs_2_), channel_id=1, source_target_pairs={{0,2},{1,3},{2,0},{3,1},{4,6},{5,7},{6,4},{7,5},{8,10},{9,11},{10,... | collective-permute-start | bytes 147464 | tf_op jit(solution)/shard_map/ppermute | solution.py:39
  9.9 5.7 %collective-permute-start.7 = (bf16[4,6144]{1,0:T(4,128)(2,1)S(1)}, bf16[4,6144]{1,0:T(4,128)(2,1)S(1)}, u32[]{:S(2)}, u32[]{:S(2)}) collective-permute-start(bf16[4,6144]{1,0:T(4,128)(2,1)S(1)} %pack.1.refs_2_), channel_id=1, source_target_pairs={{0,1},{1,0},{2,3},{3,2},{4,5},{5,4},{6,7},{7,6},{8,9},{9,8},{10,11... | collective-permute-start | bytes 147464 | tf_op jit(solution)/shard_map/ppermute | solution.py:39
  9.9 6.2 %collective-permute-start.4 = (bf16[4,6144]{1,0:T(4,128)(2,1)S(1)}, bf16[4,6144]{1,0:T(4,128)(2,1)S(1)}, u32[]{:S(2)}, u32[]{:S(2)}) collective-permute-start(bf16[4,6144]{1,0:T(4,128)(2,1)S(1)} %collective-permute-done.refs_3_), channel_id=1, source_target_pairs={{0,2},{1,3},{2,0},{3,1},{4,6},{5,7},{6,4},{7,5},{8,10},{9,11},{10,... | collective-permute-start | bytes 147464 | tf_op jit(solution)/shard_map/ppermute | solution.py:39
  11.0 5.1 %collective-permute-start.5 = (bf16[4,6144]{1,0:T(4,128)(2,1)S(1)}, bf16[4,6144]{1,0:T(4,128)(2,1)S(1)}, u32[]{:S(2)}, u32[]{:S(2)}) collective-permute-start(bf16[4,6144]{1,0:T(4,128)(2,1)S(1)} %collective-permute-done.1.refs_4_), channel_id=1, source_target_pairs={{0,2},{1,3},{2,0},{3,1},{4,6},{5,7},{6,4},{7,5},{8,10},{9,11},{10,... | collective-permute-start | bytes 147464 | tf_op jit(solution)/shard_map/ppermute | solution.py:39
  14.1 4.1 %collective-permute-start.6 = (bf16[4,6144]{1,0:T(4,128)(2,1)S(1)}, bf16[4,6144]{1,0:T(4,128)(2,1)S(1)}, u32[]{:S(2)}, u32[]{:S(2)}) collective-permute-start(bf16[4,6144]{1,0:T(4,128)(2,1)S(1)} %collective-permute-done.2.refs_5_), channel_id=1, source_target_pairs={{0,2},{1,3},{2,0},{3,1},{4,6},{5,7},{6,4},{7,5},{8,10},{9,11},{10,... | collective-permute-start | bytes 147464 | tf_op jit(solution)/shard_map/ppermute | solution.py:39
  15.6 3.1 %collective-permute-start.8 = (bf16[4,6144]{1,0:T(4,128)(2,1)S(1)}, bf16[4,6144]{1,0:T(4,128)(2,1)S(1)}, u32[]{:S(2)}, u32[]{:S(2)}) collective-permute-start(bf16[4,6144]{1,0:T(4,128)(2,1)S(1)} %collective-permute-done.refs_3_), channel_id=1, source_target_pairs={{0,1},{1,0},{2,3},{3,2},{4,5},{5,4},{6,7},{7,6},{8,9},{9,8},{10,11... | collective-permute-start | bytes 147464 | tf_op jit(solution)/shard_map/ppermute | solution.py:39
  16.1 2.7 %collective-permute-start.9 = (bf16[4,6144]{1,0:T(4,128)(2,1)S(1)}, bf16[4,6144]{1,0:T(4,128)(2,1)S(1)}, u32[]{:S(2)}, u32[]{:S(2)}) collective-permute-start(bf16[4,6144]{1,0:T(4,128)(2,1)S(1)} %collective-permute-done.1.refs_4_), channel_id=1, source_target_pairs={{0,1},{1,0},{2,3},{3,2},{4,5},{5,4},{6,7},{7,6},{8,9},{9,8},{10,11... | collective-permute-start | bytes 147464 | tf_op jit(solution)/shard_map/ppermute | solution.py:39
  22.5 7.3 %collective-permute-start.15 = (bf16[48,1024]{1,0:T(8,128)(2,1)S(1)}, bf16[48,1024]{1,0:T(8,128)(2,1)S(1)}, u32[]{:S(2)}, u32[]{:S(2)}) collective-permute-start(bf16[48,1024]{1,0:T(8,128)(2,1)S(1)} %get-tuple-element.26.refs_4_), channel_id=1, source_target_pairs={{0,8},{1,9},{2,10},{3,11},{4,12},{5,13},{6,14},{7,15},{8,0},{9,1},... | collective-permute-start | bytes 294920 | tf_op jit(solution)/shard_map/ppermute | solution.py:39
  22.6 8.7 %collective-permute-start.16 = (bf16[48,1024]{1,0:T(8,128)(2,1)S(1)}, bf16[48,1024]{1,0:T(8,128)(2,1)S(1)}, u32[]{:S(2)}, u32[]{:S(2)}) collective-permute-start(bf16[48,1024]{1,0:T(8,128)(2,1)S(1)} %get-tuple-element.26.refs_4_), channel_id=1, source_target_pairs={{0,4},{1,5},{2,6},{3,7},{4,0},{5,1},{6,2},{7,3},{8,12},{9,13},{10,... | collective-permute-start | bytes 294920 | tf_op jit(solution)/shard_map/ppermute | solution.py:39
  25.1 6.8 %collective-permute-start.18 = (bf16[48,1024]{1,0:T(8,128)(2,1)S(1)}, bf16[48,1024]{1,0:T(8,128)(2,1)S(1)}, u32[]{:S(2)}, u32[]{:S(2)}) collective-permute-start(bf16[48,1024]{1,0:T(8,128)(2,1)S(1)} %get-tuple-element.26.refs_4_), channel_id=1, source_target_pairs={{0,2},{1,3},{2,0},{3,1},{4,6},{5,7},{6,4},{7,5},{8,10},{9,11},{10,... | collective-permute-start | bytes 294920 | tf_op jit(solution)/shard_map/ppermute | solution.py:39
  26.6 5.3 %collective-permute-start.22 = (bf16[48,1024]{1,0:T(8,128)(2,1)S(1)}, bf16[48,1024]{1,0:T(8,128)(2,1)S(1)}, u32[]{:S(2)}, u32[]{:S(2)}) collective-permute-start(bf16[48,1024]{1,0:T(8,128)(2,1)S(1)} %get-tuple-element.26.refs_4_), channel_id=1, source_target_pairs={{0,1},{1,0},{2,3},{3,2},{4,5},{5,4},{6,7},{7,6},{8,9},{9,8},{10,11... | collective-permute-start | bytes 294920 | tf_op jit(solution)/shard_map/ppermute | solution.py:39
  29.8 4.7 %collective-permute-start.17 = (bf16[48,1024]{1,0:T(8,128)(2,1)S(1)}, bf16[48,1024]{1,0:T(8,128)(2,1)S(1)}, u32[]{:S(2)}, u32[]{:S(2)}) collective-permute-start(bf16[48,1024]{1,0:T(8,128)(2,1)S(1)} %collective-permute-done.15.refs_5_), channel_id=1, source_target_pairs={{0,4},{1,5},{2,6},{3,7},{4,0},{5,1},{6,2},{7,3},{8,12},{9,13},{10,... | collective-permute-start | bytes 294920 | tf_op jit(solution)/shard_map/ppermute | solution.py:39
  29.8 6.2 %collective-permute-start.19 = (bf16[48,1024]{1,0:T(8,128)(2,1)S(1)}, bf16[48,1024]{1,0:T(8,128)(2,1)S(1)}, u32[]{:S(2)}, u32[]{:S(2)}) collective-permute-start(bf16[48,1024]{1,0:T(8,128)(2,1)S(1)} %collective-permute-done.15.refs_5_), channel_id=1, source_target_pairs={{0,2},{1,3},{2,0},{3,1},{4,6},{5,7},{6,4},{7,5},{8,10},{9,11},{10,... | collective-permute-start | bytes 294920 | tf_op jit(solution)/shard_map/ppermute | solution.py:39
  31.3 5.6 %collective-permute-start.20 = (bf16[48,1024]{1,0:T(8,128)(2,1)S(1)}, bf16[48,1024]{1,0:T(8,128)(2,1)S(1)}, u32[]{:S(2)}, u32[]{:S(2)}) collective-permute-start(bf16[48,1024]{1,0:T(8,128)(2,1)S(1)} %collective-permute-done.16.refs_6_), channel_id=1, source_target_pairs={{0,2},{1,3},{2,0},{3,1},{4,6},{5,7},{6,4},{7,5},{8,10},{9,11},{10,... | collective-permute-start | bytes 294920 | tf_op jit(solution)/shard_map/ppermute | solution.py:39
  31.9 5.1 %collective-permute-start.23 = (bf16[48,1024]{1,0:T(8,128)(2,1)S(1)}, bf16[48,1024]{1,0:T(8,128)(2,1)S(1)}, u32[]{:S(2)}, u32[]{:S(2)}) collective-permute-start(bf16[48,1024]{1,0:T(8,128)(2,1)S(1)} %collective-permute-done.15.refs_5_), channel_id=1, source_target_pairs={{0,1},{1,0},{2,3},{3,2},{4,5},{5,4},{6,7},{7,6},{8,9},{9,8},{10,11... | collective-permute-start | bytes 294920 | tf_op jit(solution)/shard_map/ppermute | solution.py:39
  31.9 5.6 %collective-permute-start.24 = (bf16[48,1024]{1,0:T(8,128)(2,1)S(1)}, bf16[48,1024]{1,0:T(8,128)(2,1)S(1)}, u32[]{:S(2)}, u32[]{:S(2)}) collective-permute-start(bf16[48,1024]{1,0:T(8,128)(2,1)S(1)} %collective-permute-done.16.refs_6_), channel_id=1, source_target_pairs={{0,1},{1,0},{2,3},{3,2},{4,5},{5,4},{6,7},{7,6},{8,9},{9,8},{10,11... | collective-permute-start | bytes 294920 | tf_op jit(solution)/shard_map/ppermute | solution.py:39
  34.5 4.6 %collective-permute-start.21 = (bf16[48,1024]{1,0:T(8,128)(2,1)S(1)}, bf16[48,1024]{1,0:T(8,128)(2,1)S(1)}, u32[]{:S(2)}, u32[]{:S(2)}) collective-permute-start(bf16[48,1024]{1,0:T(8,128)(2,1)S(1)} %collective-permute-done.17.refs_7_), channel_id=1, source_target_pairs={{0,2},{1,3},{2,0},{3,1},{4,6},{5,7},{6,4},{7,5},{8,10},{9,11},{10,... | collective-permute-start | bytes 294920 | tf_op jit(solution)/shard_map/ppermute | solution.py:39
  36.0 3.1 %collective-permute-start.26 = (bf16[48,1024]{1,0:T(8,128)(2,1)S(1)}, bf16[48,1024]{1,0:T(8,128)(2,1)S(1)}, u32[]{:S(2)}, u32[]{:S(2)}) collective-permute-start(bf16[48,1024]{1,0:T(8,128)(2,1)S(1)} %collective-permute-done.18.refs_8_), channel_id=1, source_target_pairs={{0,1},{1,0},{2,3},{3,2},{4,5},{5,4},{6,7},{7,6},{8,9},{9,8},{10,11... | collective-permute-start | bytes 294920 | tf_op jit(solution)/shard_map/ppermute | solution.py:39
  43.0 8.5 %collective-permute-start.30 = (bf16[192,128]{1,0:T(8,128)(2,1)S(1)}, bf16[192,128]{1,0:T(8,128)(2,1)S(1)}, u32[]{:S(2)}, u32[]{:S(2)}) collective-permute-start(bf16[192,128]{1,0:T(8,128)(2,1)S(1)} %get-tuple-element.28.refs_4_), channel_id=1, source_target_pairs={{0,8},{1,9},{2,10},{3,11},{4,12},{5,13},{6,14},{7,15},{8,0},{9,1},... | collective-permute-start | bytes 147464 | tf_op jit(solution)/shard_map/ppermute | solution.py:39
  45.0 6.5 %collective-permute-start.31 = (bf16[192,128]{1,0:T(8,128)(2,1)S(1)}, bf16[192,128]{1,0:T(8,128)(2,1)S(1)}, u32[]{:S(2)}, u32[]{:S(2)}) collective-permute-start(bf16[192,128]{1,0:T(8,128)(2,1)S(1)} %get-tuple-element.28.refs_4_), channel_id=1, source_target_pairs={{0,4},{1,5},{2,6},{3,7},{4,0},{5,1},{6,2},{7,3},{8,12},{9,13},{10,... | collective-permute-start | bytes 147464 | tf_op jit(solution)/shard_map/ppermute | solution.py:39
  45.5 6.0 %collective-permute-start.32 = (bf16[192,128]{1,0:T(8,128)(2,1)S(1)}, bf16[192,128]{1,0:T(8,128)(2,1)S(1)}, u32[]{:S(2)}, u32[]{:S(2)}) collective-permute-start(bf16[192,128]{1,0:T(8,128)(2,1)S(1)} %get-tuple-element.28.refs_4_), channel_id=1, source_target_pairs={{0,12},{1,13},{2,14},{3,15},{4,8},{5,9},{6,10},{7,11},{8,4},{9,5},... | collective-permute-start | bytes 147464 | tf_op jit(solution)/shard_map/ppermute | solution.py:39
  47.4 4.1 %collective-permute-start.33 = (bf16[192,128]{1,0:T(8,128)(2,1)S(1)}, bf16[192,128]{1,0:T(8,128)(2,1)S(1)}, u32[]{:S(2)}, u32[]{:S(2)}) collective-permute-start(bf16[192,128]{1,0:T(8,128)(2,1)S(1)} %get-tuple-element.28.refs_4_), channel_id=1, source_target_pairs={{0,2},{1,3},{2,0},{3,1},{4,6},{5,7},{6,4},{7,5},{8,10},{9,11},{10,... | collective-permute-start | bytes 147464 | tf_op jit(solution)/shard_map/ppermute | solution.py:39
  48.9 3.8 %collective-permute-start.37 = (bf16[192,128]{1,0:T(8,128)(2,1)S(1)}, bf16[192,128]{1,0:T(8,128)(2,1)S(1)}, u32[]{:S(2)}, u32[]{:S(2)}) collective-permute-start(bf16[192,128]{1,0:T(8,128)(2,1)S(1)} %get-tuple-element.28.refs_4_), channel_id=1, source_target_pairs={{0,1},{1,0},{2,3},{3,2},{4,5},{5,4},{6,7},{7,6},{8,9},{9,8},{10,11... | collective-permute-start | bytes 147464 | tf_op jit(solution)/shard_map/ppermute | solution.py:39
  52.1 2.6 %collective-permute-start.39 = (bf16[192,128]{1,0:T(8,128)(2,1)S(1)}, bf16[192,128]{1,0:T(8,128)(2,1)S(1)}, u32[]{:S(2)}, u32[]{:S(2)}) collective-permute-start(bf16[192,128]{1,0:T(8,128)(2,1)S(1)} %collective-permute-done.31.refs_6_), channel_id=1, source_target_pairs={{0,1},{1,0},{2,3},{3,2},{4,5},{5,4},{6,7},{7,6},{8,9},{9,8},{10,11... | collective-permute-start | bytes 147464 | tf_op jit(solution)/shard_map/ppermute | solution.py:39
  52.2 3.9 %collective-permute-start.40 = (bf16[192,128]{1,0:T(8,128)(2,1)S(1)}, bf16[192,128]{1,0:T(8,128)(2,1)S(1)}, u32[]{:S(2)}, u32[]{:S(2)}) collective-permute-start(bf16[192,128]{1,0:T(8,128)(2,1)S(1)} %collective-permute-done.32.refs_7_), channel_id=1, source_target_pairs={{0,1},{1,0},{2,3},{3,2},{4,5},{5,4},{6,7},{7,6},{8,9},{9,8},{10,11... | collective-permute-start | bytes 147464 | tf_op jit(solution)/shard_map/ppermute | solution.py:39
  52.6 3.5 %collective-permute-start.41 = (bf16[192,128]{1,0:T(8,128)(2,1)S(1)}, bf16[192,128]{1,0:T(8,128)(2,1)S(1)}, u32[]{:S(2)}, u32[]{:S(2)}) collective-permute-start(bf16[192,128]{1,0:T(8,128)(2,1)S(1)} %collective-permute-done.33.refs_8_), channel_id=1, source_target_pairs={{0,1},{1,0},{2,3},{3,2},{4,5},{5,4},{6,7},{7,6},{8,9},{9,8},{10,11... | collective-permute-start | bytes 147464 | tf_op jit(solution)/shard_map/ppermute | solution.py:39
  52.7 6.0 %collective-permute-start.34 = (bf16[192,128]{1,0:T(8,128)(2,1)S(1)}, bf16[192,128]{1,0:T(8,128)(2,1)S(1)}, u32[]{:S(2)}, u32[]{:S(2)}) collective-permute-start(bf16[192,128]{1,0:T(8,128)(2,1)S(1)} %collective-permute-done.30.refs_5_), channel_id=1, source_target_pairs={{0,2},{1,3},{2,0},{3,1},{4,6},{5,7},{6,4},{7,5},{8,10},{9,11},{10,... | collective-permute-start | bytes 147464 | tf_op jit(solution)/shard_map/ppermute | solution.py:39
  54.1 4.7 %collective-permute-start.35 = (bf16[192,128]{1,0:T(8,128)(2,1)S(1)}, bf16[192,128]{1,0:T(8,128)(2,1)S(1)}, u32[]{:S(2)}, u32[]{:S(2)}) collective-permute-start(bf16[192,128]{1,0:T(8,128)(2,1)S(1)} %collective-permute-done.31.refs_6_), channel_id=1, source_target_pairs={{0,2},{1,3},{2,0},{3,1},{4,6},{5,7},{6,4},{7,5},{8,10},{9,11},{10,... | collective-permute-start | bytes 147464 | tf_op jit(solution)/shard_map/ppermute | solution.py:39
  54.7 4.2 %collective-permute-start.36 = (bf16[192,128]{1,0:T(8,128)(2,1)S(1)}, bf16[192,128]{1,0:T(8,128)(2,1)S(1)}, u32[]{:S(2)}, u32[]{:S(2)}) collective-permute-start(bf16[192,128]{1,0:T(8,128)(2,1)S(1)} %collective-permute-done.32.refs_7_), channel_id=1, source_target_pairs={{0,2},{1,3},{2,0},{3,1},{4,6},{5,7},{6,4},{7,5},{8,10},{9,11},{10,... | collective-permute-start | bytes 147464 | tf_op jit(solution)/shard_map/ppermute | solution.py:39
  (23 other events, 175.2 us)

commit v6 on v5

--- a/solution.py
+++ b/solution.py
@@ -345,7 +345,7 @@
     for j in range(devices):
         flat[j * entries : (j + 1) * entries, :] = fetch(pieces[j], stages[:2]).astype(F32)
 
-    @pl.loop(0, heads)
+    @pl.loop(0, heads, unroll=4)
     def _(h):
         base = pl.multiple_of(h * sessions, 8)
         for s in range(sessions):

time: 64.5 us -> 64.4 us (level)
  no operation moved by 1% of the time
where the time goes in v6:
time: 64.4 us; the launch traced here: 64.2 us
  starting transfers between devices  32.5 us (50%)
  waiting for transfers between devices  15.3 us (24%)
  Pallas kernels  13.7 us (21%)
  local copies, waits for them, and re-layouts  1.04 us (2%)
  other arithmetic  0.85 us (1%)
  between operations  0.84 us (1%)
    ppermute x45, starting transfers between devices, cross(): return lax.ppermute(piece, 'batch', [(i, i ^ bit) for i in range(devices)])  32.5 us
    ppermute x45, waiting for transfers between devices, cross(): return lax.ppermute(piece, 'batch', [(i, i ^ bit) for i in range(devices)])  15.3 us
    pallas_call x2, Pallas kernels, update_tiles(): pl.pallas_call(functools.partial(update_kernel, first, count), out_shape=...  5.14 us
    pallas_call x1, Pallas kernels, finish(): pl.pallas_call(functools.partial(finish_kernel, devices, per), out_shape=...  3.53 us
    pallas_call x1, Pallas kernels, read_states(): pl.pallas_call(functools.partial(readout_kernel, devices), out_shape=(jax...  2.55 us
    pallas_call x1, Pallas kernels, project(): pl.pallas_call(functools.partial(project_kernel, devices, heads, slots, s...  2.49 us
  transfers between devices with their start and end apart: 45, of which 14 were waited for; matrix products, arithmetic and copies ran while one was open for 0% of the time, Pallas kernels for 8%

profile of v6, /device:TPU:0, one launch (start us, length us, event | category | flops | bytes accessed | tf_op | source)
XLA Modules:
  0.0 64.2 jit_solution(4756438396276154917)
XLA Ops:
  0.6 0.9 %multiply_add_fusion.origin_ref = s32[3,32]{1,0:T(4,128)S(1)} fusion(s32[3,32]{1,0:T(4,128)} %param.18, s32[3,32]{1,0:T(4,128)} %param.17), kind=kLoop, calls=%fused_computation | loop fusion | flops 192 | bytes 1152 | tf_op jit(solution)/shard_map/add | solution.py:429
  1.5 1.0 %copy-done.6 = bf16[3,6144]{1,0:T(4,128)(2,1)S(1)} copy-done((bf16[3,6144]{1,0:T(4,128)(2,1)S(1)}, bf16[3,6144]{1,0:T(4,128)(2,1)}, u32[]{:S(2)}) %copy-start.6) | copy-done | bytes 36888
  2.5 4.1 %collective-permute-start = (bf16[4,6144]{1,0:T(4,128)(2,1)S(1)}, bf16[4,6144]{1,0:T(4,128)(2,1)S(1)}, u32[]{:S(2)}, u32[]{:S(2)}) collective-permute-start(bf16[4,6144]{1,0:T(4,128)(2,1)S(1)} %pack.1.refs_2_), channel_id=1, source_target_pairs={{0,8},{1,9},{2,10},{3,11},{4,12},{5,13},{6,14},{7,15},{8,0},{9,1},... | collective-permute-start | bytes 147464 | tf_op jit(solution)/shard_map/ppermute | solution.py:39
  6.6 1.6 %collective-permute-start.1 = (bf16[4,6144]{1,0:T(4,128)(2,1)S(1)}, bf16[4,6144]{1,0:T(4,128)(2,1)S(1)}, u32[]{:S(2)}, u32[]{:S(2)}) collective-permute-start(bf16[4,6144]{1,0:T(4,128)(2,1)S(1)} %pack.1.refs_2_), channel_id=1, source_target_pairs={{0,4},{1,5},{2,6},{3,7},{4,0},{5,1},{6,2},{7,3},{8,12},{9,13},{10,... | collective-permute-start | bytes 147464 | tf_op jit(solution)/shard_map/ppermute | solution.py:39
  8.2 1.7 %collective-permute-start.3 = (bf16[4,6144]{1,0:T(4,128)(2,1)S(1)}, bf16[4,6144]{1,0:T(4,128)(2,1)S(1)}, u32[]{:S(2)}, u32[]{:S(2)}) collective-permute-start(bf16[4,6144]{1,0:T(4,128)(2,1)S(1)} %pack.1.refs_2_), channel_id=1, source_target_pairs={{0,2},{1,3},{2,0},{3,1},{4,6},{5,7},{6,4},{7,5},{8,10},{9,11},{10,... | collective-permute-start | bytes 147464 | tf_op jit(solution)/shard_map/ppermute | solution.py:39
  9.9 1.1 %collective-permute-start.4 = (bf16[4,6144]{1,0:T(4,128)(2,1)S(1)}, bf16[4,6144]{1,0:T(4,128)(2,1)S(1)}, u32[]{:S(2)}, u32[]{:S(2)}) collective-permute-start(bf16[4,6144]{1,0:T(4,128)(2,1)S(1)} %collective-permute-done.refs_3_), channel_id=1, source_target_pairs={{0,2},{1,3},{2,0},{3,1},{4,6},{5,7},{6,4},{7,5},{8,10},{9,11},{10,... | collective-permute-start | bytes 147464 | tf_op jit(solution)/shard_map/ppermute | solution.py:39
  11.0 1.2 %collective-permute-start.5 = (bf16[4,6144]{1,0:T(4,128)(2,1)S(1)}, bf16[4,6144]{1,0:T(4,128)(2,1)S(1)}, u32[]{:S(2)}, u32[]{:S(2)}) collective-permute-start(bf16[4,6144]{1,0:T(4,128)(2,1)S(1)} %collective-permute-done.1.refs_4_), channel_id=1, source_target_pairs={{0,2},{1,3},{2,0},{3,1},{4,6},{5,7},{6,4},{7,5},{8,10},{9,11},{10,... | collective-permute-start | bytes 147464 | tf_op jit(solution)/shard_map/ppermute | solution.py:39
  12.2 1.9 %collective-permute-done.2.refs_5_ = bf16[4,6144]{1,0:T(4,128)(2,1)S(1)} collective-permute-done((bf16[4,6144]{1,0:T(4,128)(2,1)S(1)}, bf16[4,6144]{1,0:T(4,128)(2,1)S(1)}, u32[]{:S(2)}, u32[]{:S(2)}) %collective-permute-start.2) | collective-permute-done | bytes 49184 | tf_op jit(solution)/shard_map/ppermute | solution.py:39
  14.1 1.5 %collective-permute-start.6 = (bf16[4,6144]{1,0:T(4,128)(2,1)S(1)}, bf16[4,6144]{1,0:T(4,128)(2,1)S(1)}, u32[]{:S(2)}, u32[]{:S(2)}) collective-permute-start(bf16[4,6144]{1,0:T(4,128)(2,1)S(1)} %collective-permute-done.2.refs_5_), channel_id=1, source_target_pairs={{0,2},{1,3},{2,0},{3,1},{4,6},{5,7},{6,4},{7,5},{8,10},{9,11},{10,... | collective-permute-start | bytes 147464 | tf_op jit(solution)/shard_map/ppermute | solution.py:39
  16.6 1.6 %collective-permute-done.6.refs_9_ = bf16[4,6144]{1,0:T(4,128)(2,1)S(1)} collective-permute-done((bf16[4,6144]{1,0:T(4,128)(2,1)S(1)}, bf16[4,6144]{1,0:T(4,128)(2,1)S(1)}, u32[]{:S(2)}, u32[]{:S(2)}) %collective-permute-start.6) | collective-permute-done | bytes 49184 | tf_op jit(solution)/shard_map/ppermute | solution.py:39
  18.8 0.6 collective-permute-done.12.refs_15_
  20.0 2.5 %project.1 = (bf16[48,1024]{1,0:T(8,128)(2,1)S(1)}, s32[32,48]{1,0:T(8,128)S(1)}, s32[8,256]{1,0:T(8,128)S(1)}) custom-call(s32[12,1,16]{2,1,0:T(1,128)S(1)} %bitcast.5, bf16[6144,1024]{1,0:T(8,128)(2,1)S(1)} %bitcast.3, bf16[4,6144]{1,0:T(4,128)(2,1)S(1)} %pack.1.refs_2_, bf16[4,6144]{1,0:T(4,128)(2,1)S(1)} %collective-permute-done.refs_3_, ...), custom_call_target="tpu_custom_call" | custom-call | flops 603979776 | bytes 12582912 | tf_op jit(solution)/shard_map/project/pallas_call | solution.py:181
  22.6 2.4 %collective-permute-start.16 = (bf16[48,1024]{1,0:T(8,128)(2,1)S(1)}, bf16[48,1024]{1,0:T(8,128)(2,1)S(1)}, u32[]{:S(2)}, u32[]{:S(2)}) collective-permute-start(bf16[48,1024]{1,0:T(8,128)(2,1)S(1)} %get-tuple-element.26.refs_4_), channel_id=1, source_target_pairs={{0,4},{1,5},{2,6},{3,7},{4,0},{5,1},{6,2},{7,3},{8,12},{9,13},{10,... | collective-permute-start | bytes 294920 | tf_op jit(solution)/shard_map/ppermute | solution.py:39
  25.1 1.5 %collective-permute-start.18 = (bf16[48,1024]{1,0:T(8,128)(2,1)S(1)}, bf16[48,1024]{1,0:T(8,128)(2,1)S(1)}, u32[]{:S(2)}, u32[]{:S(2)}) collective-permute-start(bf16[48,1024]{1,0:T(8,128)(2,1)S(1)} %get-tuple-element.26.refs_4_), channel_id=1, source_target_pairs={{0,2},{1,3},{2,0},{3,1},{4,6},{5,7},{6,4},{7,5},{8,10},{9,11},{10,... | collective-permute-start | bytes 294920 | tf_op jit(solution)/shard_map/ppermute | solution.py:39
  26.6 3.3 %collective-permute-done.15.refs_5_ = bf16[48,1024]{1,0:T(8,128)(2,1)S(1)} collective-permute-done((bf16[48,1024]{1,0:T(8,128)(2,1)S(1)}, bf16[48,1024]{1,0:T(8,128)(2,1)S(1)}, u32[]{:S(2)}, u32[]{:S(2)}) %collective-permute-start.15) | collective-permute-done | bytes 98336 | tf_op jit(solution)/shard_map/ppermute | solution.py:39
  29.8 1.5 %collective-permute-start.19 = (bf16[48,1024]{1,0:T(8,128)(2,1)S(1)}, bf16[48,1024]{1,0:T(8,128)(2,1)S(1)}, u32[]{:S(2)}, u32[]{:S(2)}) collective-permute-start(bf16[48,1024]{1,0:T(8,128)(2,1)S(1)} %collective-permute-done.15.refs_5_), channel_id=1, source_target_pairs={{0,2},{1,3},{2,0},{3,1},{4,6},{5,7},{6,4},{7,5},{8,10},{9,11},{10,... | collective-permute-start | bytes 294920 | tf_op jit(solution)/shard_map/ppermute | solution.py:39
  32.4 2.1 %collective-permute-done.17.refs_7_ = bf16[48,1024]{1,0:T(8,128)(2,1)S(1)} collective-permute-done((bf16[48,1024]{1,0:T(8,128)(2,1)S(1)}, bf16[48,1024]{1,0:T(8,128)(2,1)S(1)}, u32[]{:S(2)}, u32[]{:S(2)}) %collective-permute-start.17) | collective-permute-done | bytes 98336 | tf_op jit(solution)/shard_map/ppermute | solution.py:39
  34.5 1.5 %collective-permute-start.21 = (bf16[48,1024]{1,0:T(8,128)(2,1)S(1)}, bf16[48,1024]{1,0:T(8,128)(2,1)S(1)}, u32[]{:S(2)}, u32[]{:S(2)}) collective-permute-start(bf16[48,1024]{1,0:T(8,128)(2,1)S(1)} %collective-permute-done.17.refs_7_), channel_id=1, source_target_pairs={{0,2},{1,3},{2,0},{3,1},{4,6},{5,7},{6,4},{7,5},{8,10},{9,11},{10,... | collective-permute-start | bytes 294920 | tf_op jit(solution)/shard_map/ppermute | solution.py:39
  36.0 0.9 %collective-permute-done.20.refs_10_ = bf16[48,1024]{1,0:T(8,128)(2,1)S(1)} collective-permute-done((bf16[48,1024]{1,0:T(8,128)(2,1)S(1)}, bf16[48,1024]{1,0:T(8,128)(2,1)S(1)}, u32[]{:S(2)}, u32[]{:S(2)}) %collective-permute-start.20) | collective-permute-done | bytes 98336 | tf_op jit(solution)/shard_map/ppermute | solution.py:39
  37.5 1.6 %collective-permute-done.21.refs_11_ = bf16[48,1024]{1,0:T(8,128)(2,1)S(1)} collective-permute-done((bf16[48,1024]{1,0:T(8,128)(2,1)S(1)}, bf16[48,1024]{1,0:T(8,128)(2,1)S(1)}, u32[]{:S(2)}, u32[]{:S(2)}) %collective-permute-start.21) | collective-permute-done | bytes 98336 | tf_op jit(solution)/shard_map/ppermute | solution.py:39
  39.2 1.3 %collective-permute-done.29.refs_19_ = bf16[48,1024]{1,0:T(8,128)(2,1)S(1)} collective-permute-done((bf16[48,1024]{1,0:T(8,128)(2,1)S(1)}, bf16[48,1024]{1,0:T(8,128)(2,1)S(1)}, u32[]{:S(2)}, u32[]{:S(2)}) %collective-permute-start.29) | collective-permute-done | bytes 98336 | tf_op jit(solution)/shard_map/ppermute | solution.py:39
  40.4 2.5 %readout.1 = (bf16[192,128]{1,0:T(8,128)(2,1)S(1)}, f32[6152,128]{1,0:T(8,128)S(1)}, f32[168,128]{1,0:T(8,128)S(1)}, f32[168,128]{1,0:T(8,128)S(1)}) custom-call(s32[8,256]{1,0:T(8,128)S(1)} %get-tuple-element.25.refs_0_, f32[32]{0:T(128)S(1)} %copy-done.5, f32[168]{0:T(256)S(1)} %copy-done.3, bf16[168,128,128]{2,1,0:T(8,128)(2,1)S(1)} %copy-done, ...), custom_call_target="tpu_custom_call" | custom-call | flops 5505024 | bytes 22020096 | tf_op jit(solution)/shard_map/readout/pallas_call | solution.py:263
  43.0 2.0 %collective-permute-start.30 = (bf16[192,128]{1,0:T(8,128)(2,1)S(1)}, bf16[192,128]{1,0:T(8,128)(2,1)S(1)}, u32[]{:S(2)}, u32[]{:S(2)}) collective-permute-start(bf16[192,128]{1,0:T(8,128)(2,1)S(1)} %get-tuple-element.28.refs_4_), channel_id=1, source_target_pairs={{0,8},{1,9},{2,10},{3,11},{4,12},{5,13},{6,14},{7,15},{8,0},{9,1},... | collective-permute-start | bytes 147464 | tf_op jit(solution)/shard_map/ppermute | solution.py:39
  45.5 2.0 %collective-permute-start.32 = (bf16[192,128]{1,0:T(8,128)(2,1)S(1)}, bf16[192,128]{1,0:T(8,128)(2,1)S(1)}, u32[]{:S(2)}, u32[]{:S(2)}) collective-permute-start(bf16[192,128]{1,0:T(8,128)(2,1)S(1)} %get-tuple-element.28.refs_4_), channel_id=1, source_target_pairs={{0,12},{1,13},{2,14},{3,15},{4,8},{5,9},{6,10},{7,11},{8,4},{9,5},... | collective-permute-start | bytes 147464 | tf_op jit(solution)/shard_map/ppermute | solution.py:39
  47.4 1.5 %collective-permute-start.33 = (bf16[192,128]{1,0:T(8,128)(2,1)S(1)}, bf16[192,128]{1,0:T(8,128)(2,1)S(1)}, u32[]{:S(2)}, u32[]{:S(2)}) collective-permute-start(bf16[192,128]{1,0:T(8,128)(2,1)S(1)} %get-tuple-element.28.refs_4_), channel_id=1, source_target_pairs={{0,2},{1,3},{2,0},{3,1},{4,6},{5,7},{6,4},{7,5},{8,10},{9,11},{10,... | collective-permute-start | bytes 147464 | tf_op jit(solution)/shard_map/ppermute | solution.py:39
  48.9 2.5 %update.2.refs_6_ = bf16[168,128,128]{2,1,0:T(8,128)(2,1)} custom-call(s32[8,256]{1,0:T(8,128)S(1)} %get-tuple-element.25.refs_0_, f32[32]{0:T(128)S(1)} %copy-done.5, f32[168]{0:T(256)S(1)} %copy-done.3, bf16[168,128,128]{2,1,0:T(8,128)(2,1)S(1)} %copy-done, f32[168,128]{1,0:T(8,128)S(1)} %get-tuple-element.29.refs_4_, f32[168,128]{1,0:T(8,128)S(1)} %get-tuple-element.30.refs_5_), custom_call_target="tpu_custom_call" | custom-call | bytes 5242880 | tf_op jit(solution)/shard_map/update/pallas_call | solution.py:319
  52.7 1.4 %collective-permute-start.34 = (bf16[192,128]{1,0:T(8,128)(2,1)S(1)}, bf16[192,128]{1,0:T(8,128)(2,1)S(1)}, u32[]{:S(2)}, u32[]{:S(2)}) collective-permute-start(bf16[192,128]{1,0:T(8,128)(2,1)S(1)} %collective-permute-done.30.refs_5_), channel_id=1, source_target_pairs={{0,2},{1,3},{2,0},{3,1},{4,6},{5,7},{6,4},{7,5},{8,10},{9,11},{10,... | collective-permute-start | bytes 147464 | tf_op jit(solution)/shard_map/ppermute | solution.py:39
  54.1 0.7 %collective-permute-start.35 = (bf16[192,128]{1,0:T(8,128)(2,1)S(1)}, bf16[192,128]{1,0:T(8,128)(2,1)S(1)}, u32[]{:S(2)}, u32[]{:S(2)}) collective-permute-start(bf16[192,128]{1,0:T(8,128)(2,1)S(1)} %collective-permute-done.31.refs_6_), channel_id=1, source_target_pairs={{0,2},{1,3},{2,0},{3,1},{4,6},{5,7},{6,4},{7,5},{8,10},{9,11},{10,... | collective-permute-start | bytes 147464 | tf_op jit(solution)/shard_map/ppermute | solution.py:39
  54.7 1.4 %collective-permute-start.36 = (bf16[192,128]{1,0:T(8,128)(2,1)S(1)}, bf16[192,128]{1,0:T(8,128)(2,1)S(1)}, u32[]{:S(2)}, u32[]{:S(2)}) collective-permute-start(bf16[192,128]{1,0:T(8,128)(2,1)S(1)} %collective-permute-done.32.refs_7_), channel_id=1, source_target_pairs={{0,2},{1,3},{2,0},{3,1},{4,6},{5,7},{6,4},{7,5},{8,10},{9,11},{10,... | collective-permute-start | bytes 147464 | tf_op jit(solution)/shard_map/ppermute | solution.py:39
  56.1 2.6 %update.3 = bf16[168,128,128]{2,1,0:T(8,128)(2,1)} custom-call(s32[8,256]{1,0:T(8,128)S(1)} %get-tuple-element.25.refs_0_, f32[32]{0:T(128)S(1)} %copy-done.5, f32[168]{0:T(256)S(1)} %copy-done.3, bf16[168,128,128]{2,1,0:T(8,128)(2,1)S(1)} %copy-done, f32[168,128]{1,0:T(8,128)S(1)} %get-tuple-element.29.refs_4_, ...), custom_call_target="tpu_custom_call", output_to_operand_aliasing={{}: (6, {})} | custom-call | bytes 5767168 | tf_op jit(solution)/shard_map/update/pallas_call | solution.py:319
  59.4 0.7 %collective-permute-done.42.refs_17_ = bf16[192,128]{1,0:T(8,128)(2,1)S(1)} collective-permute-done((bf16[192,128]{1,0:T(8,128)(2,1)S(1)}, bf16[192,128]{1,0:T(8,128)(2,1)S(1)}, u32[]{:S(2)}, u32[]{:S(2)}) %collective-permute-start.42) | collective-permute-done | bytes 49184 | tf_op jit(solution)/shard_map/ppermute | solution.py:39
  60.6 3.5 %finish.1 = bf16[48,384]{1,0:T(8,128)(2,1)} custom-call(s32[32,48]{1,0:T(8,128)S(1)} %get-tuple-element.24.refs_0_, f32[6152,128]{1,0:T(8,128)S(1)} %get-tuple-element.27.refs_1_, f32[32,128]{1,0:T(8,128)S(1)} %bitcast.4, bf16[4096,384]{1,0:T(8,128)(2,1)S(1)} %copy-done.1, bf16[192,128]{1,0:T(8,128)(2,1)S(1)} %get-tuple-element.28.refs_4_, ...), custom_call_target="tpu_custom_call" | custom-call | flops 150994944 | bytes 3145728 | tf_op jit(solution)/shard_map/finish/pallas_call | solution.py:377
  (86 shorter events, 6.9 us)
Async XLA Ops:
  2.5 7.4 %collective-permute-start = (bf16[4,6144]{1,0:T(4,128)(2,1)S(1)}, bf16[4,6144]{1,0:T(4,128)(2,1)S(1)}, u32[]{:S(2)}, u32[]{:S(2)}) collective-permute-start(bf16[4,6144]{1,0:T(4,128)(2,1)S(1)} %pack.1.refs_2_), channel_id=1, source_target_pairs={{0,8},{1,9},{2,10},{3,11},{4,12},{5,13},{6,14},{7,15},{8,0},{9,1},... | collective-permute-start | bytes 147464 | tf_op jit(solution)/shard_map/ppermute | solution.py:39
  6.6 4.4 %collective-permute-start.1 = (bf16[4,6144]{1,0:T(4,128)(2,1)S(1)}, bf16[4,6144]{1,0:T(4,128)(2,1)S(1)}, u32[]{:S(2)}, u32[]{:S(2)}) collective-permute-start(bf16[4,6144]{1,0:T(4,128)(2,1)S(1)} %pack.1.refs_2_), channel_id=1, source_target_pairs={{0,4},{1,5},{2,6},{3,7},{4,0},{5,1},{6,2},{7,3},{8,12},{9,13},{10,... | collective-permute-start | bytes 147464 | tf_op jit(solution)/shard_map/ppermute | solution.py:39
  8.2 5.9 %collective-permute-start.2 = (bf16[4,6144]{1,0:T(4,128)(2,1)S(1)}, bf16[4,6144]{1,0:T(4,128)(2,1)S(1)}, u32[]{:S(2)}, u32[]{:S(2)}) collective-permute-start(bf16[4,6144]{1,0:T(4,128)(2,1)S(1)} %pack.1.refs_2_), channel_id=1, source_target_pairs={{0,12},{1,13},{2,14},{3,15},{4,8},{5,9},{6,10},{7,11},{8,4},{9,5},... | collective-permute-start | bytes 147464 | tf_op jit(solution)/shard_map/ppermute | solution.py:39
  8.2 7.4 %collective-permute-start.3 = (bf16[4,6144]{1,0:T(4,128)(2,1)S(1)}, bf16[4,6144]{1,0:T(4,128)(2,1)S(1)}, u32[]{:S(2)}, u32[]{:S(2)}) collective-permute-start(bf16[4,6144]{1,0:T(4,128)(2,1)S(1)} %pack.1.refs_2_), channel_id=1, source_target_pairs={{0,2},{1,3},{2,0},{3,1},{4,6},{5,7},{6,4},{7,5},{8,10},{9,11},{10,... | collective-permute-start | bytes 147464 | tf_op jit(solution)/shard_map/ppermute | solution.py:39
  9.9 5.7 %collective-permute-start.7 = (bf16[4,6144]{1,0:T(4,128)(2,1)S(1)}, bf16[4,6144]{1,0:T(4,128)(2,1)S(1)}, u32[]{:S(2)}, u32[]{:S(2)}) collective-permute-start(bf16[4,6144]{1,0:T(4,128)(2,1)S(1)} %pack.1.refs_2_), channel_id=1, source_target_pairs={{0,1},{1,0},{2,3},{3,2},{4,5},{5,4},{6,7},{7,6},{8,9},{9,8},{10,11... | collective-permute-start | bytes 147464 | tf_op jit(solution)/shard_map/ppermute | solution.py:39
  9.9 6.2 %collective-permute-start.4 = (bf16[4,6144]{1,0:T(4,128)(2,1)S(1)}, bf16[4,6144]{1,0:T(4,128)(2,1)S(1)}, u32[]{:S(2)}, u32[]{:S(2)}) collective-permute-start(bf16[4,6144]{1,0:T(4,128)(2,1)S(1)} %collective-permute-done.refs_3_), channel_id=1, source_target_pairs={{0,2},{1,3},{2,0},{3,1},{4,6},{5,7},{6,4},{7,5},{8,10},{9,11},{10,... | collective-permute-start | bytes 147464 | tf_op jit(solution)/shard_map/ppermute | solution.py:39
  11.0 5.1 %collective-permute-start.5 = (bf16[4,6144]{1,0:T(4,128)(2,1)S(1)}, bf16[4,6144]{1,0:T(4,128)(2,1)S(1)}, u32[]{:S(2)}, u32[]{:S(2)}) collective-permute-start(bf16[4,6144]{1,0:T(4,128)(2,1)S(1)} %collective-permute-done.1.refs_4_), channel_id=1, source_target_pairs={{0,2},{1,3},{2,0},{3,1},{4,6},{5,7},{6,4},{7,5},{8,10},{9,11},{10,... | collective-permute-start | bytes 147464 | tf_op jit(solution)/shard_map/ppermute | solution.py:39
  14.1 4.1 %collective-permute-start.6 = (bf16[4,6144]{1,0:T(4,128)(2,1)S(1)}, bf16[4,6144]{1,0:T(4,128)(2,1)S(1)}, u32[]{:S(2)}, u32[]{:S(2)}) collective-permute-start(bf16[4,6144]{1,0:T(4,128)(2,1)S(1)} %collective-permute-done.2.refs_5_), channel_id=1, source_target_pairs={{0,2},{1,3},{2,0},{3,1},{4,6},{5,7},{6,4},{7,5},{8,10},{9,11},{10,... | collective-permute-start | bytes 147464 | tf_op jit(solution)/shard_map/ppermute | solution.py:39
  15.6 3.1 %collective-permute-start.8 = (bf16[4,6144]{1,0:T(4,128)(2,1)S(1)}, bf16[4,6144]{1,0:T(4,128)(2,1)S(1)}, u32[]{:S(2)}, u32[]{:S(2)}) collective-permute-start(bf16[4,6144]{1,0:T(4,128)(2,1)S(1)} %collective-permute-done.refs_3_), channel_id=1, source_target_pairs={{0,1},{1,0},{2,3},{3,2},{4,5},{5,4},{6,7},{7,6},{8,9},{9,8},{10,11... | collective-permute-start | bytes 147464 | tf_op jit(solution)/shard_map/ppermute | solution.py:39
  16.1 2.7 %collective-permute-start.9 = (bf16[4,6144]{1,0:T(4,128)(2,1)S(1)}, bf16[4,6144]{1,0:T(4,128)(2,1)S(1)}, u32[]{:S(2)}, u32[]{:S(2)}) collective-permute-start(bf16[4,6144]{1,0:T(4,128)(2,1)S(1)} %collective-permute-done.1.refs_4_), channel_id=1, source_target_pairs={{0,1},{1,0},{2,3},{3,2},{4,5},{5,4},{6,7},{7,6},{8,9},{9,8},{10,11... | collective-permute-start | bytes 147464 | tf_op jit(solution)/shard_map/ppermute | solution.py:39
  22.5 7.3 %collective-permute-start.15 = (bf16[48,1024]{1,0:T(8,128)(2,1)S(1)}, bf16[48,1024]{1,0:T(8,128)(2,1)S(1)}, u32[]{:S(2)}, u32[]{:S(2)}) collective-permute-start(bf16[48,1024]{1,0:T(8,128)(2,1)S(1)} %get-tuple-element.26.refs_4_), channel_id=1, source_target_pairs={{0,8},{1,9},{2,10},{3,11},{4,12},{5,13},{6,14},{7,15},{8,0},{9,1},... | collective-permute-start | bytes 294920 | tf_op jit(solution)/shard_map/ppermute | solution.py:39
  22.6 8.7 %collective-permute-start.16 = (bf16[48,1024]{1,0:T(8,128)(2,1)S(1)}, bf16[48,1024]{1,0:T(8,128)(2,1)S(1)}, u32[]{:S(2)}, u32[]{:S(2)}) collective-permute-start(bf16[48,1024]{1,0:T(8,128)(2,1)S(1)} %get-tuple-element.26.refs_4_), channel_id=1, source_target_pairs={{0,4},{1,5},{2,6},{3,7},{4,0},{5,1},{6,2},{7,3},{8,12},{9,13},{10,... | collective-permute-start | bytes 294920 | tf_op jit(solution)/shard_map/ppermute | solution.py:39
  25.1 6.8 %collective-permute-start.18 = (bf16[48,1024]{1,0:T(8,128)(2,1)S(1)}, bf16[48,1024]{1,0:T(8,128)(2,1)S(1)}, u32[]{:S(2)}, u32[]{:S(2)}) collective-permute-start(bf16[48,1024]{1,0:T(8,128)(2,1)S(1)} %get-tuple-element.26.refs_4_), channel_id=1, source_target_pairs={{0,2},{1,3},{2,0},{3,1},{4,6},{5,7},{6,4},{7,5},{8,10},{9,11},{10,... | collective-permute-start | bytes 294920 | tf_op jit(solution)/shard_map/ppermute | solution.py:39
  26.6 5.3 %collective-permute-start.22 = (bf16[48,1024]{1,0:T(8,128)(2,1)S(1)}, bf16[48,1024]{1,0:T(8,128)(2,1)S(1)}, u32[]{:S(2)}, u32[]{:S(2)}) collective-permute-start(bf16[48,1024]{1,0:T(8,128)(2,1)S(1)} %get-tuple-element.26.refs_4_), channel_id=1, source_target_pairs={{0,1},{1,0},{2,3},{3,2},{4,5},{5,4},{6,7},{7,6},{8,9},{9,8},{10,11... | collective-permute-start | bytes 294920 | tf_op jit(solution)/shard_map/ppermute | solution.py:39
  29.8 4.7 %collective-permute-start.17 = (bf16[48,1024]{1,0:T(8,128)(2,1)S(1)}, bf16[48,1024]{1,0:T(8,128)(2,1)S(1)}, u32[]{:S(2)}, u32[]{:S(2)}) collective-permute-start(bf16[48,1024]{1,0:T(8,128)(2,1)S(1)} %collective-permute-done.15.refs_5_), channel_id=1, source_target_pairs={{0,4},{1,5},{2,6},{3,7},{4,0},{5,1},{6,2},{7,3},{8,12},{9,13},{10,... | collective-permute-start | bytes 294920 | tf_op jit(solution)/shard_map/ppermute | solution.py:39
  29.8 6.2 %collective-permute-start.19 = (bf16[48,1024]{1,0:T(8,128)(2,1)S(1)}, bf16[48,1024]{1,0:T(8,128)(2,1)S(1)}, u32[]{:S(2)}, u32[]{:S(2)}) collective-permute-start(bf16[48,1024]{1,0:T(8,128)(2,1)S(1)} %collective-permute-done.15.refs_5_), channel_id=1, source_target_pairs={{0,2},{1,3},{2,0},{3,1},{4,6},{5,7},{6,4},{7,5},{8,10},{9,11},{10,... | collective-permute-start | bytes 294920 | tf_op jit(solution)/shard_map/ppermute | solution.py:39
  31.3 5.6 %collective-permute-start.20 = (bf16[48,1024]{1,0:T(8,128)(2,1)S(1)}, bf16[48,1024]{1,0:T(8,128)(2,1)S(1)}, u32[]{:S(2)}, u32[]{:S(2)}) collective-permute-start(bf16[48,1024]{1,0:T(8,128)(2,1)S(1)} %collective-permute-done.16.refs_6_), channel_id=1, source_target_pairs={{0,2},{1,3},{2,0},{3,1},{4,6},{5,7},{6,4},{7,5},{8,10},{9,11},{10,... | collective-permute-start | bytes 294920 | tf_op jit(solution)/shard_map/ppermute | solution.py:39
  31.9 5.1 %collective-permute-start.23 = (bf16[48,1024]{1,0:T(8,128)(2,1)S(1)}, bf16[48,1024]{1,0:T(8,128)(2,1)S(1)}, u32[]{:S(2)}, u32[]{:S(2)}) collective-permute-start(bf16[48,1024]{1,0:T(8,128)(2,1)S(1)} %collective-permute-done.15.refs_5_), channel_id=1, source_target_pairs={{0,1},{1,0},{2,3},{3,2},{4,5},{5,4},{6,7},{7,6},{8,9},{9,8},{10,11... | collective-permute-start | bytes 294920 | tf_op jit(solution)/shard_map/ppermute | solution.py:39
  31.9 5.6 %collective-permute-start.24 = (bf16[48,1024]{1,0:T(8,128)(2,1)S(1)}, bf16[48,1024]{1,0:T(8,128)(2,1)S(1)}, u32[]{:S(2)}, u32[]{:S(2)}) collective-permute-start(bf16[48,1024]{1,0:T(8,128)(2,1)S(1)} %collective-permute-done.16.refs_6_), channel_id=1, source_target_pairs={{0,1},{1,0},{2,3},{3,2},{4,5},{5,4},{6,7},{7,6},{8,9},{9,8},{10,11... | collective-permute-start | bytes 294920 | tf_op jit(solution)/shard_map/ppermute | solution.py:39
  34.5 4.6 %collective-permute-start.21 = (bf16[48,1024]{1,0:T(8,128)(2,1)S(1)}, bf16[48,1024]{1,0:T(8,128)(2,1)S(1)}, u32[]{:S(2)}, u32[]{:S(2)}) collective-permute-start(bf16[48,1024]{1,0:T(8,128)(2,1)S(1)} %collective-permute-done.17.refs_7_), channel_id=1, source_target_pairs={{0,2},{1,3},{2,0},{3,1},{4,6},{5,7},{6,4},{7,5},{8,10},{9,11},{10,... | collective-permute-start | bytes 294920 | tf_op jit(solution)/shard_map/ppermute | solution.py:39
  36.0 3.1 %collective-permute-start.26 = (bf16[48,1024]{1,0:T(8,128)(2,1)S(1)}, bf16[48,1024]{1,0:T(8,128)(2,1)S(1)}, u32[]{:S(2)}, u32[]{:S(2)}) collective-permute-start(bf16[48,1024]{1,0:T(8,128)(2,1)S(1)} %collective-permute-done.18.refs_8_), channel_id=1, source_target_pairs={{0,1},{1,0},{2,3},{3,2},{4,5},{5,4},{6,7},{7,6},{8,9},{9,8},{10,11... | collective-permute-start | bytes 294920 | tf_op jit(solution)/shard_map/ppermute | solution.py:39
  43.0 8.5 %collective-permute-start.30 = (bf16[192,128]{1,0:T(8,128)(2,1)S(1)}, bf16[192,128]{1,0:T(8,128)(2,1)S(1)}, u32[]{:S(2)}, u32[]{:S(2)}) collective-permute-start(bf16[192,128]{1,0:T(8,128)(2,1)S(1)} %get-tuple-element.28.refs_4_), channel_id=1, source_target_pairs={{0,8},{1,9},{2,10},{3,11},{4,12},{5,13},{6,14},{7,15},{8,0},{9,1},... | collective-permute-start | bytes 147464 | tf_op jit(solution)/shard_map/ppermute | solution.py:39
  45.0 6.5 %collective-permute-start.31 = (bf16[192,128]{1,0:T(8,128)(2,1)S(1)}, bf16[192,128]{1,0:T(8,128)(2,1)S(1)}, u32[]{:S(2)}, u32[]{:S(2)}) collective-permute-start(bf16[192,128]{1,0:T(8,128)(2,1)S(1)} %get-tuple-element.28.refs_4_), channel_id=1, source_target_pairs={{0,4},{1,5},{2,6},{3,7},{4,0},{5,1},{6,2},{7,3},{8,12},{9,13},{10,... | collective-permute-start | bytes 147464 | tf_op jit(solution)/shard_map/ppermute | solution.py:39
  45.5 6.0 %collective-permute-start.32 = (bf16[192,128]{1,0:T(8,128)(2,1)S(1)}, bf16[192,128]{1,0:T(8,128)(2,1)S(1)}, u32[]{:S(2)}, u32[]{:S(2)}) collective-permute-start(bf16[192,128]{1,0:T(8,128)(2,1)S(1)} %get-tuple-element.28.refs_4_), channel_id=1, source_target_pairs={{0,12},{1,13},{2,14},{3,15},{4,8},{5,9},{6,10},{7,11},{8,4},{9,5},... | collective-permute-start | bytes 147464 | tf_op jit(solution)/shard_map/ppermute | solution.py:39
  47.4 4.1 %collective-permute-start.33 = (bf16[192,128]{1,0:T(8,128)(2,1)S(1)}, bf16[192,128]{1,0:T(8,128)(2,1)S(1)}, u32[]{:S(2)}, u32[]{:S(2)}) collective-permute-start(bf16[192,128]{1,0:T(8,128)(2,1)S(1)} %get-tuple-element.28.refs_4_), channel_id=1, source_target_pairs={{0,2},{1,3},{2,0},{3,1},{4,6},{5,7},{6,4},{7,5},{8,10},{9,11},{10,... | collective-permute-start | bytes 147464 | tf_op jit(solution)/shard_map/ppermute | solution.py:39
  48.9 3.8 %collective-permute-start.37 = (bf16[192,128]{1,0:T(8,128)(2,1)S(1)}, bf16[192,128]{1,0:T(8,128)(2,1)S(1)}, u32[]{:S(2)}, u32[]{:S(2)}) collective-permute-start(bf16[192,128]{1,0:T(8,128)(2,1)S(1)} %get-tuple-element.28.refs_4_), channel_id=1, source_target_pairs={{0,1},{1,0},{2,3},{3,2},{4,5},{5,4},{6,7},{7,6},{8,9},{9,8},{10,11... | collective-permute-start | bytes 147464 | tf_op jit(solution)/shard_map/ppermute | solution.py:39
  52.1 2.6 %collective-permute-start.39 = (bf16[192,128]{1,0:T(8,128)(2,1)S(1)}, bf16[192,128]{1,0:T(8,128)(2,1)S(1)}, u32[]{:S(2)}, u32[]{:S(2)}) collective-permute-start(bf16[192,128]{1,0:T(8,128)(2,1)S(1)} %collective-permute-done.31.refs_6_), channel_id=1, source_target_pairs={{0,1},{1,0},{2,3},{3,2},{4,5},{5,4},{6,7},{7,6},{8,9},{9,8},{10,11... | collective-permute-start | bytes 147464 | tf_op jit(solution)/shard_map/ppermute | solution.py:39
  52.2 3.9 %collective-permute-start.40 = (bf16[192,128]{1,0:T(8,128)(2,1)S(1)}, bf16[192,128]{1,0:T(8,128)(2,1)S(1)}, u32[]{:S(2)}, u32[]{:S(2)}) collective-permute-start(bf16[192,128]{1,0:T(8,128)(2,1)S(1)} %collective-permute-done.32.refs_7_), channel_id=1, source_target_pairs={{0,1},{1,0},{2,3},{3,2},{4,5},{5,4},{6,7},{7,6},{8,9},{9,8},{10,11... | collective-permute-start | bytes 147464 | tf_op jit(solution)/shard_map/ppermute | solution.py:39
  52.6 3.5 %collective-permute-start.41 = (bf16[192,128]{1,0:T(8,128)(2,1)S(1)}, bf16[192,128]{1,0:T(8,128)(2,1)S(1)}, u32[]{:S(2)}, u32[]{:S(2)}) collective-permute-start(bf16[192,128]{1,0:T(8,128)(2,1)S(1)} %collective-permute-done.33.refs_8_), channel_id=1, source_target_pairs={{0,1},{1,0},{2,3},{3,2},{4,5},{5,4},{6,7},{7,6},{8,9},{9,8},{10,11... | collective-permute-start | bytes 147464 | tf_op jit(solution)/shard_map/ppermute | solution.py:39
  52.7 6.0 %collective-permute-start.34 = (bf16[192,128]{1,0:T(8,128)(2,1)S(1)}, bf16[192,128]{1,0:T(8,128)(2,1)S(1)}, u32[]{:S(2)}, u32[]{:S(2)}) collective-permute-start(bf16[192,128]{1,0:T(8,128)(2,1)S(1)} %collective-permute-done.30.refs_5_), channel_id=1, source_target_pairs={{0,2},{1,3},{2,0},{3,1},{4,6},{5,7},{6,4},{7,5},{8,10},{9,11},{10,... | collective-permute-start | bytes 147464 | tf_op jit(solution)/shard_map/ppermute | solution.py:39
  54.1 4.7 %collective-permute-start.35 = (bf16[192,128]{1,0:T(8,128)(2,1)S(1)}, bf16[192,128]{1,0:T(8,128)(2,1)S(1)}, u32[]{:S(2)}, u32[]{:S(2)}) collective-permute-start(bf16[192,128]{1,0:T(8,128)(2,1)S(1)} %collective-permute-done.31.refs_6_), channel_id=1, source_target_pairs={{0,2},{1,3},{2,0},{3,1},{4,6},{5,7},{6,4},{7,5},{8,10},{9,11},{10,... | collective-permute-start | bytes 147464 | tf_op jit(solution)/shard_map/ppermute | solution.py:39
  54.7 4.2 %collective-permute-start.36 = (bf16[192,128]{1,0:T(8,128)(2,1)S(1)}, bf16[192,128]{1,0:T(8,128)(2,1)S(1)}, u32[]{:S(2)}, u32[]{:S(2)}) collective-permute-start(bf16[192,128]{1,0:T(8,128)(2,1)S(1)} %collective-permute-done.32.refs_7_), channel_id=1, source_target_pairs={{0,2},{1,3},{2,0},{3,1},{4,6},{5,7},{6,4},{7,5},{8,10},{9,11},{10,... | collective-permute-start | bytes 147464 | tf_op jit(solution)/shard_map/ppermute | solution.py:39
  (23 other events, 175.2 us)
